TPU v7x, 32 devices: a whole 2x2x4 slice. The times are simulated.
32 devices in a mesh: by: 4 (over z), bx: 8 (over y, x, core).
Axes of the slice: x: 2, y: 2, z: 4, core: 2. Of those that a mesh axis runs over, the one named last changes fastest.
Arguments:
- eastward_flow: float32 [62, 32, 2048], P(None, 'by', 'bx'), may hold values from -6 to 6
- northward_flow: float32 [62, 32, 2048], P(None, 'by', 'bx'), may hold values from -6 to 6
- heat_anomaly: float32 [62, 32, 2048], P(None, 'by', 'bx'), may hold values from -6 to 6
- salt_anomaly: float32 [62, 32, 2048], P(None, 'by', 'bx'), may hold values from -6 to 6
- air_stress_forcing: float32 [2, 32, 2048], P(None, 'by', 'bx'), may hold values from -6 to 6
- earlier_sea_height_load: float32 [32, 2048], P('by', 'bx'), may hold values from -6 to 6
- ocean_layer_depths: int32 [32, 2048], P('by', 'bx'), may hold values from 0 to 62, as said below
Outputs:
- east_new: float32 [62, 32, 2048], P(None, 'by', 'bx')
- north_new: float32 [62, 32, 2048], P(None, 'by', 'bx')
- temperature_new: float32 [62, 32, 2048], P(None, 'by', 'bx')
- salinity_new: float32 [62, 32, 2048], P(None, 'by', 'bx')
- surface_new: float32 [32, 2048], P('by', 'bx')
Inputs may be any that keep to these rules, and one draw needn't show every extreme that they name: `ocean_layer_depths`: land (0) covers whole aligned tiles of 8 x 8 cells; every ocean column has 1 to 62 levels.
All inputs are finite; a program needn't handle non-finite values.
Results may differ from a plain program's by a relative error of at most 0.0003.
Values sent between devices are 32-bit elements; how exact they have to be, the bound alone decides.
No kernel may reach another device: no remote copies, remote signals or barrier semaphores. Data moves between devices by JAX's collectives and lax.ppermute only.
A program may use at most 192 MiB of HBM per device.

v0:
```python
import functools
import math

import jax
import jax.numpy as jnp
from jax import lax
from jax.experimental import pallas as pl
from jax.experimental.pallas import tpu as pltpu
from jax.sharding import PartitionSpec as P

ITERS = 4
KAPPA = 0.004
ADVECT = 0.25
PRESS = 0.1
WIND = 0.5
PHI = 0.5
DIVERGE = 2.0
LOWER = 0.2
UPPER = 2.0

SUB = 8
LANES = 128
FIELDS = 4
RIM = 4
EDGE = 8
EXTRA = 2
CHUNKS = (2, 2, 2, 2)
FAR = 1000000
F32 = jnp.float32


def chebyshev_weights(count):
    middle = 0.5 * (UPPER + LOWER)
    half_span = 0.5 * (UPPER - LOWER)
    ratio_value = middle / half_span
    rho_now = 1.0 / ratio_value
    updates = []
    for index in range(count - 1):
        rho_next = 1.0 / (2.0 * ratio_value - rho_now)
        updates.append((rho_next * rho_now, 2.0 * rho_next / half_span))
        rho_now = rho_next
    return (1.0 / middle, updates)


def first_level(chunk):
    return SUB * sum(CHUNKS[:chunk]) - (EXTRA if chunk else 0)


def chunk_levels(chunk):
    return SUB * CHUNKS[chunk] - (0 if chunk else EXTRA)


def pack_kernel(rows, *refs):
    count = len(CHUNKS)
    fields = refs[:FIELDS]
    wind, surface, depth = refs[FIELDS : FIELDS + 3]
    outs = refs[FIELDS + 3 :]
    halves = [(outs[2 * c], outs[2 * c + 1]) for c in range(count)]
    to_west, to_east = outs[2 * count : 2 * count + 2]
    held, sems = outs[2 * count + 2 :]

    def copy(f, lane):
        return pltpu.make_async_copy(
            fields[f].at[:, pl.ds(lane * LANES, LANES)], held.at[f, lane], sems.at[f, lane]
        )

    for f in range(FIELDS):
        for lane in range(2):
            copy(f, lane).start()
    flat = (
        (depth[...].astype(F32), surface[...]),
        (wind[0], wind[1]),
    )
    for f in range(FIELDS):
        for lane in range(2):
            copy(f, lane).wait()
        for c in range(count):
            for t in range(CHUNKS[c]):
                used = min(SUB, chunk_levels(c) - SUB * t)
                base = (first_level(c) + SUB * t) * rows
                for r in range(rows):
                    half = halves[c][r // RIM]
                    for lane in range(2):
                        span = pl.ds(lane * LANES, LANES)
                        half[f, r % RIM, t, pl.ds(0, used), span] = held[
                            f, lane, pl.ds(base + r, used, stride=rows), :
                        ]
                    for extra in range(SUB - used):
                        if f < len(flat):
                            line = flat[f][extra][r : r + 1, :]
                        else:
                            line = jnp.zeros((1, 2 * LANES), F32)
                        half[f, r % RIM, t, pl.ds(used + extra, 1), :] = line
    lanes = lax.broadcasted_iota(jnp.int32, (SUB, LANES), 1)
    slot = 0
    for c in range(count):
        for t in range(CHUNKS[c]):
            for group in range(2):
                west = jnp.zeros((SUB, LANES), F32)
                east = jnp.zeros((SUB, LANES), F32)
                for q in range(RIM):
                    for f in range(FIELDS):
                        place = (q * FIELDS + f) * EDGE
                        other = (place - EDGE) % LANES
                        block = halves[c][group][f, q, t]
                        low = block[:, :LANES]
                        high = block[:, LANES:]
                        if place:
                            low = pltpu.roll(low, place, 1)
                            high = pltpu.roll(high, place, 1)
                        west = jnp.where((lanes >= place) & (lanes < place + EDGE), low, west)
                        east = jnp.where((lanes >= other) & (lanes < other + EDGE), high, east)
                to_west[group, slot] = west
                to_east[group, slot] = east
            slot += 1


def pack(fields, wind, surface, depth):
    levels, rows, columns = fields[0].shape
    flat = [item.reshape(levels * rows, columns) for item in fields]
    total = sum(CHUNKS)
    shapes = []
    for tiles in CHUNKS:
        shapes += [jax.ShapeDtypeStruct((FIELDS, RIM, tiles, SUB, columns), F32)] * 2
    shapes += [jax.ShapeDtypeStruct((2, total, SUB, LANES), F32)] * 2
    outs = pl.pallas_call(
        functools.partial(pack_kernel, rows),
        out_shape=shapes,
        in_specs=[pl.BlockSpec(memory_space=pltpu.HBM)] * FIELDS
        + [pl.BlockSpec(memory_space=pltpu.VMEM)] * 3,
        out_specs=[pl.BlockSpec(memory_space=pltpu.VMEM)] * len(shapes),
        scratch_shapes=[
            pltpu.VMEM((FIELDS, 2, levels * rows, LANES), F32),
            pltpu.SemaphoreType.DMA((FIELDS, 2)),
        ],
        compiler_params=pltpu.CompilerParams(vmem_limit_bytes=12 * 1024 * 1024),
        name="pack",
    )(*flat, wind, surface, depth)
    halves = [(outs[2 * c], outs[2 * c + 1]) for c in range(len(CHUNKS))]
    return halves, outs[-2], outs[-1]


def east_of(value):
    return pltpu.roll(value, value.shape[-1] - 1, value.ndim - 1)


def west_of(value):
    return pltpu.roll(value, 1, value.ndim - 1)


def step_kernel(chunk, rows, *refs):
    first = chunk == 0
    last = chunk == len(CHUNKS) - 1
    tiles = CHUNKS[chunk]
    levels = chunk_levels(chunk)
    tall = rows + 2 * RIM
    refs = list(refs)

    def take(count):
        taken = refs[:count]
        del refs[:count]
        return taken

    rotate = take(1)[0]
    south, low, high, north = take(4)
    sides = take(4)
    if not first:
        depth_in, carry_in, sums_in = take(3)
        take(FIELDS)
    outs = take(FIELDS)
    if first:
        depth_out, surface_out = take(2)
    if last:
        sums_low, sums_high = take(2)
    else:
        carry_out, sums_out = take(2)
    cur, wets, wets_x, wets_w, wets_y, press, press_x, press_y, laps, mixes, between, held = take(12)
    if last:
        carry, sums = take(2)
    else:
        carry, sums = carry_out, sums_out
    deep = depth_out if first else depth_in
    (sems,) = take(1)

    if first:
        carry[...] = jnp.zeros(carry.shape, F32)
        sums[...] = jnp.zeros(sums.shape, F32)
    else:
        carry[...] = carry_in[...]
        sums[...] = sums_in[...]

    lanes = lax.broadcasted_iota(jnp.int32, (SUB, LANES), 1)
    start = sum(CHUNKS[:chunk])
    blocks = (south, low, high, north)
    wide = low.shape[-1] + LANES
    own = low.shape[-1]
    every = range(FIELDS)

    def rim_of(f, a, t):
        group, q = a // RIM, a % RIM
        if group == 0:
            from_east, from_west = sides[2][0, start + t], sides[2][1, start + t]
        elif group == 3:
            from_east, from_west = sides[3][0, start + t], sides[3][1, start + t]
        else:
            from_east, from_west = sides[0][group - 1, start + t], sides[1][group - 1, start + t]
        place = (q * FIELDS + f) * EDGE
        both = jnp.where((lanes >= place) & (lanes < place + EDGE), from_east, from_west)
        return pltpu.roll(both, LANES - place, 1) if place else both

    if first:
        for a in range(tall):
            for extra, ref in ((0, depth_out), (1, surface_out)):
                slot = SUB - EXTRA + extra
                line = blocks[a // RIM][0, a % RIM, tiles - 1]
                ref[pl.ds(a, 1), pl.ds(0, own)] = line[slot : slot + 1, :]
                line = rim_of(0, a, tiles - 1)
                ref[pl.ds(a, 1), pl.ds(own, LANES)] = line[slot : slot + 1, :]

    subs = lax.broadcasted_iota(jnp.int32, (SUB, wide), 0)

    def pressure(get, lowest, highest, carry_at):
        rows_p = range(lowest - 1, highest + 2)
        sums_p = [((-0.8 * PRESS) * get(2, a) + (0.6 * PRESS) * get(3, a)) * wets[a] for a in rows_p]
        for shift in (1, 2, 4):
            moved = [pltpu.roll(value, shift, 0) for value in sums_p]
            sums_p = [
                value + jnp.where(subs >= shift, other, 0.0) for value, other in zip(sums_p, moved)
            ]
        before = [carry[carry_at + k] for k in range(len(sums_p))]
        sums_p = [value + other for value, other in zip(sums_p, before)]
        ends = [jnp.broadcast_to(value[SUB - 1 : SUB, :], value.shape) for value in sums_p]
        for k, a in enumerate(rows_p):
            press[a] = sums_p[k]
            carry[carry_at + k] = ends[k]
        slope = wets_y[lowest - 1] * (press[lowest] - press[lowest - 1])
        for a in range(lowest, highest + 1):
            here = press[a]
            east, west = east_of(here), west_of(here)
            slope_before = slope
            slope = wets_y[a] * (press[a + 1] - here)
            press_x[a] = 0.5 * (wets_x[a] * (east - here) + wets_w[a] * (here - west))
            press_y[a] = 0.5 * (slope + slope_before)

    def tendency(get, lowest, highest, carry_at, emit):
        pressure(get, lowest, highest, carry_at)

        def turned(get_row):
            values = [get_row(f) for f in every]
            return values, [east_of(x) for x in values], [west_of(x) for x in values]

        below = [get(f, lowest - 2) for f in every]
        here, east, west = turned(lambda f: get(f, lowest - 1))
        face = wets_y[lowest - 2]
        up = [face * (x - y) for x, y in zip(here, below)]
        for a in range(lowest - 1, highest + 2):
            if a <= highest:
                after, east_after, west_after = turned(lambda f: get(f, a + 1))
            else:
                after = [get(f, a + 1) for f in every]
            face, side_x, side_w = wets_y[a], wets_x[a], wets_w[a]
            up_before = up
            up = [face * (x - y) for x, y in zip(after, here)]
            right = [side_x * (x - y) for x, y in zip(east, here)]
            left = [side_w * (x - y) for x, y in zip(here, west)]
            lap = [(right[f] - left[f]) + (up[f] - up_before[f]) for f in every]
            if lowest <= a <= highest:
                u, v = (-0.5 * ADVECT) * here[0], (-0.5 * ADVECT) * here[1]
                mixed = [u * (right[f] + left[f]) + v * (up[f] + up_before[f]) for f in every]
                turn = rotate[a] * wets[a]
                mixed[0] = mixed[0] + (turn * here[1] - press_x[a])
                mixed[1] = mixed[1] - (turn * here[0] + press_y[a])
                for f in every:
                    mixes[f, a] = mixed[f]
            for f in every:
                laps[f, a] = lap[f]
            if a <= highest:
                here, east, west = after, east_after, west_after

        below = [laps[f, lowest - 1] for f in every]
        here, east, west = turned(lambda f: laps[f, lowest])
        face = wets_y[lowest - 1]
        up = [face * (x - y) for x, y in zip(here, below)]
        for a in range(lowest, highest + 1):
            if a < highest:
                after, east_after, west_after = turned(lambda f: laps[f, a + 1])
            else:
                after = [laps[f, a + 1] for f in every]
            face, side_x, side_w = wets_y[a], wets_x[a], wets_w[a]
            up_before = up
            up = [face * (x - y) for x, y in zip(after, here)]
            smooth = [
                (side_x * (east[f] - here[f]) - side_w * (here[f] - west[f]))
                + (up[f] - up_before[f])
                for f in every
            ]
            emit(a, [mixes[f, a] - KAPPA * smooth[f] for f in every])
            if a < highest:
                here, east, west = after, east_after, west_after

    def tile(t, _):
        for a in range(tall):
            for f in every:
                cur[f, a, :, pl.ds(0, own)] = blocks[a // RIM][f, a % RIM, t]
                cur[f, a, :, pl.ds(own, LANES)] = rim_of(f, a, t)
        level = subs + (first_level(chunk) + SUB * t)
        if first:
            level = jnp.where(level >= levels, FAR, level)
        level = level.astype(F32)
        top = jnp.where(level == 0.0, WIND, 0.0)
        deeps = [deep[pl.ds(a, 1), :] for a in range(tall)]
        for a in range(tall):
            wets[a] = jnp.where(level < deeps[a], 1.0, 0.0)
            wets_x[a] = jnp.where(level < jnp.minimum(deeps[a], east_of(deeps[a])), 1.0, 0.0)
            wets_w[a] = jnp.where(level < jnp.minimum(deeps[a], west_of(deeps[a])), 1.0, 0.0)
            if a + 1 < tall:
                wets_y[a] = jnp.where(level < jnp.minimum(deeps[a], deeps[a + 1]), 1.0, 0.0)

        def winded(a, values):
            if not first:
                return values
            windy = top * wets[a]
            values = list(values)
            for f in range(2):
                slot = SUB - EXTRA + f
                line = jnp.concatenate(
                    [
                        blocks[a // RIM][1, a % RIM, tiles - 1][slot : slot + 1, :],
                        rim_of(1, a, tiles - 1)[slot : slot + 1, :],
                    ],
                    axis=1,
                )
                values[f] = values[f] + windy * line
            return values

        def emit_first(a, values):
            values = winded(a, values)
            values = [cur[f, a] + values[f] for f in every]
            for f in every:
                between[f, a] = values[f]

        tendency(lambda f, a: cur[f, a], 2, tall - 3, 0, emit_first)

        def emit_second(a, values):
            values = winded(a, values)
            news = [0.5 * ((cur[f, a] + between[f, a]) + values[f]) for f in every]
            r = a - RIM
            adds = [sums[f, r] + wets[a] * news[f] for f in range(2)]
            for f in range(2):
                sums[f, r] = adds[f]
            for f in every:
                for lane in range(2):
                    held[f, lane, pl.ds(t * (SUB * rows) + r, SUB, stride=rows), :] = news[f][
                        :, lane * LANES : (lane + 1) * LANES
                    ]

        tendency(lambda f, a: between[f, a], RIM, tall - RIM - 1, tall - 2, emit_second)
        return 0

    lax.fori_loop(0, tiles, tile, 0)

    def copy(f, lane):
        return pltpu.make_async_copy(
            held.at[f, lane, pl.ds(0, levels * rows)],
            outs[f].at[pl.ds(first_level(chunk) * rows, levels * rows), pl.ds(lane * LANES, LANES)],
            sems.at[f, lane],
        )

    for f in range(FIELDS):
        for lane in range(2):
            copy(f, lane).start()
    if last:
        depth_levels = first_level(chunk) + levels
        for f in range(2):
            for r in range(rows):
                line = jnp.sum(sums[f, r], axis=0, keepdims=True) / depth_levels
                if r < RIM:
                    sums_low[f, pl.ds(r, 1), :] = line
                else:
                    sums_high[f, pl.ds(r - RIM, 1), :] = line
    for f in range(FIELDS):
        for lane in range(2):
            copy(f, lane).wait()


def step(chunk, rows, levels, columns, rotate, blocks, sides, kept, news):
    first = chunk == 0
    last = chunk == len(CHUNKS) - 1
    tiles = CHUNKS[chunk]
    wide = columns + LANES
    tall = rows + 2 * RIM
    vmem = pl.BlockSpec(memory_space=pltpu.VMEM)
    hbm = pl.BlockSpec(memory_space=pl.ANY)
    operands = [rotate, *blocks, *sides]
    in_specs = [pl.BlockSpec(memory_space=pltpu.SMEM)] + [vmem] * 8
    if not first:
        operands += [*kept, *news]
        in_specs += [vmem] * 3 + [hbm] * FIELDS
    carry = (tall - 2 + rows + 2, SUB, wide)
    sums = (2, rows, SUB, wide)
    shapes = [jax.ShapeDtypeStruct((levels * rows, columns), F32)] * FIELDS
    out_specs = [hbm] * FIELDS
    row = pltpu.VMEM((tall, SUB, wide), F32)
    fields = pltpu.VMEM((FIELDS, tall, SUB, wide), F32)
    scratch = [fields] + [row] * 7 + [fields] * 3
    scratch += [pltpu.VMEM((FIELDS, 2, tiles * SUB * rows, LANES), F32)]
    if first:
        shapes += [jax.ShapeDtypeStruct((tall, wide), F32)] * 2
    if last:
        shapes += [jax.ShapeDtypeStruct((2, RIM, wide), F32)] * 2
        scratch += [pltpu.VMEM(carry, F32), pltpu.VMEM(sums, F32)]
    else:
        shapes += [jax.ShapeDtypeStruct(carry, F32), jax.ShapeDtypeStruct(sums, F32)]
    out_specs += [vmem] * (len(shapes) - FIELDS)
    scratch += [pltpu.SemaphoreType.DMA((FIELDS, 2))]
    aliases = {} if first else {len(operands) - FIELDS + f: f for f in range(FIELDS)}
    return pl.pallas_call(
        functools.partial(step_kernel, chunk, rows),
        out_shape=shapes,
        in_specs=in_specs,
        out_specs=out_specs,
        scratch_shapes=scratch,
        input_output_aliases=aliases,
        compiler_params=pltpu.CompilerParams(vmem_limit_bytes=16 * 1024 * 1024),
        name="step",
    )(*operands)


def solve_kernel(levels, rows, deep_ref, surface_ref, south, low, high, north, out):
    deep = deep_ref[...]
    surface = surface_ref[...]
    flows = [
        jnp.concatenate([south[f], low[f], high[f], north[f]], axis=0) for f in range(2)
    ]
    tall = deep.shape[0]

    def east(x):
        return pltpu.roll(x, x.shape[1] - 1, 1)

    def west(x):
        return pltpu.roll(x, 1, 1)

    def up(x):
        return pltpu.roll(x, tall - 1, 0)

    def down(x):
        return pltpu.roll(x, 1, 0)

    ocean = jnp.where(deep > 0.0, 1.0, 0.0)
    across = ocean * east(ocean) * (east(flows[0]) - flows[0])
    along = ocean * up(ocean) * (up(flows[1]) - flows[1])
    slope = 0.5 * (across + west(across)) + 0.5 * (along + down(along))
    forcing = ocean * (PHI * surface - DIVERGE * slope)
    pair = jnp.minimum(deep, east(deep))
    corner = jnp.minimum(pair, up(pair)) / levels
    column = corner + down(corner)
    diagonal = PHI + 0.5 * (column + west(column))

    def operator(e):
        plus = e + up(e)
        minus = up(e) - e
        flux_x = corner * (0.5 * (east(plus) - plus))
        flux_y = corner * (0.5 * (east(minus) + minus))
        fx = flux_x + down(flux_x)
        fy = flux_y + west(flux_y)
        spread = 0.5 * ((fx - west(fx)) + (fy - down(fy)))
        return PHI * e - spread

    opening, updates = chebyshev_weights(ITERS)
    residual = forcing - operator(surface)
    direction = opening * (residual / diagonal)
    total = surface
    for index in range(ITERS):
        total = total + direction
        if index + 1 < ITERS:
            residual = residual - operator(direction)
            keep, push = updates[index]
            direction = keep * direction + push * (residual / diagonal)
    out[...] = total[RIM : RIM + rows, : out.shape[1]]


def body(
    eastward_flow,
    northward_flow,
    heat_anomaly,
    salt_anomaly,
    air_stress_forcing,
    earlier_sea_height_load,
    ocean_layer_depths,
):
    levels, rows, columns = eastward_flow.shape
    assert rows == 2 * RIM and columns == 2 * LANES and levels + EXTRA == SUB * sum(CHUNKS)
    along_y, along_x = lax.axis_size("by"), lax.axis_size("bx")
    to_north = [(i, i + 1) for i in range(along_y - 1)]
    to_south = [(i + 1, i) for i in range(along_y - 1)]
    to_east = [(i, (i + 1) % along_x) for i in range(along_x)]
    to_west = [((i + 1) % along_x, i) for i in range(along_x)]

    row_index = lax.axis_index("by") * rows - RIM + jnp.arange(rows + 2 * RIM)
    rotate = 1.2 * jnp.sin(
        0.9 * math.pi * ((row_index.astype(F32) + 0.5) / (rows * along_y) - 0.5)
    )

    fields = (eastward_flow, northward_flow, heat_anomaly, salt_anomaly)
    halves, west_edge, east_edge = pack(
        fields, air_stress_forcing, earlier_sea_height_load, ocean_layer_depths
    )
    from_east = lax.ppermute(west_edge, "bx", to_west)
    from_west = lax.ppermute(east_edge, "bx", to_east)

    def send(low, high):
        return lax.ppermute(high, "by", to_north), lax.ppermute(low, "by", to_south)

    rims = [send(*halves[0])]
    corner_south = lax.ppermute(jnp.stack([from_east[1], from_west[1]]), "by", to_north)
    corner_north = lax.ppermute(jnp.stack([from_east[0], from_west[0]]), "by", to_south)
    *rims[0], corner_south, corner_north, low, high = lax.optimization_barrier(
        (*rims[0], corner_south, corner_north, *halves[1])
    )
    halves[1] = (low, high)
    rims.append(send(low, high))
    sides = (from_east, from_west, corner_south, corner_north)

    kept, news = None, None
    for chunk in range(len(CHUNKS)):
        low, high = halves[chunk]
        south, north = rims[chunk]
        outs = step(
            chunk, rows, levels, columns, rotate, (south, low, high, north), sides, kept, news
        )
        news, rest = outs[:FIELDS], outs[FIELDS:]
        if chunk == 0:
            deep, surface = rest[:2]
            rest = rest[2:]
        if chunk + 2 < len(CHUNKS):
            low, high, *rest = lax.optimization_barrier((*halves[chunk + 2], *rest))
            halves[chunk + 2] = (low, high)
            rims.append(send(low, high))
        kept = (deep, *rest)
    low, high = rest
    south = lax.ppermute(high, "by", to_north)
    north = lax.ppermute(low, "by", to_south)
    surface_new = pl.pallas_call(
        functools.partial(solve_kernel, levels, rows),
        out_shape=jax.ShapeDtypeStruct((rows, columns), F32),
        in_specs=[pl.BlockSpec(memory_space=pltpu.VMEM)] * 6,
        out_specs=pl.BlockSpec(memory_space=pltpu.VMEM),
        name="solve",
    )(deep, surface, south, low, high, north)
    shaped = [item.reshape(levels, rows, columns) for item in news]
    return (*shaped, surface_new)


def solution(mesh):
    return jax.shard_map(
        body,
        mesh=mesh,
        in_specs=(P(None, "by", "bx"),) * 5 + (P("by", "bx"),) * 2,
        out_specs=(P(None, "by", "bx"),) * 4 + (P("by", "bx"),),
        check_vma=False,
    )
```

profile of v0, /device:TPU:0, one launch (start us, length us, event | category | flops | bytes accessed | tf_op | source)
XLA Modules:
  0.0 77.9 jit_solution(13218163723108454211)
XLA Ops:
  1.7 1.0 %copy-done.1 = f32[62,8,256]{2,1,0:T(8,128)S(1)} copy-done((f32[62,8,256]{2,1,0:T(8,128)S(1)}, f32[62,8,256]{2,1,0:T(8,128)}, u32[]{:S(2)}) %copy-start.1) | copy-done | bytes 507928
  2.7 1.0 %copy-done.2 = f32[62,8,256]{2,1,0:T(8,128)S(1)} copy-done((f32[62,8,256]{2,1,0:T(8,128)S(1)}, f32[62,8,256]{2,1,0:T(8,128)}, u32[]{:S(2)}) %copy-start.2) | copy-done | bytes 507928
  6.9 1.1 %pack.1 = (f32[4,4,2,8,256]{4,3,2,1,0:T(8,128)S(1)}, f32[4,4,2,8,256]{4,3,2,1,0:T(8,128)S(1)}, f32[4,4,2,8,256]{4,3,2,1,0:T(8,128)S(1)}, f32[4,4,2,8,256]{4,3,2,...) custom-call(f32[496,256]{1,0:T(8,128)S(1)} %bitcast.8, ...), custom_call_target="tpu_custom_call" | custom-call | tf_op jit(solution)/shard_map/pack/pallas_call | solution.py:126
  8.0 3.4 %collective-permute-start.2 = (f32[2,8,8,128]{3,2,1,0:T(8,128)S(1)}, f32[2,8,8,128]{3,2,1,0:T(8,128)S(1)}, u32[]{:S(2)}, u32[]{:S(2)}) collective-permute-start(f32[2,8,8,128]{3,2,1,0:T(8,128)S(1)} %get-tuple-element.59), channel_id=1, source_target_pairs={{1,0},{2,1},{3,2},{4,3},{5,4},{6,5},{7,6},{0,7},{9,8},{10,9},{11,1... | collective-permute-start | bytes 196616 | tf_op jit(solution)/shard_map/ppermute | solution.py:508
  11.4 3.5 %collective-permute-start = (f32[4,4,2,8,256]{4,3,2,1,0:T(8,128)S(1)}, f32[4,4,2,8,256]{4,3,2,1,0:T(8,128)S(1)}, u32[]{:S(2)}, u32[]{:S(2)}) collective-permute-start(f32[4,4,2,8,256]{4,3,2,1,0:T(8,128)S(1)} %get-tuple-element.57.refs_3_), channel_id=1, source_target_pairs={{0,8},{8,16},{16,24},{1,9},{9,17},{17,25},{2,10},{10,18},{18,26},{... | collective-permute-start | bytes 786440 | tf_op jit(solution)/shard_map/ppermute | solution.py:512
  14.9 1.3 %collective-permute-start.1 = (f32[4,4,2,8,256]{4,3,2,1,0:T(8,128)S(1)}, f32[4,4,2,8,256]{4,3,2,1,0:T(8,128)S(1)}, u32[]{:S(2)}, u32[]{:S(2)}) collective-permute-start(f32[4,4,2,8,256]{4,3,2,1,0:T(8,128)S(1)} %get-tuple-element.58.refs_2_), channel_id=1, source_target_pairs={{8,0},{16,8},{24,16},{9,1},{17,9},{25,17},{10,2},{18,10},{26,18},{... | collective-permute-start | bytes 786440 | tf_op jit(solution)/shard_map/ppermute | solution.py:512
  16.3 4.5 %collective-permute-start.4 = (f32[2,8,8,128]{3,2,1,0:T(8,128)S(1)}, f32[2,8,8,128]{3,2,1,0:T(8,128)S(1)}, u32[]{:S(2)}, u32[]{:S(2)}) collective-permute-start(f32[2,8,8,128]{3,2,1,0:T(8,128)S(1)} %pad_maximum_fusion), channel_id=1, source_target_pairs={{0,8},{8,16},{16,24},{1,9},{9,17},{17,25},{2,10},{10,18},{18,26},{... | collective-permute-start | bytes 196616 | tf_op jit(solution)/shard_map/ppermute | solution.py:515
  20.8 1.3 %collective-permute-start.5 = (f32[2,8,8,128]{3,2,1,0:T(8,128)S(1)}, f32[2,8,8,128]{3,2,1,0:T(8,128)S(1)}, u32[]{:S(2)}, u32[]{:S(2)}) collective-permute-start(f32[2,8,8,128]{3,2,1,0:T(8,128)S(1)} %pad_maximum_fusion.1), channel_id=1, source_target_pairs={{8,0},{16,8},{24,16},{9,1},{17,9},{25,17},{10,2},{18,10},{26,18},{... | collective-permute-start | bytes 196616 | tf_op jit(solution)/shard_map/ppermute | solution.py:516
  22.7 4.3 %collective-permute-done.5.refs_8_ = f32[2,8,8,128]{3,2,1,0:T(8,128)S(1)} collective-permute-done((f32[2,8,8,128]{3,2,1,0:T(8,128)S(1)}, f32[2,8,8,128]{3,2,1,0:T(8,128)S(1)}, u32[]{:S(2)}, u32[]{:S(2)}) %collective-permute-start.5) | collective-permute-done | bytes 65568 | tf_op jit(solution)/shard_map/ppermute | solution.py:516
  27.0 3.5 %collective-permute-start.6 = (f32[4,4,2,8,256]{4,3,2,1,0:T(8,128)S(1)}, f32[4,4,2,8,256]{4,3,2,1,0:T(8,128)S(1)}, u32[]{:S(2)}, u32[]{:S(2)}) collective-permute-start(f32[4,4,2,8,256]{4,3,2,1,0:T(8,128)S(1)} %get-tuple-element.63.refs_3_), channel_id=1, source_target_pairs={{0,8},{8,16},{16,24},{1,9},{9,17},{17,25},{2,10},{10,18},{18,26},{... | collective-permute-start | bytes 786440 | tf_op jit(solution)/shard_map/ppermute | solution.py:512
  30.5 1.3 %collective-permute-start.7 = (f32[4,4,2,8,256]{4,3,2,1,0:T(8,128)S(1)}, f32[4,4,2,8,256]{4,3,2,1,0:T(8,128)S(1)}, u32[]{:S(2)}, u32[]{:S(2)}) collective-permute-start(f32[4,4,2,8,256]{4,3,2,1,0:T(8,128)S(1)} %get-tuple-element.64.refs_2_), channel_id=1, source_target_pairs={{8,0},{16,8},{24,16},{9,1},{17,9},{25,17},{10,2},{18,10},{26,18},{... | collective-permute-start | bytes 786440 | tf_op jit(solution)/shard_map/ppermute | solution.py:512
  31.8 5.3 %step.4 = (f32[496,256]{1,0:T(8,128)}, f32[496,256]{1,0:T(8,128)}, f32[496,256]{1,0:T(8,128)}, f32[496,256]{1,0:T(8,128)}, f32[16,384]{1,0:T(8,128)S(1)}, /*inde...) custom-call(f32[16]{0:T(128)S(1)} %sine_multiply_fusion.refs_0_, ...), custom_call_target="tpu_custom_call" | custom-call | tf_op jit(solution)/shard_map/step/pallas_call | solution.py:417
  37.2 4.6 %collective-permute-start.10 = (f32[4,4,2,8,256]{4,3,2,1,0:T(8,128)S(1)}, f32[4,4,2,8,256]{4,3,2,1,0:T(8,128)S(1)}, u32[]{:S(2)}, u32[]{:S(2)}) collective-permute-start(f32[4,4,2,8,256]{4,3,2,1,0:T(8,128)S(1)} %get-tuple-element.84.refs_3_), channel_id=1, source_target_pairs={{0,8},{8,16},{16,24},{1,9},{9,17},{17,25},{2,10},{10,18},{18,26},{... | collective-permute-start | bytes 786440 | tf_op jit(solution)/shard_map/ppermute | solution.py:512
  41.8 1.3 %collective-permute-start.11 = (f32[4,4,2,8,256]{4,3,2,1,0:T(8,128)S(1)}, f32[4,4,2,8,256]{4,3,2,1,0:T(8,128)S(1)}, u32[]{:S(2)}, u32[]{:S(2)}) collective-permute-start(f32[4,4,2,8,256]{4,3,2,1,0:T(8,128)S(1)} %get-tuple-element.85.refs_2_), channel_id=1, source_target_pairs={{8,0},{16,8},{24,16},{9,1},{17,9},{25,17},{10,2},{18,10},{26,18},{... | collective-permute-start | bytes 786440 | tf_op jit(solution)/shard_map/ppermute | solution.py:512
  43.1 5.1 %step.5 = (f32[496,256]{1,0:T(8,128)}, f32[496,256]{1,0:T(8,128)}, f32[496,256]{1,0:T(8,128)}, f32[496,256]{1,0:T(8,128)}, f32[24,8,384]{2,1,0:T(8,128)S(1)}, /*index=5*/f32[2,8,8,384]{3,2,1,0:T(8,128)S(1)}) custom-call(f32[16]{0:T(128)S(1)} %sine_multiply_fusion.refs_0_, ...), custom_call_target="tpu_custom_call", output_to_operand_aliasing={{0}: (12, {}), {1}: (13, {}), {2}: (14, {}), {3}: (15, {})} | custom-call | tf_op jit(solution)/shard_map/step/pallas_call | solution.py:417
  48.2 4.6 %collective-permute-start.8 = (f32[4,4,2,8,256]{4,3,2,1,0:T(8,128)S(1)}, f32[4,4,2,8,256]{4,3,2,1,0:T(8,128)S(1)}, u32[]{:S(2)}, u32[]{:S(2)}) collective-permute-start(f32[4,4,2,8,256]{4,3,2,1,0:T(8,128)S(1)} %get-tuple-element.82.refs_3_), channel_id=1, source_target_pairs={{0,8},{8,16},{16,24},{1,9},{9,17},{17,25},{2,10},{10,18},{18,26},{... | collective-permute-start | bytes 786440 | tf_op jit(solution)/shard_map/ppermute | solution.py:512
  52.8 1.3 %collective-permute-start.9 = (f32[4,4,2,8,256]{4,3,2,1,0:T(8,128)S(1)}, f32[4,4,2,8,256]{4,3,2,1,0:T(8,128)S(1)}, u32[]{:S(2)}, u32[]{:S(2)}) collective-permute-start(f32[4,4,2,8,256]{4,3,2,1,0:T(8,128)S(1)} %get-tuple-element.83.refs_2_), channel_id=1, source_target_pairs={{8,0},{16,8},{24,16},{9,1},{17,9},{25,17},{10,2},{18,10},{26,18},{... | collective-permute-start | bytes 786440 | tf_op jit(solution)/shard_map/ppermute | solution.py:512
  54.1 5.2 %step.6 = (f32[496,256]{1,0:T(8,128)}, f32[496,256]{1,0:T(8,128)}, f32[496,256]{1,0:T(8,128)}, f32[496,256]{1,0:T(8,128)}, f32[24,8,384]{2,1,0:T(8,128)S(1)}, /*index=5*/f32[2,8,8,384]{3,2,1,0:T(8,128)S(1)}) custom-call(f32[16]{0:T(128)S(1)} %sine_multiply_fusion.refs_0_, ...), custom_call_target="tpu_custom_call", output_to_operand_aliasing={{0}: (12, {}), {1}: (13, {}), {2}: (14, {}), {3}: (15, {})} | custom-call | tf_op jit(solution)/shard_map/step/pallas_call | solution.py:417
  59.3 1.8 %collective-permute-done.9.refs_4_ = f32[4,4,2,8,256]{4,3,2,1,0:T(8,128)S(1)} collective-permute-done((f32[4,4,2,8,256]{4,3,2,1,0:T(8,128)S(1)}, f32[4,4,2,8,256]{4,3,2,1,0:T(8,128)S(1)}, u32[]{:S(2)}, u32[]{:S(2)}) %collective-permute-start.9) | collective-permute-done | bytes 262176 | tf_op jit(solution)/shard_map/ppermute | solution.py:512
  61.1 5.1 %step.7 = (f32[496,256]{1,0:T(8,128)}, f32[496,256]{1,0:T(8,128)}, f32[496,256]{1,0:T(8,128)}, f32[496,256]{1,0:T(8,128)}, f32[2,4,384]{2,1,0:T(4,128)S(1)}, /*index=5*/f32[2,4,384]{2,1,0:T(4,128)S(1)}) custom-call(f32[16]{0:T(128)S(1)} %sine_multiply_fusion.refs_0_, ...), custom_call_target="tpu_custom_call", output_to_operand_aliasing={{0}: (12, {}), {1}: (13, {}), {2}: (14, {}), {3}: (15, {})} | custom-call | tf_op jit(solution)/shard_map/step/pallas_call | solution.py:417
  66.2 3.5 %collective-permute-start.12 = (f32[2,4,384]{2,1,0:T(4,128)S(1)}, f32[2,4,384]{2,1,0:T(4,128)S(1)}, u32[]{:S(2)}, u32[]{:S(2)}) collective-permute-start(f32[2,4,384]{2,1,0:T(4,128)S(1)} %get-tuple-element.103.high), channel_id=1, source_target_pairs={{0,8},{8,16},{16,24},{1,9},{9,17},{17,25},{2,10},{10,18},{18,26},{... | collective-permute-start | bytes 36872 | tf_op jit(solution)/shard_map/ppermute | solution.py:541
  69.7 1.3 %collective-permute-start.13 = (f32[2,4,384]{2,1,0:T(4,128)S(1)}, f32[2,4,384]{2,1,0:T(4,128)S(1)}, u32[]{:S(2)}, u32[]{:S(2)}) collective-permute-start(f32[2,4,384]{2,1,0:T(4,128)S(1)} %get-tuple-element.104.low), channel_id=1, source_target_pairs={{8,0},{16,8},{24,16},{9,1},{17,9},{25,17},{10,2},{18,10},{26,18},{... | collective-permute-start | bytes 36872 | tf_op jit(solution)/shard_map/ppermute | solution.py:542
  71.0 4.2 %collective-permute-done.13.north = f32[2,4,384]{2,1,0:T(4,128)S(1)} collective-permute-done((f32[2,4,384]{2,1,0:T(4,128)S(1)}, f32[2,4,384]{2,1,0:T(4,128)S(1)}, u32[]{:S(2)}, u32[]{:S(2)}) %collective-permute-start.13) | collective-permute-done | bytes 12320 | tf_op jit(solution)/shard_map/ppermute | solution.py:542
  75.8 2.1 %solve.1 = f32[8,256]{1,0:T(8,128)} custom-call(f32[16,384]{1,0:T(8,128)} %copy-done.4, f32[16,384]{1,0:T(8,128)} %copy-done.5, f32[2,4,384]{2,1,0:T(4,128)} %copy-done.11, f32[2,4,384]{2,1,0:T(4,128)} %copy-done.7, f32[2,4,384]{2,1,0:T(4,128)} %copy-done.8, f32[2,4,384]{2,1,0:T(4,128)} %copy-done.12), custom_call_target="tpu_custom_call" | custom-call | tf_op jit(solution)/shard_map/solve/pallas_call | solution.py:543
  (41 shorter events, 5.5 us)
Async XLA Ops:
  0.6 1.0 %copy-start = (f32[62,8,256]{2,1,0:T(8,128)S(1)}, f32[62,8,256]{2,1,0:T(8,128)}, u32[]{:S(2)}) copy-start(f32[62,8,256]{2,1,0:T(8,128)} %param.7) | copy-start | bytes 1523716
  1.7 1.0 %copy-start.1 = (f32[62,8,256]{2,1,0:T(8,128)S(1)}, f32[62,8,256]{2,1,0:T(8,128)}, u32[]{:S(2)}) copy-start(f32[62,8,256]{2,1,0:T(8,128)} %param.8) | copy-start | bytes 1523716
  2.7 1.0 %copy-start.2 = (f32[62,8,256]{2,1,0:T(8,128)S(1)}, f32[62,8,256]{2,1,0:T(8,128)}, u32[]{:S(2)}) copy-start(f32[62,8,256]{2,1,0:T(8,128)} %param.9) | copy-start | bytes 1523716
  3.7 1.0 %copy-start.3 = (f32[62,8,256]{2,1,0:T(8,128)S(1)}, f32[62,8,256]{2,1,0:T(8,128)}, u32[]{:S(2)}) copy-start(f32[62,8,256]{2,1,0:T(8,128)} %param.10) | copy-start | bytes 1523716
  4.8 0.7 copy-start.6
  8.0 8.2 %collective-permute-start.2 = (f32[2,8,8,128]{3,2,1,0:T(8,128)S(1)}, f32[2,8,8,128]{3,2,1,0:T(8,128)S(1)}, u32[]{:S(2)}, u32[]{:S(2)}) collective-permute-start(f32[2,8,8,128]{3,2,1,0:T(8,128)S(1)} %get-tuple-element.59), channel_id=1, source_target_pairs={{1,0},{2,1},{3,2},{4,3},{5,4},{6,5},{7,6},{0,7},{9,8},{10,9},{11,1... | collective-permute-start | bytes 196616 | tf_op jit(solution)/shard_map/ppermute | solution.py:508
  11.4 4.8 %collective-permute-start.3 = (f32[2,8,8,128]{3,2,1,0:T(8,128)S(1)}, f32[2,8,8,128]{3,2,1,0:T(8,128)S(1)}, u32[]{:S(2)}, u32[]{:S(2)}) collective-permute-start(f32[2,8,8,128]{3,2,1,0:T(8,128)S(1)} %get-tuple-element.60), channel_id=1, source_target_pairs={{0,1},{1,2},{2,3},{3,4},{4,5},{5,6},{6,7},{7,0},{8,9},{9,10},{10,1... | collective-permute-start | bytes 196616 | tf_op jit(solution)/shard_map/ppermute | solution.py:509
  11.4 15.6 %collective-permute-start = (f32[4,4,2,8,256]{4,3,2,1,0:T(8,128)S(1)}, f32[4,4,2,8,256]{4,3,2,1,0:T(8,128)S(1)}, u32[]{:S(2)}, u32[]{:S(2)}) collective-permute-start(f32[4,4,2,8,256]{4,3,2,1,0:T(8,128)S(1)} %get-tuple-element.57.refs_3_), channel_id=1, source_target_pairs={{0,8},{8,16},{16,24},{1,9},{9,17},{17,25},{2,10},{10,18},{18,26},{... | collective-permute-start | bytes 786440 | tf_op jit(solution)/shard_map/ppermute | solution.py:512
  14.9 12.1 %collective-permute-start.1 = (f32[4,4,2,8,256]{4,3,2,1,0:T(8,128)S(1)}, f32[4,4,2,8,256]{4,3,2,1,0:T(8,128)S(1)}, u32[]{:S(2)}, u32[]{:S(2)}) collective-permute-start(f32[4,4,2,8,256]{4,3,2,1,0:T(8,128)S(1)} %get-tuple-element.58.refs_2_), channel_id=1, source_target_pairs={{8,0},{16,8},{24,16},{9,1},{17,9},{25,17},{10,2},{18,10},{26,18},{... | collective-permute-start | bytes 786440 | tf_op jit(solution)/shard_map/ppermute | solution.py:512
  16.3 6.4 %collective-permute-start.4 = (f32[2,8,8,128]{3,2,1,0:T(8,128)S(1)}, f32[2,8,8,128]{3,2,1,0:T(8,128)S(1)}, u32[]{:S(2)}, u32[]{:S(2)}) collective-permute-start(f32[2,8,8,128]{3,2,1,0:T(8,128)S(1)} %pad_maximum_fusion), channel_id=1, source_target_pairs={{0,8},{8,16},{16,24},{1,9},{9,17},{17,25},{2,10},{10,18},{18,26},{... | collective-permute-start | bytes 196616 | tf_op jit(solution)/shard_map/ppermute | solution.py:515
  20.8 6.2 %collective-permute-start.5 = (f32[2,8,8,128]{3,2,1,0:T(8,128)S(1)}, f32[2,8,8,128]{3,2,1,0:T(8,128)S(1)}, u32[]{:S(2)}, u32[]{:S(2)}) collective-permute-start(f32[2,8,8,128]{3,2,1,0:T(8,128)S(1)} %pad_maximum_fusion.1), channel_id=1, source_target_pairs={{8,0},{16,8},{24,16},{9,1},{17,9},{25,17},{10,2},{18,10},{26,18},{... | collective-permute-start | bytes 196616 | tf_op jit(solution)/shard_map/ppermute | solution.py:516
  27.0 16.1 %collective-permute-start.6 = (f32[4,4,2,8,256]{4,3,2,1,0:T(8,128)S(1)}, f32[4,4,2,8,256]{4,3,2,1,0:T(8,128)S(1)}, u32[]{:S(2)}, u32[]{:S(2)}) collective-permute-start(f32[4,4,2,8,256]{4,3,2,1,0:T(8,128)S(1)} %get-tuple-element.63.refs_3_), channel_id=1, source_target_pairs={{0,8},{8,16},{16,24},{1,9},{9,17},{17,25},{2,10},{10,18},{18,26},{... | collective-permute-start | bytes 786440 | tf_op jit(solution)/shard_map/ppermute | solution.py:512
  30.5 12.6 %collective-permute-start.7 = (f32[4,4,2,8,256]{4,3,2,1,0:T(8,128)S(1)}, f32[4,4,2,8,256]{4,3,2,1,0:T(8,128)S(1)}, u32[]{:S(2)}, u32[]{:S(2)}) collective-permute-start(f32[4,4,2,8,256]{4,3,2,1,0:T(8,128)S(1)} %get-tuple-element.64.refs_2_), channel_id=1, source_target_pairs={{8,0},{16,8},{24,16},{9,1},{17,9},{25,17},{10,2},{18,10},{26,18},{... | collective-permute-start | bytes 786440 | tf_op jit(solution)/shard_map/ppermute | solution.py:512
  37.2 11.0 %copy-start.5 = (f32[16,384]{1,0:T(8,128)}, f32[16,384]{1,0:T(8,128)S(1)}, u32[]{:S(2)}) copy-start(f32[16,384]{1,0:T(8,128)S(1)} %get-tuple-element.102.surface_ref) | copy-start | bytes 73732
  37.2 23.9 %copy-start.4 = (f32[16,384]{1,0:T(8,128)}, f32[16,384]{1,0:T(8,128)S(1)}, u32[]{:S(2)}) copy-start(f32[16,384]{1,0:T(8,128)S(1)} %get-tuple-element.69.refs_9_.deep_ref) | copy-start | bytes 73732
  37.2 16.9 %collective-permute-start.10 = (f32[4,4,2,8,256]{4,3,2,1,0:T(8,128)S(1)}, f32[4,4,2,8,256]{4,3,2,1,0:T(8,128)S(1)}, u32[]{:S(2)}, u32[]{:S(2)}) collective-permute-start(f32[4,4,2,8,256]{4,3,2,1,0:T(8,128)S(1)} %get-tuple-element.84.refs_3_), channel_id=1, source_target_pairs={{0,8},{8,16},{16,24},{1,9},{9,17},{17,25},{2,10},{10,18},{18,26},{... | collective-permute-start | bytes 786440 | tf_op jit(solution)/shard_map/ppermute | solution.py:512
  41.8 12.3 %collective-permute-start.11 = (f32[4,4,2,8,256]{4,3,2,1,0:T(8,128)S(1)}, f32[4,4,2,8,256]{4,3,2,1,0:T(8,128)S(1)}, u32[]{:S(2)}, u32[]{:S(2)}) collective-permute-start(f32[4,4,2,8,256]{4,3,2,1,0:T(8,128)S(1)} %get-tuple-element.85.refs_2_), channel_id=1, source_target_pairs={{8,0},{16,8},{24,16},{9,1},{17,9},{25,17},{10,2},{18,10},{26,18},{... | collective-permute-start | bytes 786440 | tf_op jit(solution)/shard_map/ppermute | solution.py:512
  48.2 11.1 %collective-permute-start.8 = (f32[4,4,2,8,256]{4,3,2,1,0:T(8,128)S(1)}, f32[4,4,2,8,256]{4,3,2,1,0:T(8,128)S(1)}, u32[]{:S(2)}, u32[]{:S(2)}) collective-permute-start(f32[4,4,2,8,256]{4,3,2,1,0:T(8,128)S(1)} %get-tuple-element.82.refs_3_), channel_id=1, source_target_pairs={{0,8},{8,16},{16,24},{1,9},{9,17},{17,25},{2,10},{10,18},{18,26},{... | collective-permute-start | bytes 786440 | tf_op jit(solution)/shard_map/ppermute | solution.py:512
  52.8 8.3 %collective-permute-start.9 = (f32[4,4,2,8,256]{4,3,2,1,0:T(8,128)S(1)}, f32[4,4,2,8,256]{4,3,2,1,0:T(8,128)S(1)}, u32[]{:S(2)}, u32[]{:S(2)}) collective-permute-start(f32[4,4,2,8,256]{4,3,2,1,0:T(8,128)S(1)} %get-tuple-element.83.refs_2_), channel_id=1, source_target_pairs={{8,0},{16,8},{24,16},{9,1},{17,9},{25,17},{10,2},{18,10},{26,18},{... | collective-permute-start | bytes 786440 | tf_op jit(solution)/shard_map/ppermute | solution.py:512
  66.2 9.1 %copy-start.7 = (f32[2,4,384]{2,1,0:T(4,128)}, f32[2,4,384]{2,1,0:T(4,128)S(1)}, u32[]{:S(2)}) copy-start(f32[2,4,384]{2,1,0:T(4,128)S(1)} %get-tuple-element.104.low) | copy-start | bytes 36868
  66.2 9.1 %copy-start.8 = (f32[2,4,384]{2,1,0:T(4,128)}, f32[2,4,384]{2,1,0:T(4,128)S(1)}, u32[]{:S(2)}) copy-start(f32[2,4,384]{2,1,0:T(4,128)S(1)} %get-tuple-element.103.high) | copy-start | bytes 36868
  66.2 4.9 %collective-permute-start.12 = (f32[2,4,384]{2,1,0:T(4,128)S(1)}, f32[2,4,384]{2,1,0:T(4,128)S(1)}, u32[]{:S(2)}, u32[]{:S(2)}) collective-permute-start(f32[2,4,384]{2,1,0:T(4,128)S(1)} %get-tuple-element.103.high), channel_id=1, source_target_pairs={{0,8},{8,16},{16,24},{1,9},{9,17},{17,25},{2,10},{10,18},{18,26},{... | collective-permute-start | bytes 36872 | tf_op jit(solution)/shard_map/ppermute | solution.py:541
  69.7 5.6 %collective-permute-start.13 = (f32[2,4,384]{2,1,0:T(4,128)S(1)}, f32[2,4,384]{2,1,0:T(4,128)S(1)}, u32[]{:S(2)}, u32[]{:S(2)}) collective-permute-start(f32[2,4,384]{2,1,0:T(4,128)S(1)} %get-tuple-element.104.low), channel_id=1, source_target_pairs={{8,0},{16,8},{24,16},{9,1},{17,9},{25,17},{10,2},{18,10},{26,18},{... | collective-permute-start | bytes 36872 | tf_op jit(solution)/shard_map/ppermute | solution.py:542
  71.0 4.2 %copy-start.11 = (f32[2,4,384]{2,1,0:T(4,128)}, f32[2,4,384]{2,1,0:T(4,128)S(1)}, u32[]{:S(2)}) copy-start(f32[2,4,384]{2,1,0:T(4,128)S(1)} %collective-permute-done.12.south) | copy-start | bytes 36868
  (3 other events, 2.0 us)
where the time goes:
time: 78.7 us; the launch traced here: 77.9 us
  starting transfers between devices  35.2 us (45%)
  Pallas kernels  23.9 us (30%)
  waiting for transfers between devices  10.9 us (14%)
  local copies, waits for them, and re-layouts  6.87 us (9%)
  between operations  0.93 us (1%)
    pallas_call x4, Pallas kernels, step(): pl.pallas_call(functools.partial(step_kernel, chunk, rows), out_shape=sha...  20.7 us
    ppermute x4, starting transfers between devices, send(): lax.ppermute(high, 'by', to_north)  16.1 us
    unnamed x26, local copies, waits for them, and re-layouts  6.85 us
    ppermute x4, starting transfers between devices, send(): lax.ppermute(low, 'by', to_south)  5.17 us
    ppermute x1, starting transfers between devices, body(): lax.ppermute(jnp.stack([from_east[1], from_west[1]]), 'by', to_north)  4.55 us
    ppermute x1, waiting for transfers between devices, body(): lax.ppermute(jnp.stack([from_east[0], from_west[0]]), 'by', to_south)  4.29 us
    ppermute x1, waiting for transfers between devices, body(): north = lax.ppermute(low, 'by', to_south)  4.2 us
    ppermute x1, starting transfers between devices, body(): south = lax.ppermute(high, 'by', to_north)  3.46 us
  transfers between devices with their start and end apart: 14, of which 5 were waited for; matrix products, arithmetic and copies ran while one was open for 0% of the time, Pallas kernels for 20%

commit v1 on v0

v1 whole, which is shorter than its diff:
```python
import functools
import math

import jax
import jax.numpy as jnp
from jax import lax
from jax.experimental import pallas as pl
from jax.experimental.pallas import tpu as pltpu
from jax.sharding import PartitionSpec as P

ITERS = 4
KAPPA = 0.004
ADVECT = 0.25
PRESS = 0.1
WIND = 0.5
PHI = 0.5
DIVERGE = 2.0
LOWER = 0.2
UPPER = 2.0

SUB = 8
LANES = 128
FIELDS = 4
RIM = 4
EDGE = 8
EXTRA = 2
CHUNKS = (2, 2, 2, 2)
AHEAD = 3
FAR = 1000000
BATCH = 4
GROUPS = ((0, 1), (2, 3))
SMALL_VMEM = 4 * 1024 * 1024
PACK_VMEM = 103 * 512 * 1024
F32 = jnp.float32


def chebyshev_weights(count):
    middle = 0.5 * (UPPER + LOWER)
    half_span = 0.5 * (UPPER - LOWER)
    ratio_value = middle / half_span
    rho_now = 1.0 / ratio_value
    updates = []
    for index in range(count - 1):
        rho_next = 1.0 / (2.0 * ratio_value - rho_now)
        updates.append((rho_next * rho_now, 2.0 * rho_next / half_span))
        rho_now = rho_next
    return (1.0 / middle, updates)


def swaps(count, first, ring):
    pairs = []
    for i in range(first, count if ring else count - 1, 2):
        j = (i + 1) % count
        pairs += [(i, j), (j, i)]
    return pairs


def first_level(chunk):
    return SUB * sum(CHUNKS[:chunk]) - (EXTRA if chunk else 0)


def chunk_levels(chunk):
    return SUB * CHUNKS[chunk] - (0 if chunk else EXTRA)


def parities():
    return lax.axis_index("by") & 1, lax.axis_index("bx") & 1


def first_rows():
    odd = lax.axis_index("by") & 1
    return (1 - odd) * RIM, odd * RIM


def place_tile(half, held, rows, group, f, chunk, t, line):
    used = min(SUB, chunk_levels(chunk) - SUB * t)
    base = (first_level(chunk) + SUB * t) * rows
    first = first_rows()[group]
    for q in range(RIM):
        for lane in range(2):
            half[f * RIM + q, t, pl.ds(0, used), pl.ds(lane * LANES, LANES)] = held[
                f, lane, pl.ds(base + first + q, used, stride=rows), :
            ]
        for extra in range(SUB - used):
            half[f * RIM + q, t, pl.ds(used + extra, 1), :] = line(f, extra, first + q)


def pack_kernel(rows, *refs):
    fields = refs[:FIELDS]
    flat = refs[FIELDS]
    *halves, across_a, across_b, held, sems = refs[FIELDS + 1 :]

    def copy(f, lane):
        return pltpu.make_async_copy(
            fields[f].at[:, pl.ds(lane * LANES, LANES)], held.at[f, lane], sems.at[f, lane]
        )

    for f in range(FIELDS):
        for lane in range(2):
            copy(f, lane).start()

    def line(f, extra, row):
        if f < 2:
            return flat[EXTRA * f + extra, pl.ds(row, 1), :]
        return jnp.zeros((1, 2 * LANES), F32)

    for f in range(FIELDS):
        for lane in range(2):
            copy(f, lane).wait()
        for c in range(len(CHUNKS)):
            for t in range(CHUNKS[c]):
                for group in range(2):
                    place_tile(halves[2 * c + group], held, rows, group, f, c, t, line)
    lanes = lax.broadcasted_iota(jnp.int32, (SUB, LANES), 1)
    odd = jnp.broadcast_to(lax.axis_index("bx") & 1, (SUB, LANES)) == 1
    slot = 0
    for c in range(len(CHUNKS)):
        for t in range(CHUNKS[c]):
            for group in range(2):
                west = jnp.zeros((SUB, LANES), F32)
                east = jnp.zeros((SUB, LANES), F32)
                for q in range(RIM):
                    for f in range(FIELDS):
                        place = (q * FIELDS + f) * EDGE
                        other = (place - EDGE) % LANES
                        block = halves[2 * c + group][f * RIM + q, t]
                        low = block[:, :LANES]
                        high = block[:, LANES:]
                        if place:
                            low = pltpu.roll(low, place, 1)
                            high = pltpu.roll(high, place, 1)
                        west = jnp.where((lanes >= place) & (lanes < place + EDGE), low, west)
                        east = jnp.where((lanes >= other) & (lanes < other + EDGE), high, east)
                across_a[group, slot] = jnp.where(odd, west, east)
                across_b[group, slot] = jnp.where(odd, east, west)
            slot += 1


def half_shapes(columns):
    return [
        jax.ShapeDtypeStruct((FIELDS * RIM + 1, tiles, SUB, columns), F32)
        for tiles in CHUNKS
        for _ in range(2)
    ]


def pack(fields, lines):
    levels, rows, columns = fields[0].shape
    flat = [item.reshape(levels * rows, columns) for item in fields]
    shapes = half_shapes(columns)
    shapes += [jax.ShapeDtypeStruct((2, sum(CHUNKS), SUB, LANES), F32)] * 2
    *halves, across_a, across_b = pl.pallas_call(
        functools.partial(pack_kernel, rows),
        out_shape=shapes,
        in_specs=[pl.BlockSpec(memory_space=pltpu.HBM)] * FIELDS
        + [pl.BlockSpec(memory_space=pltpu.VMEM)],
        out_specs=[pl.BlockSpec(memory_space=pltpu.VMEM)] * len(shapes),
        scratch_shapes=[
            pltpu.VMEM((FIELDS, 2, levels * rows, LANES), F32),
            pltpu.SemaphoreType.DMA((FIELDS, 2)),
        ],
        compiler_params=pltpu.CompilerParams(vmem_limit_bytes=PACK_VMEM),
        name="pack",
    )(*flat, lines)
    return halves, across_a, across_b


def rims_kernel(across_a, across_b, *refs):
    count = 2 * len(CHUNKS)
    halves, sems = refs[count : 2 * count], refs[2 * count]
    copies = []
    for k, half in enumerate(halves):
        slots = pl.ds(sum(CHUNKS[: k // 2]), CHUNKS[k // 2])
        for lane, across in enumerate((across_a, across_b)):
            copies.append(
                pltpu.make_async_copy(
                    across.at[k % 2, slots],
                    half.at[FIELDS * RIM, :, :, pl.ds(lane * LANES, LANES)],
                    sems.at[k, lane],
                )
            )
    for copy in copies:
        copy.start()
    for copy in copies:
        copy.wait()


def put_rims(halves, across_a, across_b):
    count = len(halves)
    anywhere = pl.BlockSpec(memory_space=pl.ANY)
    outs = pl.pallas_call(
        rims_kernel,
        out_shape=[jax.ShapeDtypeStruct(item.shape, F32) for item in halves],
        in_specs=[anywhere] * (count + 2),
        out_specs=[anywhere] * count,
        scratch_shapes=[pltpu.SemaphoreType.DMA((count, 2))],
        input_output_aliases={2 + k: k for k in range(count)},
        compiler_params=pltpu.CompilerParams(vmem_limit_bytes=SMALL_VMEM),
        name="rims",
    )(across_a, across_b, *halves)
    return [list(outs[k : k + 2]) for k in range(0, count, 2)]


def east_of(value):
    return pltpu.roll(value, value.shape[-1] - 1, value.ndim - 1)


def west_of(value):
    return pltpu.roll(value, 1, value.ndim - 1)


def step_kernel(chunk, rows, *refs):
    first = chunk == 0
    last = chunk == len(CHUNKS) - 1
    tiles = CHUNKS[chunk]
    levels = chunk_levels(chunk)
    tall = rows + 2 * RIM
    refs = list(refs)

    def take(count):
        taken = refs[:count]
        del refs[:count]
        return taken

    (rotate,) = take(1)
    met_a, own_a, own_b, met_b = blocks = take(4)
    if not first:
        deeps_in, carry_in, sums_in = take(3)
        take(FIELDS)
    outs = take(FIELDS)
    if first:
        deeps, depth_out, surface_out = take(3)
    else:
        deeps = deeps_in
    if last:
        sums_a, sums_b = take(2)
    else:
        carry_out, sums_out = take(2)
    cur, wets, wets_x, wets_w, wets_y, press, press_x, press_y, laps, mixes, between, held = take(12)
    if first:
        (winds,) = take(1)
    if last:
        carry, sums = take(2)
    else:
        carry, sums = carry_out, sums_out
    (sems,) = take(1)

    if first:
        carry[...] = jnp.zeros(carry.shape, F32)
        sums[...] = jnp.zeros(sums.shape, F32)
    else:
        carry[...] = carry_in[...]
        sums[...] = sums_in[...]

    lanes = lax.broadcasted_iota(jnp.int32, (SUB, LANES), 1)
    own = own_a.shape[-1]
    wide = own + LANES
    every = range(FIELDS)
    odd_y, odd_x = parities()
    bases = [odd_y * (RIM * k) + (1 - odd_y) * (RIM * (3 - k)) for k in range(4)]
    swapped = ((lanes // EDGE) & 1) != 1 - odd_x

    def rims_of(k, t):
        both = blocks[k][FIELDS * RIM, t]
        one, two = both[:, :LANES], both[:, LANES:]
        mixed = (jnp.where(swapped, one, two), jnp.where(swapped, two, one))

        def rim(f, q):
            place = (q * FIELDS + f) * EDGE
            return pltpu.roll(mixed[f % 2], LANES - place, 1) if place else mixed[f % 2]

        return rim

    if first:
        for k in range(4):
            rim = rims_of(k, tiles - 1)
            for q in range(RIM):
                block = [
                    jnp.concatenate([blocks[k][f * RIM + q, tiles - 1], rim(f, q)], axis=1)
                    for f in range(2)
                ]
                for f, extra, ref in (
                    (0, 0, deeps.at[0]),
                    (0, 1, deeps.at[1]),
                    (1, 0, winds.at[0]),
                    (1, 1, winds.at[1]),
                ):
                    slot = SUB - EXTRA + extra
                    ref[bases[k] + q] = jnp.broadcast_to(block[f][slot : slot + 1, :], (SUB, wide))
        for a in range(tall):
            surface_out[pl.ds(a, 1), :] = deeps[1, a, pl.ds(0, 1), :]
            depth_out[pl.ds(a, 1), :] = deeps[0, a, pl.ds(0, 1), :]
        for a in range(tall):
            here = deeps[0, a]
            deeps[1, a] = jnp.minimum(here, east_of(here))
            deeps[2, a] = jnp.minimum(here, west_of(here))
            deeps[3, a] = jnp.minimum(here, deeps[0, min(a + 1, tall - 1)])

    subs = lax.broadcasted_iota(jnp.int32, (SUB, wide), 0)

    def pressure(get, lowest, highest, carry_at):
        for first_row in range(lowest - 1, highest + 2, BATCH):
            rows_p = range(first_row, min(first_row + BATCH, highest + 2))
            sums_p = [
                ((-0.4 * PRESS) * get(2, a) + (0.3 * PRESS) * get(3, a)) * wets[a] for a in rows_p
            ]
            for shift in (1, 2, 4):
                moved = [pltpu.roll(value, shift, 0) for value in sums_p]
                sums_p = [
                    value + jnp.where(subs >= shift, other, 0.0)
                    for value, other in zip(sums_p, moved)
                ]
            places = [carry_at + a - (lowest - 1) for a in rows_p]
            sums_p = [value + carry[place] for value, place in zip(sums_p, places)]
            ends = [jnp.broadcast_to(value[SUB - 1 : SUB, :], value.shape) for value in sums_p]
            for k, a in enumerate(rows_p):
                press[a] = sums_p[k]
                carry[places[k]] = ends[k]
        slope = wets_y[lowest - 1] * (press[lowest] - press[lowest - 1])
        for first_row in range(lowest, highest + 1, BATCH):
            rows_p = range(first_row, min(first_row + BATCH, highest + 1))
            here = [press[a] for a in rows_p]
            east = [east_of(x) for x in here]
            west = [west_of(x) for x in here]
            across = [
                wets_x[a] * (east[k] - here[k]) + wets_w[a] * (here[k] - west[k])
                for k, a in enumerate(rows_p)
            ]
            here.append(press[rows_p[-1] + 1])
            slopes = [slope] + [
                wets_y[a] * (here[k + 1] - here[k]) for k, a in enumerate(rows_p)
            ]
            slope = slopes[-1]
            for k, a in enumerate(rows_p):
                press_x[a] = across[k]
                press_y[a] = slopes[k + 1] + slopes[k]

    def tendency(get, lowest, highest, carry_at, emit):
        pressure(get, lowest, highest, carry_at)
        for group in GROUPS:
            first_pass(get, lowest, highest, group)
        for group in GROUPS:
            second_pass(lowest, highest, group, emit)

    def turned(get, group, a):
        values = [get(f, a) for f in group]
        return values, [east_of(x) for x in values], [west_of(x) for x in values]

    def first_pass(get, lowest, highest, group):
        span = range(len(group))
        below = [get(f, lowest - 2) for f in group]
        here, east, west = turned(get, group, lowest - 1)
        face = wets_y[lowest - 2]
        up = [face * (x - y) for x, y in zip(here, below)]
        for a in range(lowest - 1, highest + 2):
            if a <= highest:
                after, east_after, west_after = turned(get, group, a + 1)
            else:
                after = [get(f, a + 1) for f in group]
            face, side_x, side_w = wets_y[a], wets_x[a], wets_w[a]
            up_before = up
            up = [face * (x - y) for x, y in zip(after, here)]
            right = [side_x * (x - y) for x, y in zip(east, here)]
            left = [side_w * (x - y) for x, y in zip(here, west)]
            lap = [(right[i] - left[i]) + (up[i] - up_before[i]) for i in span]
            if lowest <= a <= highest:
                flows = here if group[0] == 0 else [get(0, a), get(1, a)]
                u, v = (-0.5 * ADVECT) * flows[0], (-0.5 * ADVECT) * flows[1]
                mixed = [u * (right[i] + left[i]) + v * (up[i] + up_before[i]) for i in span]
                if group[0] == 0:
                    turn = rotate[pl.ds(a, 1), :] * wets[a]
                    mixed[0] = mixed[0] + (turn * here[1] - press_x[a])
                    mixed[1] = mixed[1] - (turn * here[0] + press_y[a])
                for i, f in enumerate(group):
                    mixes[f, a] = mixed[i]
            for i, f in enumerate(group):
                laps[f, a] = lap[i]
            if a <= highest:
                here, east, west = after, east_after, west_after

    def second_pass(lowest, highest, group, emit):
        span = range(len(group))

        def get(f, a):
            return laps[f, a]

        below = [get(f, lowest - 1) for f in group]
        here, east, west = turned(get, group, lowest)
        face = wets_y[lowest - 1]
        up = [face * (x - y) for x, y in zip(here, below)]
        for a in range(lowest, highest + 1):
            if a < highest:
                after, east_after, west_after = turned(get, group, a + 1)
            else:
                after = [get(f, a + 1) for f in group]
            face, side_x, side_w = wets_y[a], wets_x[a], wets_w[a]
            up_before = up
            up = [face * (x - y) for x, y in zip(after, here)]
            smooth = [
                (side_x * (east[i] - here[i]) - side_w * (here[i] - west[i]))
                + (up[i] - up_before[i])
                for i in span
            ]
            emit(a, group, [mixes[f, a] - KAPPA * smooth[i] for i, f in enumerate(group)])
            if a < highest:
                here, east, west = after, east_after, west_after

    def tile(t, _):
        for k in range(4):
            rim = rims_of(k, t)
            for q in range(RIM):
                for f in every:
                    cur[f, bases[k] + q, :, pl.ds(0, own)] = blocks[k][f * RIM + q, t]
                    cur[f, bases[k] + q, :, pl.ds(own, LANES)] = rim(f, q)
        level = subs + (first_level(chunk) + SUB * t)
        if first:
            level = jnp.where(level >= levels, FAR, level)
        level = level.astype(F32)
        top = jnp.where(level == 0.0, WIND, 0.0)
        for a in range(tall):
            for k, ref in enumerate((wets, wets_x, wets_w, wets_y)):
                ref[a] = jnp.where(level < deeps[k, a], 1.0, 0.0)

        def winded(a, group, values):
            if not first or group[0] != 0:
                return values
            windy = top * wets[a]
            return [values[f] + windy * winds[f, a] for f in range(2)] + values[2:]

        def emit_first(a, group, values):
            values = winded(a, group, values)
            values = [cur[f, a] + value for f, value in zip(group, values)]
            for f, value in zip(group, values):
                between[f, a] = value

        tendency(lambda f, a: cur[f, a], 2, tall - 3, 0, emit_first)

        def emit_second(a, group, values):
            values = winded(a, group, values)
            news = [0.5 * ((cur[f, a] + between[f, a]) + value) for f, value in zip(group, values)]
            r = a - RIM
            if group[0] == 0:
                adds = [sums[f, r] + wets[a] * news[f] for f in range(2)]
                for f in range(2):
                    sums[f, r] = adds[f]
            for f, new in zip(group, news):
                for lane in range(2):
                    held[f, lane, pl.ds(t * (SUB * rows) + r, SUB, stride=rows), :] = new[
                        :, lane * LANES : (lane + 1) * LANES
                    ]

        tendency(lambda f, a: between[f, a], RIM, tall - RIM - 1, tall - 2, emit_second)

        @pl.when(t < tiles - 1)
        def _():
            for f in every:
                for lane in range(2):
                    copy(f, lane, t, SUB).start()

        return 0

    def copy(f, lane, t, count):
        size = count * rows
        at = (first_level(chunk) + SUB * t) * rows
        return pltpu.make_async_copy(
            held.at[f, lane, pl.ds(t * (SUB * rows), size)],
            outs[f].at[pl.ds(at, size), pl.ds(lane * LANES, LANES)],
            sems.at[t, f, lane],
        )

    lax.fori_loop(0, tiles, tile, 0)
    final = levels - SUB * (tiles - 1)
    for f in every:
        for lane in range(2):
            copy(f, lane, tiles - 1, final).start()
    if last:
        depth_levels = first_level(chunk) + levels
        for f in range(2):
            for ref, at in ((sums_a, (1 - odd_y) * RIM), (sums_b, odd_y * RIM)):
                for q in range(RIM):
                    line = jnp.sum(sums[f, at + q], axis=0, keepdims=True) / depth_levels
                    ref[f, pl.ds(q, 1), :] = line
    for t in range(tiles):
        for f in every:
            for lane in range(2):
                copy(f, lane, t, final if t == tiles - 1 else SUB).wait()


def step(chunk, rows, levels, columns, rotate, blocks, kept, news):
    first = chunk == 0
    last = chunk == len(CHUNKS) - 1
    tiles = CHUNKS[chunk]
    wide = columns + LANES
    tall = rows + 2 * RIM
    vmem = pl.BlockSpec(memory_space=pltpu.VMEM)
    hbm = pl.BlockSpec(memory_space=pl.ANY)
    operands = [rotate, *blocks]
    in_specs = [vmem] * 5
    if not first:
        operands += [*kept, *news]
        in_specs += [vmem] * 3 + [hbm] * FIELDS
    carry = (tall - 2 + rows + 2, SUB, wide)
    sums = (2, rows, SUB, wide)
    shapes = [jax.ShapeDtypeStruct((levels * rows, columns), F32)] * FIELDS
    out_specs = [hbm] * FIELDS
    row = pltpu.VMEM((tall, SUB, wide), F32)
    fields = pltpu.VMEM((FIELDS, tall, SUB, wide), F32)
    scratch = [fields] + [row] * 7 + [fields] * 3
    scratch += [pltpu.VMEM((FIELDS, 2, tiles * SUB * rows, LANES), F32)]
    if first:
        shapes += [jax.ShapeDtypeStruct((4, tall, SUB, wide), F32)]
        shapes += [jax.ShapeDtypeStruct((tall, wide), F32)] * 2
        scratch += [pltpu.VMEM((2, tall, SUB, wide), F32)]
    if last:
        shapes += [jax.ShapeDtypeStruct((2, RIM, wide), F32)] * 2
        scratch += [pltpu.VMEM(carry, F32), pltpu.VMEM(sums, F32)]
    else:
        shapes += [jax.ShapeDtypeStruct(carry, F32), jax.ShapeDtypeStruct(sums, F32)]
    out_specs += [vmem] * (len(shapes) - FIELDS)
    scratch += [pltpu.SemaphoreType.DMA((tiles, FIELDS, 2))]
    aliases = {} if first else {len(operands) - FIELDS + f: f for f in range(FIELDS)}
    return pl.pallas_call(
        functools.partial(step_kernel, chunk, rows),
        out_shape=shapes,
        in_specs=in_specs,
        out_specs=out_specs,
        scratch_shapes=scratch,
        input_output_aliases=aliases,
        compiler_params=pltpu.CompilerParams(vmem_limit_bytes=16 * 1024 * 1024),
        name="step",
    )(*operands)


def shift_rows(x, count):
    return pltpu.roll(x, count % x.shape[0], 0)


def weighed(weights, e):
    east, west = east_of(e), west_of(e)
    return (
        weights[0] * shift_rows(east, -1) + weights[1] * shift_rows(west, -1)
    ) + (weights[2] * shift_rows(east, 1) + weights[3] * shift_rows(west, 1))


def prepare_kernel(levels, deep_ref, surface_ref, out):
    deep = deep_ref[...]
    surface = surface_ref[...]
    ocean = jnp.where(deep > 0.0, 1.0, 0.0)
    pair = jnp.minimum(deep, east_of(deep))
    north_east = jnp.minimum(pair, shift_rows(pair, -1)) / levels
    north_west = west_of(north_east)
    corners = (north_east, north_west, shift_rows(north_east, 1), shift_rows(north_west, 1))
    share = 1.0 / (PHI + 0.5 * ((corners[0] + corners[1]) + (corners[2] + corners[3])))
    weights = [(0.5 * share) * corner for corner in corners]
    for k in range(4):
        out[k] = weights[k]
    out[4] = (PHI * ocean * share) * surface - (surface - weighed(weights, surface))
    across = ocean * east_of(ocean)
    along = ocean * shift_rows(ocean, -1)
    scale = (-0.5 * DIVERGE) * share
    out[5] = scale * across
    out[6] = scale * west_of(across)
    out[7] = scale * along
    out[8] = scale * shift_rows(along, 1)
    out[9] = surface


def solve_kernel(rows, ready, met_a, own_a, own_b, met_b, out):
    odd = jnp.broadcast_to(parities()[0], ready.shape[1:]) == 1
    flows = []
    for f in range(2):
        lines = [ref[f] for ref in (met_a, own_a, own_b, met_b)]
        flows.append(
            jnp.where(odd, jnp.concatenate(lines, axis=0), jnp.concatenate(lines[::-1], axis=0))
        )
    weights = [ready[k] for k in range(4)]
    east, north = flows
    scaled = ready[4] + (
        (ready[5] * (east_of(east) - east) + ready[6] * (east - west_of(east)))
        + (
            ready[7] * (shift_rows(north, -1) - north)
            + ready[8] * (north - shift_rows(north, 1))
        )
    )
    opening, updates = chebyshev_weights(ITERS)
    direction = opening * scaled
    total = ready[9]
    for index in range(ITERS):
        total = total + direction
        if index + 1 < ITERS:
            scaled = scaled - (direction - weighed(weights, direction))
            keep, push = updates[index]
            direction = keep * direction + push * scaled
    out[...] = total[RIM : RIM + rows, : out.shape[1]]


def body(
    eastward_flow,
    northward_flow,
    heat_anomaly,
    salt_anomaly,
    air_stress_forcing,
    earlier_sea_height_load,
    ocean_layer_depths,
):
    levels, rows, columns = eastward_flow.shape
    assert rows == 2 * RIM and columns == 2 * LANES and levels + EXTRA == SUB * sum(CHUNKS)
    along_y, along_x = lax.axis_size("by"), lax.axis_size("bx")
    pairs_y = (swaps(along_y, 0, False), swaps(along_y, 1, False))
    pairs_x = (swaps(along_x, 0, True), swaps(along_x, 1, True))
    row_index = lax.axis_index("by") * rows - RIM + jnp.arange(rows + 2 * RIM)
    rotate = 1.2 * jnp.sin(
        0.9 * math.pi * ((row_index.astype(F32) + 0.5) / (rows * along_y) - 0.5)
    )
    rotate = jnp.broadcast_to(rotate[:, None], (rows + 2 * RIM, columns + LANES))

    fields = (eastward_flow, northward_flow, heat_anomaly, salt_anomaly)
    lines = jnp.concatenate(
        [
            jnp.stack([ocean_layer_depths.astype(F32), earlier_sea_height_load]),
            air_stress_forcing,
        ]
    )
    halves, edge_a, edge_b = pack(fields, lines)
    across_a = lax.ppermute(edge_a, "bx", pairs_x[0])
    across_b = lax.ppermute(edge_b, "bx", pairs_x[1])
    halves = put_rims(halves, across_a, across_b)

    def send(own):
        return [lax.ppermute(item, "by", pairs) for item, pairs in zip(own, pairs_y)]

    rims = [send(halves[chunk]) for chunk in range(AHEAD)]
    kept, news = None, None
    for chunk in range(len(CHUNKS)):
        own_a, own_b = halves[chunk]
        met_a, met_b = rims[chunk]
        blocks = (met_a, own_a, own_b, met_b)
        outs = step(chunk, rows, levels, columns, rotate, blocks, kept, news)
        news, rest = outs[:FIELDS], outs[FIELDS:]
        if chunk == 0:
            deeps, depth_wide, surface_wide = rest[:3]
            rest = rest[3:]
        later = chunk + AHEAD
        if later < len(CHUNKS):
            *halves[later], one, two = lax.optimization_barrier((*halves[later], *rest))
            rest = (one, two)
            rims.append(send(halves[later]))
        kept = (deeps, *rest)
    own_a, own_b = rest
    depth_wide, surface_wide, own_a, own_b = lax.optimization_barrier(
        (depth_wide, surface_wide, own_a, own_b)
    )
    met_a, met_b = send((own_a, own_b))
    vmem = pl.BlockSpec(memory_space=pltpu.VMEM)
    ready = pl.pallas_call(
        functools.partial(prepare_kernel, levels),
        out_shape=jax.ShapeDtypeStruct((10, *depth_wide.shape), F32),
        in_specs=[vmem] * 2,
        out_specs=vmem,
        compiler_params=pltpu.CompilerParams(vmem_limit_bytes=SMALL_VMEM),
        name="prepare",
    )(depth_wide, surface_wide)
    surface_new = pl.pallas_call(
        functools.partial(solve_kernel, rows),
        out_shape=jax.ShapeDtypeStruct((rows, columns), F32),
        in_specs=[vmem] * 5,
        out_specs=vmem,
        compiler_params=pltpu.CompilerParams(vmem_limit_bytes=SMALL_VMEM),
        name="solve",
    )(ready, met_a, own_a, own_b, met_b)
    shaped = [item.reshape(levels, rows, columns) for item in news]
    return (*shaped, surface_new)


def solution(mesh):
    return jax.shard_map(
        body,
        mesh=mesh,
        in_specs=(P(None, "by", "bx"),) * 5 + (P("by", "bx"),) * 2,
        out_specs=(P(None, "by", "bx"),) * 4 + (P("by", "bx"),),
        check_vma=False,
    )
```

time: 78.7 us -> 52.3 us (0.66)
  the two profiles are of different devices: /device:TPU:0 before, /device:TPU:12 now
where the time goes in v1:
time: 52.3 us; the launch traced here: 51.9 us
  Pallas kernels  22.4 us (43%)
  starting transfers between devices  19.5 us (37%)
  waiting for transfers between devices  7.7 us (15%)
  other arithmetic  1.45 us (3%)
  between operations  0.83 us (2%)
    pallas_call x4, Pallas kernels, step(): pl.pallas_call(functools.partial(step_kernel, chunk, rows), out_shape=sha...  18.7 us
    ppermute x10, starting transfers between devices, send(): lax.ppermute(item, 'by', pairs)  17.8 us
    ppermute x10, waiting for transfers between devices, send(): lax.ppermute(item, 'by', pairs)  4.22 us
    ppermute x1, waiting for transfers between devices, body(): across_b = lax.ppermute(edge_b, 'bx', pairs_x[1])  3.47 us
    pallas_call x1, Pallas kernels, pack(): pl.pallas_call(functools.partial(pack_kernel, rows), out_shape=shapes, in...  2.27 us
    ppermute x1, starting transfers between devices, body(): across_b = lax.ppermute(edge_b, 'bx', pairs_x[1])  1.54 us
  transfers between devices with their start and end apart: 12, of which 4 were waited for; matrix products, arithmetic and copies ran while one was open for 0% of the time, Pallas kernels for 27%

profile of v1, /device:TPU:12, one launch (start us, length us, event | category | flops | bytes accessed | tf_op | source)
XLA Modules:
  0.0 51.9 jit_solution(10643726817365647913)
XLA Ops:
  0.6 0.7 %convert_bitcast_fusion = f32[1,8,256]{2,1,0:T(8,128)S(1)} fusion(s32[8,256]{1,0:T(8,128)} %param.13), kind=kLoop, calls=%fused_computation.1 | loop fusion | flops 2048 | bytes 16384 | tf_op jit(solution)/shard_map/stack | solution.py:620
  1.4 0.7 %pad_maximum_fusion.refs_4_ = f32[4,8,256]{2,1,0:T(8,128)S(1)} fusion(f32[2,8,256]{2,1,0:T(8,128)S(1)} %copy-done, f32[1,8,256]{2,1,0:T(8,128)} %bitcast.19, f32[1,8,256]{2,1,0:T(8,128)S(1)} %convert_bitcast_fusion), kind=kLoop, calls=%fused_computation | loop fusion | flops 16384 | bytes 65536 | tf_op jit(solution)/shard_map/concatenate | solution.py:618
  2.0 2.3 %pack.1 = (f32[17,2,8,256]{3,2,1,0:T(8,128)S(1)}, f32[17,2,8,256]{3,2,1,0:T(8,128)S(1)}, f32[17,2,8,256]{3,2,1,0:T(8,128)S(1)}, f32[17,2,8,256]{3,2,1,0:T(8,128)...) custom-call(f32[496,256]{1,0:T(8,128)} %bitcast.15, ...), custom_call_target="tpu_custom_call" | custom-call | tf_op jit(solution)/shard_map/pack/pallas_call | solution.py:152
  4.3 0.1 collective-permute-start
  4.4 1.5 %collective-permute-start.1 = (f32[2,8,8,128]{3,2,1,0:T(8,128)S(1)}, f32[2,8,8,128]{3,2,1,0:T(8,128)S(1)}, u32[]{:S(2)}, u32[]{:S(2)}) collective-permute-start(f32[2,8,8,128]{3,2,1,0:T(8,128)S(1)} %get-tuple-element.59), channel_id=1, source_target_pairs={{1,2},{2,1},{3,4},{4,3},{5,6},{6,5},{7,0},{0,7},{9,10},{10,9},{11,... | collective-permute-start | bytes 196616 | tf_op jit(solution)/shard_map/ppermute | solution.py:626
  6.0 3.5 %collective-permute-done.1.across_b = f32[2,8,8,128]{3,2,1,0:T(8,128)S(1)} collective-permute-done((f32[2,8,8,128]{3,2,1,0:T(8,128)S(1)}, f32[2,8,8,128]{3,2,1,0:T(8,128)S(1)}, u32[]{:S(2)}, u32[]{:S(2)}) %collective-permute-start.1) | collective-permute-done | bytes 65568 | tf_op jit(solution)/shard_map/ppermute | solution.py:626
  9.4 0.3 rims.1
  9.7 0.2 collective-permute-start.2
  9.9 5.0 %collective-permute-start.3 = (f32[17,2,8,256]{3,2,1,0:T(8,128)S(1)}, f32[17,2,8,256]{3,2,1,0:T(8,128)S(1)}, u32[]{:S(2)}, u32[]{:S(2)}) collective-permute-start(f32[17,2,8,256]{3,2,1,0:T(8,128)S(1)} %get-tuple-element.71.refs_3_), channel_id=1, source_target_pairs={{8,16},{16,8},{9,17},{17,9},{10,18},{18,10},{11,19},{19,11},{12,20... | collective-permute-start | bytes 835592 | tf_op jit(solution)/shard_map/ppermute | solution.py:630
  15.0 1.9 %collective-permute-start.9 = (f32[17,2,8,256]{3,2,1,0:T(8,128)S(1)}, f32[17,2,8,256]{3,2,1,0:T(8,128)S(1)}, u32[]{:S(2)}, u32[]{:S(2)}) collective-permute-start(f32[17,2,8,256]{3,2,1,0:T(8,128)S(1)} %get-tuple-element.80.refs_3_), channel_id=1, source_target_pairs={{8,16},{16,8},{9,17},{17,9},{10,18},{18,10},{11,19},{19,11},{12,20... | collective-permute-start | bytes 835592 | tf_op jit(solution)/shard_map/ppermute | solution.py:630
  16.9 0.8 %collective-permute-start.6 = (f32[17,2,8,256]{3,2,1,0:T(8,128)S(1)}, f32[17,2,8,256]{3,2,1,0:T(8,128)S(1)}, u32[]{:S(2)}, u32[]{:S(2)}) collective-permute-start(f32[17,2,8,256]{3,2,1,0:T(8,128)S(1)} %get-tuple-element.77.refs_2_), channel_id=1, source_target_pairs={{0,8},{8,0},{16,24},{24,16},{1,9},{9,1},{17,25},{25,17},{2,10},{10... | collective-permute-start | bytes 835592 | tf_op jit(solution)/shard_map/ppermute | solution.py:630
  17.7 1.5 %collective-permute-done.2.refs_1_ = f32[17,2,8,256]{3,2,1,0:T(8,128)S(1)} collective-permute-done((f32[17,2,8,256]{3,2,1,0:T(8,128)S(1)}, f32[17,2,8,256]{3,2,1,0:T(8,128)S(1)}, u32[]{:S(2)}, u32[]{:S(2)}) %collective-permute-start.2) | collective-permute-done | bytes 278560 | tf_op jit(solution)/shard_map/ppermute | solution.py:630
  19.2 3.7 %collective-permute-start.7 = (f32[17,2,8,256]{3,2,1,0:T(8,128)S(1)}, f32[17,2,8,256]{3,2,1,0:T(8,128)S(1)}, u32[]{:S(2)}, u32[]{:S(2)}) collective-permute-start(f32[17,2,8,256]{3,2,1,0:T(8,128)S(1)} %get-tuple-element.78.refs_3_), channel_id=1, source_target_pairs={{8,16},{16,8},{9,17},{17,9},{10,18},{18,10},{11,19},{19,11},{12,20... | collective-permute-start | bytes 835592 | tf_op jit(solution)/shard_map/ppermute | solution.py:630
  22.9 4.8 %step.4 = (f32[496,256]{1,0:T(8,128)}, f32[496,256]{1,0:T(8,128)}, f32[496,256]{1,0:T(8,128)}, f32[496,256]{1,0:T(8,128)}, f32[4,16,8,384]{3,2,1,0:T(8,128)S(1)}...) custom-call(f32[16,384]{1,0:T(8,128)S(1)} %broadcast_in_dim.2.refs_0_, ...), custom_call_target="tpu_custom_call" | custom-call | tf_op jit(solution)/shard_map/step/pallas_call | solution.py:522
  27.9 3.5 %collective-permute-start.5 = (f32[17,2,8,256]{3,2,1,0:T(8,128)S(1)}, f32[17,2,8,256]{3,2,1,0:T(8,128)S(1)}, u32[]{:S(2)}, u32[]{:S(2)}) collective-permute-start(f32[17,2,8,256]{3,2,1,0:T(8,128)S(1)} %get-tuple-element.75.refs_3_), channel_id=1, source_target_pairs={{8,16},{16,8},{9,17},{17,9},{10,18},{18,10},{11,19},{19,11},{12,20... | collective-permute-start | bytes 835592 | tf_op jit(solution)/shard_map/ppermute | solution.py:630
  31.3 4.6 %step.5 = (f32[496,256]{1,0:T(8,128)}, f32[496,256]{1,0:T(8,128)}, f32[496,256]{1,0:T(8,128)}, f32[496,256]{1,0:T(8,128)}, f32[24,8,384]{2,1,0:T(8,128)S(1)}, /*index=5*/f32[2,8,8,384]{3,2,1,0:T(8,128)S(1)}) custom-call(f32[16,384]{1,0:T(8,128)S(1)} %broadcast_in_dim.2.refs_0_, ...), custom_call_target="tpu_custom_call", output_to_operand_aliasing={{0}: (8, {}), {1}: (9, {}), {2}: (10, {}), {3}: (11, {})} | custom-call | tf_op jit(solution)/shard_map/step/pallas_call | solution.py:522
  36.0 4.6 %step.6 = (f32[496,256]{1,0:T(8,128)}, f32[496,256]{1,0:T(8,128)}, f32[496,256]{1,0:T(8,128)}, f32[496,256]{1,0:T(8,128)}, f32[24,8,384]{2,1,0:T(8,128)S(1)}, /*index=5*/f32[2,8,8,384]{3,2,1,0:T(8,128)S(1)}) custom-call(f32[16,384]{1,0:T(8,128)S(1)} %broadcast_in_dim.2.refs_0_, ...), custom_call_target="tpu_custom_call", output_to_operand_aliasing={{0}: (8, {}), {1}: (9, {}), {2}: (10, {}), {3}: (11, {})} | custom-call | tf_op jit(solution)/shard_map/step/pallas_call | solution.py:522
  40.6 4.6 %step.7 = (f32[496,256]{1,0:T(8,128)}, f32[496,256]{1,0:T(8,128)}, f32[496,256]{1,0:T(8,128)}, f32[496,256]{1,0:T(8,128)}, f32[2,4,384]{2,1,0:T(4,128)S(1)}, /*index=5*/f32[2,4,384]{2,1,0:T(4,128)S(1)}) custom-call(f32[16,384]{1,0:T(8,128)S(1)} %broadcast_in_dim.2.refs_0_, ...), custom_call_target="tpu_custom_call", output_to_operand_aliasing={{0}: (8, {}), {1}: (9, {}), {2}: (10, {}), {3}: (11, {})} | custom-call | tf_op jit(solution)/shard_map/step/pallas_call | solution.py:522
  45.2 0.1 collective-permute-start.10
  45.3 2.6 %collective-permute-start.11 = (f32[2,4,384]{2,1,0:T(4,128)S(1)}, f32[2,4,384]{2,1,0:T(4,128)S(1)}, u32[]{:S(2)}, u32[]{:S(2)}) collective-permute-start(f32[2,4,384]{2,1,0:T(4,128)S(1)} %get-tuple-element.110.own_b), channel_id=1, source_target_pairs={{8,16},{16,8},{9,17},{17,9},{10,18},{18,10},{11,19},{19,11},{12,20... | collective-permute-start | bytes 36872 | tf_op jit(solution)/shard_map/ppermute | solution.py:630
  48.0 0.2 prepare.1.ready
  48.2 0.8 %collective-permute-done.10.met_a = f32[2,4,384]{2,1,0:T(4,128)S(1)} collective-permute-done((f32[2,4,384]{2,1,0:T(4,128)S(1)}, f32[2,4,384]{2,1,0:T(4,128)S(1)}, u32[]{:S(2)}, u32[]{:S(2)}) %collective-permute-start.10) | collective-permute-done | bytes 12320 | tf_op jit(solution)/shard_map/ppermute | solution.py:630
  49.0 1.9 %collective-permute-done.11.met_b = f32[2,4,384]{2,1,0:T(4,128)S(1)} collective-permute-done((f32[2,4,384]{2,1,0:T(4,128)S(1)}, f32[2,4,384]{2,1,0:T(4,128)S(1)}, u32[]{:S(2)}, u32[]{:S(2)}) %collective-permute-start.11) | collective-permute-done | bytes 12320 | tf_op jit(solution)/shard_map/ppermute | solution.py:630
  50.9 1.0 %solve.1 = f32[8,256]{1,0:T(8,128)} custom-call(f32[10,16,384]{2,1,0:T(8,128)S(1)} %prepare.1.ready, f32[2,4,384]{2,1,0:T(4,128)S(1)} %collective-permute-done.10.met_a, f32[2,4,384]{2,1,0:T(4,128)S(1)} %get-tuple-element.109.own_a, f32[2,4,384]{2,1,0:T(4,128)S(1)} %get-tuple-element.110.own_b, f32[2,4,384]{2,1,0:T(4,128)S(1)} %collective-permute-done.11.met_b), custom_call_target="tpu_custom_call" | custom-call | tf_op jit(solution)/shard_map/solve/pallas_call | solution.py:663
  (14 shorter events, 0.3 us)
Async XLA Ops:
  0.6 0.7 %copy-start = (f32[2,8,256]{2,1,0:T(8,128)S(1)}, f32[2,8,256]{2,1,0:T(8,128)}, u32[]{:S(2)}) copy-start(f32[2,8,256]{2,1,0:T(8,128)} %param.11) | copy-start | bytes 49156
  4.3 1.6 %collective-permute-start = (f32[2,8,8,128]{3,2,1,0:T(8,128)S(1)}, f32[2,8,8,128]{3,2,1,0:T(8,128)S(1)}, u32[]{:S(2)}, u32[]{:S(2)}) collective-permute-start(f32[2,8,8,128]{3,2,1,0:T(8,128)S(1)} %get-tuple-element.58), channel_id=1, source_target_pairs={{0,1},{1,0},{2,3},{3,2},{4,5},{5,4},{6,7},{7,6},{8,9},{9,8},{10,11... | collective-permute-start | bytes 196616 | tf_op jit(solution)/shard_map/ppermute | solution.py:625
  4.4 5.0 %collective-permute-start.1 = (f32[2,8,8,128]{3,2,1,0:T(8,128)S(1)}, f32[2,8,8,128]{3,2,1,0:T(8,128)S(1)}, u32[]{:S(2)}, u32[]{:S(2)}) collective-permute-start(f32[2,8,8,128]{3,2,1,0:T(8,128)S(1)} %get-tuple-element.59), channel_id=1, source_target_pairs={{1,2},{2,1},{3,4},{4,3},{5,6},{6,5},{7,0},{0,7},{9,10},{10,9},{11,... | collective-permute-start | bytes 196616 | tf_op jit(solution)/shard_map/ppermute | solution.py:626
  9.7 9.5 %collective-permute-start.2 = (f32[17,2,8,256]{3,2,1,0:T(8,128)S(1)}, f32[17,2,8,256]{3,2,1,0:T(8,128)S(1)}, u32[]{:S(2)}, u32[]{:S(2)}) collective-permute-start(f32[17,2,8,256]{3,2,1,0:T(8,128)S(1)} %get-tuple-element.70.refs_2_), channel_id=1, source_target_pairs={{0,8},{8,0},{16,24},{24,16},{1,9},{9,1},{17,25},{25,17},{2,10},{10... | collective-permute-start | bytes 835592 | tf_op jit(solution)/shard_map/ppermute | solution.py:630
  9.9 13.0 %collective-permute-start.3 = (f32[17,2,8,256]{3,2,1,0:T(8,128)S(1)}, f32[17,2,8,256]{3,2,1,0:T(8,128)S(1)}, u32[]{:S(2)}, u32[]{:S(2)}) collective-permute-start(f32[17,2,8,256]{3,2,1,0:T(8,128)S(1)} %get-tuple-element.71.refs_3_), channel_id=1, source_target_pairs={{8,16},{16,8},{9,17},{17,9},{10,18},{18,10},{11,19},{19,11},{12,20... | collective-permute-start | bytes 835592 | tf_op jit(solution)/shard_map/ppermute | solution.py:630
  14.8 13.0 %collective-permute-start.8 = (f32[17,2,8,256]{3,2,1,0:T(8,128)S(1)}, f32[17,2,8,256]{3,2,1,0:T(8,128)S(1)}, u32[]{:S(2)}, u32[]{:S(2)}) collective-permute-start(f32[17,2,8,256]{3,2,1,0:T(8,128)S(1)} %get-tuple-element.79.refs_2_), channel_id=1, source_target_pairs={{0,8},{8,0},{16,24},{24,16},{1,9},{9,1},{17,25},{25,17},{2,10},{10... | collective-permute-start | bytes 835592 | tf_op jit(solution)/shard_map/ppermute | solution.py:630
  15.0 16.4 %collective-permute-start.9 = (f32[17,2,8,256]{3,2,1,0:T(8,128)S(1)}, f32[17,2,8,256]{3,2,1,0:T(8,128)S(1)}, u32[]{:S(2)}, u32[]{:S(2)}) collective-permute-start(f32[17,2,8,256]{3,2,1,0:T(8,128)S(1)} %get-tuple-element.80.refs_3_), channel_id=1, source_target_pairs={{8,16},{16,8},{9,17},{17,9},{10,18},{18,10},{11,19},{19,11},{12,20... | collective-permute-start | bytes 835592 | tf_op jit(solution)/shard_map/ppermute | solution.py:630
  16.9 19.1 %collective-permute-start.6 = (f32[17,2,8,256]{3,2,1,0:T(8,128)S(1)}, f32[17,2,8,256]{3,2,1,0:T(8,128)S(1)}, u32[]{:S(2)}, u32[]{:S(2)}) collective-permute-start(f32[17,2,8,256]{3,2,1,0:T(8,128)S(1)} %get-tuple-element.77.refs_2_), channel_id=1, source_target_pairs={{0,8},{8,0},{16,24},{24,16},{1,9},{9,1},{17,25},{25,17},{2,10},{10... | collective-permute-start | bytes 835592 | tf_op jit(solution)/shard_map/ppermute | solution.py:630
  19.2 16.8 %collective-permute-start.7 = (f32[17,2,8,256]{3,2,1,0:T(8,128)S(1)}, f32[17,2,8,256]{3,2,1,0:T(8,128)S(1)}, u32[]{:S(2)}, u32[]{:S(2)}) collective-permute-start(f32[17,2,8,256]{3,2,1,0:T(8,128)S(1)} %get-tuple-element.78.refs_3_), channel_id=1, source_target_pairs={{8,16},{16,8},{9,17},{17,9},{10,18},{18,10},{11,19},{19,11},{12,20... | collective-permute-start | bytes 835592 | tf_op jit(solution)/shard_map/ppermute | solution.py:630
  27.8 12.8 %collective-permute-start.4 = (f32[17,2,8,256]{3,2,1,0:T(8,128)S(1)}, f32[17,2,8,256]{3,2,1,0:T(8,128)S(1)}, u32[]{:S(2)}, u32[]{:S(2)}) collective-permute-start(f32[17,2,8,256]{3,2,1,0:T(8,128)S(1)} %get-tuple-element.74.refs_2_), channel_id=1, source_target_pairs={{0,8},{8,0},{16,24},{24,16},{1,9},{9,1},{17,25},{25,17},{2,10},{10... | collective-permute-start | bytes 835592 | tf_op jit(solution)/shard_map/ppermute | solution.py:630
  27.9 12.8 %collective-permute-start.5 = (f32[17,2,8,256]{3,2,1,0:T(8,128)S(1)}, f32[17,2,8,256]{3,2,1,0:T(8,128)S(1)}, u32[]{:S(2)}, u32[]{:S(2)}) collective-permute-start(f32[17,2,8,256]{3,2,1,0:T(8,128)S(1)} %get-tuple-element.75.refs_3_), channel_id=1, source_target_pairs={{8,16},{16,8},{9,17},{17,9},{10,18},{18,10},{11,19},{19,11},{12,20... | collective-permute-start | bytes 835592 | tf_op jit(solution)/shard_map/ppermute | solution.py:630
  45.2 3.8 %collective-permute-start.10 = (f32[2,4,384]{2,1,0:T(4,128)S(1)}, f32[2,4,384]{2,1,0:T(4,128)S(1)}, u32[]{:S(2)}, u32[]{:S(2)}) collective-permute-start(f32[2,4,384]{2,1,0:T(4,128)S(1)} %get-tuple-element.109.own_a), channel_id=1, source_target_pairs={{0,8},{8,0},{16,24},{24,16},{1,9},{9,1},{17,25},{25,17},{2,10},{10... | collective-permute-start | bytes 36872 | tf_op jit(solution)/shard_map/ppermute | solution.py:630
  45.3 5.6 %collective-permute-start.11 = (f32[2,4,384]{2,1,0:T(4,128)S(1)}, f32[2,4,384]{2,1,0:T(4,128)S(1)}, u32[]{:S(2)}, u32[]{:S(2)}) collective-permute-start(f32[2,4,384]{2,1,0:T(4,128)S(1)} %get-tuple-element.110.own_b), channel_id=1, source_target_pairs={{8,16},{16,8},{9,17},{17,9},{10,18},{18,10},{11,19},{19,11},{12,20... | collective-permute-start | bytes 36872 | tf_op jit(solution)/shard_map/ppermute | solution.py:630

commit v2 on v1

--- a/solution.py
+++ b/solution.py
@@ -28,9 +28,9 @@
 AHEAD = 3
 FAR = 1000000
 BATCH = 4
-GROUPS = ((0, 1), (2, 3))
+GROUPS = ((0,), (1,), (2,), (3,))
 SMALL_VMEM = 4 * 1024 * 1024
-PACK_VMEM = 103 * 512 * 1024
+PACK_VMEM = 8 * 1024 * 1024
 F32 = jnp.float32
 
 
@@ -87,8 +87,14 @@
 
 def pack_kernel(rows, *refs):
     fields = refs[:FIELDS]
-    flat = refs[FIELDS]
-    *halves, across_a, across_b, held, sems = refs[FIELDS + 1 :]
+    sources = refs[FIELDS : FIELDS + 3]
+    *halves, across_a, across_b, held, sems, flat, depth, sems_flat = refs[FIELDS + 3 :]
+    small = [
+        pltpu.make_async_copy(source, into, sems_flat.at[k])
+        for k, (source, into) in enumerate(
+            zip(sources, (flat.at[pl.ds(EXTRA, EXTRA)], flat.at[1], depth))
+        )
+    ]
 
     def copy(f, lane):
         return pltpu.make_async_copy(
@@ -98,6 +104,11 @@
     for f in range(FIELDS):
         for lane in range(2):
             copy(f, lane).start()
+    for item in small:
+        item.start()
+    for item in small:
+        item.wait()
+    flat[0] = depth[...].astype(F32)
 
     def line(f, extra, row):
         if f < 2:
@@ -152,16 +163,18 @@
     *halves, across_a, across_b = pl.pallas_call(
         functools.partial(pack_kernel, rows),
         out_shape=shapes,
-        in_specs=[pl.BlockSpec(memory_space=pltpu.HBM)] * FIELDS
-        + [pl.BlockSpec(memory_space=pltpu.VMEM)],
+        in_specs=[pl.BlockSpec(memory_space=pltpu.HBM)] * (FIELDS + 3),
         out_specs=[pl.BlockSpec(memory_space=pltpu.VMEM)] * len(shapes),
         scratch_shapes=[
             pltpu.VMEM((FIELDS, 2, levels * rows, LANES), F32),
             pltpu.SemaphoreType.DMA((FIELDS, 2)),
+            pltpu.VMEM((2 * EXTRA, rows, columns), F32),
+            pltpu.VMEM((rows, columns), jnp.int32),
+            pltpu.SemaphoreType.DMA((3,)),
         ],
         compiler_params=pltpu.CompilerParams(vmem_limit_bytes=PACK_VMEM),
         name="pack",
-    )(*flat, lines)
+    )(*[pltpu.with_memory_space_constraint(item, pltpu.HBM) for item in (*flat, *lines)])
     return halves, across_a, across_b
 
 
@@ -335,12 +348,14 @@
                 press_x[a] = across[k]
                 press_y[a] = slopes[k + 1] + slopes[k]
 
-    def tendency(get, lowest, highest, carry_at, emit):
+    def tendency(get, lowest, highest, carry_at, emit, finish=None):
         pressure(get, lowest, highest, carry_at)
         for group in GROUPS:
             first_pass(get, lowest, highest, group)
         for group in GROUPS:
             second_pass(lowest, highest, group, emit)
+            if finish is not None:
+                finish(group)
 
     def turned(get, group, a):
         values = [get(f, a) for f in group]
@@ -364,13 +379,16 @@
             left = [side_w * (x - y) for x, y in zip(here, west)]
             lap = [(right[i] - left[i]) + (up[i] - up_before[i]) for i in span]
             if lowest <= a <= highest:
-                flows = here if group[0] == 0 else [get(0, a), get(1, a)]
+                flows = [here[group.index(f)] if f in group else get(f, a) for f in range(2)]
                 u, v = (-0.5 * ADVECT) * flows[0], (-0.5 * ADVECT) * flows[1]
                 mixed = [u * (right[i] + left[i]) + v * (up[i] + up_before[i]) for i in span]
-                if group[0] == 0:
-                    turn = rotate[pl.ds(a, 1), :] * wets[a]
-                    mixed[0] = mixed[0] + (turn * here[1] - press_x[a])
-                    mixed[1] = mixed[1] - (turn * here[0] + press_y[a])
+                for i, f in enumerate(group):
+                    if f < 2:
+                        turn = rotate[pl.ds(a, 1), :] * wets[a]
+                    if f == 0:
+                        mixed[i] = mixed[i] + (turn * flows[1] - press_x[a])
+                    if f == 1:
+                        mixed[i] = mixed[i] - (turn * flows[0] + press_y[a])
                 for i, f in enumerate(group):
                     mixes[f, a] = mixed[i]
             for i, f in enumerate(group):
@@ -422,10 +440,12 @@
                 ref[a] = jnp.where(level < deeps[k, a], 1.0, 0.0)
 
         def winded(a, group, values):
-            if not first or group[0] != 0:
+            if not first:
                 return values
-            windy = top * wets[a]
-            return [values[f] + windy * winds[f, a] for f in range(2)] + values[2:]
+            return [
+                value + (top * wets[a]) * winds[f, a] if f < 2 else value
+                for f, value in zip(group, values)
+            ]
 
         def emit_first(a, group, values):
             values = winded(a, group, values)
@@ -439,24 +459,28 @@
             values = winded(a, group, values)
             news = [0.5 * ((cur[f, a] + between[f, a]) + value) for f, value in zip(group, values)]
             r = a - RIM
-            if group[0] == 0:
-                adds = [sums[f, r] + wets[a] * news[f] for f in range(2)]
-                for f in range(2):
-                    sums[f, r] = adds[f]
+            adds = [sums[f, r] + wets[a] * new for f, new in zip(group, news) if f < 2]
+            for f, add in zip(group, adds):
+                sums[f, r] = add
             for f, new in zip(group, news):
                 for lane in range(2):
                     held[f, lane, pl.ds(t * (SUB * rows) + r, SUB, stride=rows), :] = new[
                         :, lane * LANES : (lane + 1) * LANES
                     ]
 
-        tendency(lambda f, a: between[f, a], RIM, tall - RIM - 1, tall - 2, emit_second)
-
-        @pl.when(t < tiles - 1)
-        def _():
-            for f in every:
-                for lane in range(2):
-                    copy(f, lane, t, SUB).start()
-
+        def finish(group):
+            def leave(count):
+                for f in group:
+                    for lane in range(2):
+                        copy(f, lane, t, count).start()
+
+            if final == SUB:
+                leave(SUB)
+            else:
+                pl.when(t < tiles - 1)(lambda: leave(SUB))
+                pl.when(t == tiles - 1)(lambda: leave(final))
+
+        tendency(lambda f, a: between[f, a], RIM, tall - RIM - 1, tall - 2, emit_second, finish)
         return 0
 
     def copy(f, lane, t, count):
@@ -468,11 +492,8 @@
             sems.at[t, f, lane],
         )
 
+    final = levels - SUB * (tiles - 1)
     lax.fori_loop(0, tiles, tile, 0)
-    final = levels - SUB * (tiles - 1)
-    for f in every:
-        for lane in range(2):
-            copy(f, lane, tiles - 1, final).start()
     if last:
         depth_levels = first_level(chunk) + levels
         for f in range(2):
@@ -615,19 +636,15 @@
     rotate = jnp.broadcast_to(rotate[:, None], (rows + 2 * RIM, columns + LANES))
 
     fields = (eastward_flow, northward_flow, heat_anomaly, salt_anomaly)
-    lines = jnp.concatenate(
-        [
-            jnp.stack([ocean_layer_depths.astype(F32), earlier_sea_height_load]),
-            air_stress_forcing,
-        ]
-    )
+    lines = (air_stress_forcing, earlier_sea_height_load, ocean_layer_depths)
     halves, edge_a, edge_b = pack(fields, lines)
     across_a = lax.ppermute(edge_a, "bx", pairs_x[0])
     across_b = lax.ppermute(edge_b, "bx", pairs_x[1])
     halves = put_rims(halves, across_a, across_b)
 
     def send(own):
-        return [lax.ppermute(item, "by", pairs) for item, pairs in zip(own, pairs_y)]
+        met_b = lax.ppermute(own[1], "by", pairs_y[1])
+        return lax.ppermute(own[0], "by", pairs_y[0]), met_b
 
     rims = [send(halves[chunk]) for chunk in range(AHEAD)]
     kept, news = None, None

time: 52.3 us -> 50.7 us (0.969)
  other arithmetic: 1.45 us -> 0.05 us
    another operation x1 -> x0, other arithmetic: 0.71 us -> none  [body(): jnp.stack([ocean_layer_depths.astype(F32), earlier_sea_height_load])]
    concatenate x1 -> x0, other arithmetic: 0.7 us -> none  [body(): jnp.concatenate([jnp.stack([ocean_layer_depths.astype(F32), earlier_sea_h...]
  transfers between devices with their start and end apart: 12 -> 12, of which waited for: 4 -> 4; matrix products, arithmetic and copies ran while one was open for 0% -> 0% of each run, Pallas kernels for 27% -> 28%
where the time goes in v2:
time: 50.7 us; the launch traced here: 50.4 us
  Pallas kernels  22.3 us (44%)
  starting transfers between devices  19.5 us (38%)
  waiting for transfers between devices  7.7 us (15%)
  between operations  0.83 us (2%)
    pallas_call x4, Pallas kernels, step(): pl.pallas_call(functools.partial(step_kernel, chunk, rows), out_shape=sha...  18.4 us
    ppermute x5, starting transfers between devices, send(): met_b = lax.ppermute(own[1], 'by', pairs_y[1])  16.7 us
    ppermute x1, waiting for transfers between devices, body(): across_b = lax.ppermute(edge_b, 'bx', pairs_x[1])  3.47 us
    pallas_call x1, Pallas kernels, pack(): pl.pallas_call(functools.partial(pack_kernel, rows), out_shape=shapes, in...  2.49 us
    ppermute x5, waiting for transfers between devices, send(): return (lax.ppermute(own[0], 'by', pairs_y[0]), met_b)  2.3 us
    ppermute x5, waiting for transfers between devices, send(): met_b = lax.ppermute(own[1], 'by', pairs_y[1])  1.92 us
    ppermute x1, starting transfers between devices, body(): across_b = lax.ppermute(edge_b, 'bx', pairs_x[1])  1.54 us
    ppermute x5, starting transfers between devices, send(): return (lax.ppermute(own[0], 'by', pairs_y[0]), met_b)  1.2 us
  transfers between devices with their start and end apart: 12, of which 4 were waited for; matrix products, arithmetic and copies ran while one was open for 0% of the time, Pallas kernels for 28%

profile of v2, /device:TPU:12, one launch (start us, length us, event | category | flops | bytes accessed | tf_op | source)
XLA Modules:
  0.0 50.4 jit_solution(5215178596230867703)
XLA Ops:
  0.6 2.5 %pack.1 = (f32[17,2,8,256]{3,2,1,0:T(8,128)S(1)}, f32[17,2,8,256]{3,2,1,0:T(8,128)S(1)}, f32[17,2,8,256]{3,2,1,0:T(8,128)S(1)}, f32[17,2,8,256]{3,2,1,0:T(8,128)...) custom-call(f32[496,256]{1,0:T(8,128)} %bitcast.12, ...), custom_call_target="tpu_custom_call" | custom-call | tf_op jit(solution)/shard_map/pack/pallas_call | solution.py:163
  3.1 0.1 collective-permute-start
  3.2 1.5 %collective-permute-start.1 = (f32[2,8,8,128]{3,2,1,0:T(8,128)S(1)}, f32[2,8,8,128]{3,2,1,0:T(8,128)S(1)}, u32[]{:S(2)}, u32[]{:S(2)}) collective-permute-start(f32[2,8,8,128]{3,2,1,0:T(8,128)S(1)} %get-tuple-element.59), channel_id=1, source_target_pairs={{1,2},{2,1},{3,4},{4,3},{5,6},{6,5},{7,0},{0,7},{9,10},{10,9},{11,... | collective-permute-start | bytes 196616 | tf_op jit(solution)/shard_map/ppermute | solution.py:642
  4.7 3.5 %collective-permute-done.1.across_b = f32[2,8,8,128]{3,2,1,0:T(8,128)S(1)} collective-permute-done((f32[2,8,8,128]{3,2,1,0:T(8,128)S(1)}, f32[2,8,8,128]{3,2,1,0:T(8,128)S(1)}, u32[]{:S(2)}, u32[]{:S(2)}) %collective-permute-start.1) | collective-permute-done | bytes 65568 | tf_op jit(solution)/shard_map/ppermute | solution.py:642
  8.2 0.3 rims.1
  8.5 0.2 collective-permute-start.2
  8.7 5.0 %collective-permute-start.3 = (f32[17,2,8,256]{3,2,1,0:T(8,128)S(1)}, f32[17,2,8,256]{3,2,1,0:T(8,128)S(1)}, u32[]{:S(2)}, u32[]{:S(2)}) collective-permute-start(f32[17,2,8,256]{3,2,1,0:T(8,128)S(1)} %get-tuple-element.71.refs_3_), channel_id=1, source_target_pairs={{8,16},{16,8},{9,17},{17,9},{10,18},{18,10},{11,19},{19,11},{12,20... | collective-permute-start | bytes 835592 | tf_op jit(solution)/shard_map/ppermute | solution.py:646
  13.6 0.1 collective-permute-start.8
  13.8 1.9 %collective-permute-start.9 = (f32[17,2,8,256]{3,2,1,0:T(8,128)S(1)}, f32[17,2,8,256]{3,2,1,0:T(8,128)S(1)}, u32[]{:S(2)}, u32[]{:S(2)}) collective-permute-start(f32[17,2,8,256]{3,2,1,0:T(8,128)S(1)} %get-tuple-element.80.refs_3_), channel_id=1, source_target_pairs={{8,16},{16,8},{9,17},{17,9},{10,18},{18,10},{11,19},{19,11},{12,20... | collective-permute-start | bytes 835592 | tf_op jit(solution)/shard_map/ppermute | solution.py:646
  15.7 0.8 %collective-permute-start.6 = (f32[17,2,8,256]{3,2,1,0:T(8,128)S(1)}, f32[17,2,8,256]{3,2,1,0:T(8,128)S(1)}, u32[]{:S(2)}, u32[]{:S(2)}) collective-permute-start(f32[17,2,8,256]{3,2,1,0:T(8,128)S(1)} %get-tuple-element.77.refs_2_), channel_id=1, source_target_pairs={{0,8},{8,0},{16,24},{24,16},{1,9},{9,1},{17,25},{25,17},{2,10},{10... | collective-permute-start | bytes 835592 | tf_op jit(solution)/shard_map/ppermute | solution.py:647
  16.5 1.5 %collective-permute-done.2.refs_1_ = f32[17,2,8,256]{3,2,1,0:T(8,128)S(1)} collective-permute-done((f32[17,2,8,256]{3,2,1,0:T(8,128)S(1)}, f32[17,2,8,256]{3,2,1,0:T(8,128)S(1)}, u32[]{:S(2)}, u32[]{:S(2)}) %collective-permute-start.2) | collective-permute-done | bytes 278560 | tf_op jit(solution)/shard_map/ppermute | solution.py:647
  18.0 3.7 %collective-permute-start.7 = (f32[17,2,8,256]{3,2,1,0:T(8,128)S(1)}, f32[17,2,8,256]{3,2,1,0:T(8,128)S(1)}, u32[]{:S(2)}, u32[]{:S(2)}) collective-permute-start(f32[17,2,8,256]{3,2,1,0:T(8,128)S(1)} %get-tuple-element.78.refs_3_), channel_id=1, source_target_pairs={{8,16},{16,8},{9,17},{17,9},{10,18},{18,10},{11,19},{19,11},{12,20... | collective-permute-start | bytes 835592 | tf_op jit(solution)/shard_map/ppermute | solution.py:646
  21.7 4.7 %step.4 = (f32[496,256]{1,0:T(8,128)}, f32[496,256]{1,0:T(8,128)}, f32[496,256]{1,0:T(8,128)}, f32[496,256]{1,0:T(8,128)}, f32[4,16,8,384]{3,2,1,0:T(8,128)S(1)}...) custom-call(f32[16,384]{1,0:T(8,128)S(1)} %broadcast_in_dim.2.refs_0_, ...), custom_call_target="tpu_custom_call" | custom-call | tf_op jit(solution)/shard_map/step/pallas_call | solution.py:543
  26.5 0.1 collective-permute-start.4
  26.5 3.5 %collective-permute-start.5 = (f32[17,2,8,256]{3,2,1,0:T(8,128)S(1)}, f32[17,2,8,256]{3,2,1,0:T(8,128)S(1)}, u32[]{:S(2)}, u32[]{:S(2)}) collective-permute-start(f32[17,2,8,256]{3,2,1,0:T(8,128)S(1)} %get-tuple-element.75.refs_3_), channel_id=1, source_target_pairs={{8,16},{16,8},{9,17},{17,9},{10,18},{18,10},{11,19},{19,11},{12,20... | collective-permute-start | bytes 835592 | tf_op jit(solution)/shard_map/ppermute | solution.py:646
  30.0 4.6 %step.5 = (f32[496,256]{1,0:T(8,128)}, f32[496,256]{1,0:T(8,128)}, f32[496,256]{1,0:T(8,128)}, f32[496,256]{1,0:T(8,128)}, f32[24,8,384]{2,1,0:T(8,128)S(1)}, /*index=5*/f32[2,8,8,384]{3,2,1,0:T(8,128)S(1)}) custom-call(f32[16,384]{1,0:T(8,128)S(1)} %broadcast_in_dim.2.refs_0_, ...), custom_call_target="tpu_custom_call", output_to_operand_aliasing={{0}: (8, {}), {1}: (9, {}), {2}: (10, {}), {3}: (11, {})} | custom-call | tf_op jit(solution)/shard_map/step/pallas_call | solution.py:543
  34.6 4.6 %step.6 = (f32[496,256]{1,0:T(8,128)}, f32[496,256]{1,0:T(8,128)}, f32[496,256]{1,0:T(8,128)}, f32[496,256]{1,0:T(8,128)}, f32[24,8,384]{2,1,0:T(8,128)S(1)}, /*index=5*/f32[2,8,8,384]{3,2,1,0:T(8,128)S(1)}) custom-call(f32[16,384]{1,0:T(8,128)S(1)} %broadcast_in_dim.2.refs_0_, ...), custom_call_target="tpu_custom_call", output_to_operand_aliasing={{0}: (8, {}), {1}: (9, {}), {2}: (10, {}), {3}: (11, {})} | custom-call | tf_op jit(solution)/shard_map/step/pallas_call | solution.py:543
  39.2 4.5 %step.7 = (f32[496,256]{1,0:T(8,128)}, f32[496,256]{1,0:T(8,128)}, f32[496,256]{1,0:T(8,128)}, f32[496,256]{1,0:T(8,128)}, f32[2,4,384]{2,1,0:T(4,128)S(1)}, /*index=5*/f32[2,4,384]{2,1,0:T(4,128)S(1)}) custom-call(f32[16,384]{1,0:T(8,128)S(1)} %broadcast_in_dim.2.refs_0_, ...), custom_call_target="tpu_custom_call", output_to_operand_aliasing={{0}: (8, {}), {1}: (9, {}), {2}: (10, {}), {3}: (11, {})} | custom-call | tf_op jit(solution)/shard_map/step/pallas_call | solution.py:543
  43.8 0.1 collective-permute-start.10
  43.8 2.6 %collective-permute-start.11 = (f32[2,4,384]{2,1,0:T(4,128)S(1)}, f32[2,4,384]{2,1,0:T(4,128)S(1)}, u32[]{:S(2)}, u32[]{:S(2)}) collective-permute-start(f32[2,4,384]{2,1,0:T(4,128)S(1)} %get-tuple-element.110.own_b), channel_id=1, source_target_pairs={{8,16},{16,8},{9,17},{17,9},{10,18},{18,10},{11,19},{19,11},{12,20... | collective-permute-start | bytes 36872 | tf_op jit(solution)/shard_map/ppermute | solution.py:646
  46.5 0.2 prepare.1.ready
  46.7 0.8 %collective-permute-done.10.met_a = f32[2,4,384]{2,1,0:T(4,128)S(1)} collective-permute-done((f32[2,4,384]{2,1,0:T(4,128)S(1)}, f32[2,4,384]{2,1,0:T(4,128)S(1)}, u32[]{:S(2)}, u32[]{:S(2)}) %collective-permute-start.10) | collective-permute-done | bytes 12320 | tf_op jit(solution)/shard_map/ppermute | solution.py:647
  47.5 1.9 %collective-permute-done.11.met_b = f32[2,4,384]{2,1,0:T(4,128)S(1)} collective-permute-done((f32[2,4,384]{2,1,0:T(4,128)S(1)}, f32[2,4,384]{2,1,0:T(4,128)S(1)}, u32[]{:S(2)}, u32[]{:S(2)}) %collective-permute-start.11) | collective-permute-done | bytes 12320 | tf_op jit(solution)/shard_map/ppermute | solution.py:646
  49.4 1.0 %solve.1 = f32[8,256]{1,0:T(8,128)} custom-call(f32[10,16,384]{2,1,0:T(8,128)S(1)} %prepare.1.ready, f32[2,4,384]{2,1,0:T(4,128)S(1)} %collective-permute-done.10.met_a, f32[2,4,384]{2,1,0:T(4,128)S(1)} %get-tuple-element.109.own_a, f32[2,4,384]{2,1,0:T(4,128)S(1)} %get-tuple-element.110.own_b, f32[2,4,384]{2,1,0:T(4,128)S(1)} %collective-permute-done.11.met_b), custom_call_target="tpu_custom_call" | custom-call | tf_op jit(solution)/shard_map/solve/pallas_call | solution.py:680
  (10 shorter events, 0.1 us)
Async XLA Ops:
  3.1 1.6 %collective-permute-start = (f32[2,8,8,128]{3,2,1,0:T(8,128)S(1)}, f32[2,8,8,128]{3,2,1,0:T(8,128)S(1)}, u32[]{:S(2)}, u32[]{:S(2)}) collective-permute-start(f32[2,8,8,128]{3,2,1,0:T(8,128)S(1)} %get-tuple-element.58), channel_id=1, source_target_pairs={{0,1},{1,0},{2,3},{3,2},{4,5},{5,4},{6,7},{7,6},{8,9},{9,8},{10,11... | collective-permute-start | bytes 196616 | tf_op jit(solution)/shard_map/ppermute | solution.py:641
  3.2 5.0 %collective-permute-start.1 = (f32[2,8,8,128]{3,2,1,0:T(8,128)S(1)}, f32[2,8,8,128]{3,2,1,0:T(8,128)S(1)}, u32[]{:S(2)}, u32[]{:S(2)}) collective-permute-start(f32[2,8,8,128]{3,2,1,0:T(8,128)S(1)} %get-tuple-element.59), channel_id=1, source_target_pairs={{1,2},{2,1},{3,4},{4,3},{5,6},{6,5},{7,0},{0,7},{9,10},{10,9},{11,... | collective-permute-start | bytes 196616 | tf_op jit(solution)/shard_map/ppermute | solution.py:642
  8.5 9.5 %collective-permute-start.2 = (f32[17,2,8,256]{3,2,1,0:T(8,128)S(1)}, f32[17,2,8,256]{3,2,1,0:T(8,128)S(1)}, u32[]{:S(2)}, u32[]{:S(2)}) collective-permute-start(f32[17,2,8,256]{3,2,1,0:T(8,128)S(1)} %get-tuple-element.70.refs_2_), channel_id=1, source_target_pairs={{0,8},{8,0},{16,24},{24,16},{1,9},{9,1},{17,25},{25,17},{2,10},{10... | collective-permute-start | bytes 835592 | tf_op jit(solution)/shard_map/ppermute | solution.py:647
  8.7 13.0 %collective-permute-start.3 = (f32[17,2,8,256]{3,2,1,0:T(8,128)S(1)}, f32[17,2,8,256]{3,2,1,0:T(8,128)S(1)}, u32[]{:S(2)}, u32[]{:S(2)}) collective-permute-start(f32[17,2,8,256]{3,2,1,0:T(8,128)S(1)} %get-tuple-element.71.refs_3_), channel_id=1, source_target_pairs={{8,16},{16,8},{9,17},{17,9},{10,18},{18,10},{11,19},{19,11},{12,20... | collective-permute-start | bytes 835592 | tf_op jit(solution)/shard_map/ppermute | solution.py:646
  13.6 12.9 %collective-permute-start.8 = (f32[17,2,8,256]{3,2,1,0:T(8,128)S(1)}, f32[17,2,8,256]{3,2,1,0:T(8,128)S(1)}, u32[]{:S(2)}, u32[]{:S(2)}) collective-permute-start(f32[17,2,8,256]{3,2,1,0:T(8,128)S(1)} %get-tuple-element.79.refs_2_), channel_id=1, source_target_pairs={{0,8},{8,0},{16,24},{24,16},{1,9},{9,1},{17,25},{25,17},{2,10},{10... | collective-permute-start | bytes 835592 | tf_op jit(solution)/shard_map/ppermute | solution.py:647
  13.8 16.3 %collective-permute-start.9 = (f32[17,2,8,256]{3,2,1,0:T(8,128)S(1)}, f32[17,2,8,256]{3,2,1,0:T(8,128)S(1)}, u32[]{:S(2)}, u32[]{:S(2)}) collective-permute-start(f32[17,2,8,256]{3,2,1,0:T(8,128)S(1)} %get-tuple-element.80.refs_3_), channel_id=1, source_target_pairs={{8,16},{16,8},{9,17},{17,9},{10,18},{18,10},{11,19},{19,11},{12,20... | collective-permute-start | bytes 835592 | tf_op jit(solution)/shard_map/ppermute | solution.py:646
  15.7 18.9 %collective-permute-start.6 = (f32[17,2,8,256]{3,2,1,0:T(8,128)S(1)}, f32[17,2,8,256]{3,2,1,0:T(8,128)S(1)}, u32[]{:S(2)}, u32[]{:S(2)}) collective-permute-start(f32[17,2,8,256]{3,2,1,0:T(8,128)S(1)} %get-tuple-element.77.refs_2_), channel_id=1, source_target_pairs={{0,8},{8,0},{16,24},{24,16},{1,9},{9,1},{17,25},{25,17},{2,10},{10... | collective-permute-start | bytes 835592 | tf_op jit(solution)/shard_map/ppermute | solution.py:647
  18.0 16.6 %collective-permute-start.7 = (f32[17,2,8,256]{3,2,1,0:T(8,128)S(1)}, f32[17,2,8,256]{3,2,1,0:T(8,128)S(1)}, u32[]{:S(2)}, u32[]{:S(2)}) collective-permute-start(f32[17,2,8,256]{3,2,1,0:T(8,128)S(1)} %get-tuple-element.78.refs_3_), channel_id=1, source_target_pairs={{8,16},{16,8},{9,17},{17,9},{10,18},{18,10},{11,19},{19,11},{12,20... | collective-permute-start | bytes 835592 | tf_op jit(solution)/shard_map/ppermute | solution.py:646
  26.5 12.7 %collective-permute-start.4 = (f32[17,2,8,256]{3,2,1,0:T(8,128)S(1)}, f32[17,2,8,256]{3,2,1,0:T(8,128)S(1)}, u32[]{:S(2)}, u32[]{:S(2)}) collective-permute-start(f32[17,2,8,256]{3,2,1,0:T(8,128)S(1)} %get-tuple-element.74.refs_2_), channel_id=1, source_target_pairs={{0,8},{8,0},{16,24},{24,16},{1,9},{9,1},{17,25},{25,17},{2,10},{10... | collective-permute-start | bytes 835592 | tf_op jit(solution)/shard_map/ppermute | solution.py:647
  26.5 12.7 %collective-permute-start.5 = (f32[17,2,8,256]{3,2,1,0:T(8,128)S(1)}, f32[17,2,8,256]{3,2,1,0:T(8,128)S(1)}, u32[]{:S(2)}, u32[]{:S(2)}) collective-permute-start(f32[17,2,8,256]{3,2,1,0:T(8,128)S(1)} %get-tuple-element.75.refs_3_), channel_id=1, source_target_pairs={{8,16},{16,8},{9,17},{17,9},{10,18},{18,10},{11,19},{19,11},{12,20... | collective-permute-start | bytes 835592 | tf_op jit(solution)/shard_map/ppermute | solution.py:646
  43.8 3.8 %collective-permute-start.10 = (f32[2,4,384]{2,1,0:T(4,128)S(1)}, f32[2,4,384]{2,1,0:T(4,128)S(1)}, u32[]{:S(2)}, u32[]{:S(2)}) collective-permute-start(f32[2,4,384]{2,1,0:T(4,128)S(1)} %get-tuple-element.109.own_a), channel_id=1, source_target_pairs={{0,8},{8,0},{16,24},{24,16},{1,9},{9,1},{17,25},{25,17},{2,10},{10... | collective-permute-start | bytes 36872 | tf_op jit(solution)/shard_map/ppermute | solution.py:647
  43.8 5.6 %collective-permute-start.11 = (f32[2,4,384]{2,1,0:T(4,128)S(1)}, f32[2,4,384]{2,1,0:T(4,128)S(1)}, u32[]{:S(2)}, u32[]{:S(2)}) collective-permute-start(f32[2,4,384]{2,1,0:T(4,128)S(1)} %get-tuple-element.110.own_b), channel_id=1, source_target_pairs={{8,16},{16,8},{9,17},{17,9},{10,18},{18,10},{11,19},{19,11},{12,20... | collective-permute-start | bytes 36872 | tf_op jit(solution)/shard_map/ppermute | solution.py:646

commit v3 on v2

--- a/solution.py
+++ b/solution.py
@@ -64,35 +64,21 @@
 
 
 def parities():
-    return lax.axis_index("by") & 1, lax.axis_index("bx") & 1
+    return 1 - (lax.axis_index("by") & 1), lax.axis_index("bx") & 1
 
 
 def first_rows():
-    odd = lax.axis_index("by") & 1
+    odd = parities()[0]
     return (1 - odd) * RIM, odd * RIM
 
 
-def place_tile(half, held, rows, group, f, chunk, t, line):
-    used = min(SUB, chunk_levels(chunk) - SUB * t)
-    base = (first_level(chunk) + SUB * t) * rows
-    first = first_rows()[group]
-    for q in range(RIM):
-        for lane in range(2):
-            half[f * RIM + q, t, pl.ds(0, used), pl.ds(lane * LANES, LANES)] = held[
-                f, lane, pl.ds(base + first + q, used, stride=rows), :
-            ]
-        for extra in range(SUB - used):
-            half[f * RIM + q, t, pl.ds(used + extra, 1), :] = line(f, extra, first + q)
-
-
-def pack_kernel(rows, *refs):
-    fields = refs[:FIELDS]
-    sources = refs[FIELDS : FIELDS + 3]
-    *halves, across_a, across_b, held, sems, flat, depth, sems_flat = refs[FIELDS + 3 :]
+def edges_kernel(rows, *refs):
+    fields, sources = refs[:FIELDS], refs[FIELDS : FIELDS + 3]
+    across_a, across_b, held, lines, mixed, depth, sems, sems_lines = refs[FIELDS + 3 :]
     small = [
-        pltpu.make_async_copy(source, into, sems_flat.at[k])
+        pltpu.make_async_copy(source, into, sems_lines.at[k])
         for k, (source, into) in enumerate(
-            zip(sources, (flat.at[pl.ds(EXTRA, EXTRA)], flat.at[1], depth))
+            zip(sources, (lines.at[pl.ds(EXTRA, EXTRA)], lines.at[1], depth))
         )
     ]
 
@@ -108,25 +94,23 @@
         item.start()
     for item in small:
         item.wait()
-    flat[0] = depth[...].astype(F32)
-
-    def line(f, extra, row):
-        if f < 2:
-            return flat[EXTRA * f + extra, pl.ds(row, 1), :]
-        return jnp.zeros((1, 2 * LANES), F32)
-
+    lines[0] = depth[...].astype(F32)
     for f in range(FIELDS):
         for lane in range(2):
             copy(f, lane).wait()
-        for c in range(len(CHUNKS)):
-            for t in range(CHUNKS[c]):
-                for group in range(2):
-                    place_tile(halves[2 * c + group], held, rows, group, f, c, t, line)
+
+    used = SUB - EXTRA
+    for f in range(FIELDS):
+        for group in range(2):
+            for q in range(RIM):
+                place_tile(mixed.at[f, group, q], held, lines, rows, group, f, q, 0, CHUNKS[0] - 1)
+
     lanes = lax.broadcasted_iota(jnp.int32, (SUB, LANES), 1)
-    odd = jnp.broadcast_to(lax.axis_index("bx") & 1, (SUB, LANES)) == 1
+    odd = jnp.broadcast_to(parities()[1], (SUB, LANES)) == 1
     slot = 0
     for c in range(len(CHUNKS)):
         for t in range(CHUNKS[c]):
+            base = (first_level(c) + SUB * t) * rows
             for group in range(2):
                 west = jnp.zeros((SUB, LANES), F32)
                 east = jnp.zeros((SUB, LANES), F32)
@@ -134,9 +118,13 @@
                     for f in range(FIELDS):
                         place = (q * FIELDS + f) * EDGE
                         other = (place - EDGE) % LANES
-                        block = halves[2 * c + group][f * RIM + q, t]
-                        low = block[:, :LANES]
-                        high = block[:, LANES:]
+                        if c == 0 and t == CHUNKS[0] - 1:
+                            low = mixed[f, group, q, :, pl.ds(0, LANES)]
+                            high = mixed[f, group, q, :, pl.ds(LANES, LANES)]
+                        else:
+                            row = pl.ds(base + first_rows()[group] + q, SUB, stride=rows)
+                            low = held[f, 0, row, :]
+                            high = held[f, 1, row, :]
                         if place:
                             low = pltpu.roll(low, place, 1)
                             high = pltpu.roll(high, place, 1)
@@ -147,35 +135,75 @@
             slot += 1
 
 
-def half_shapes(columns):
-    return [
-        jax.ShapeDtypeStruct((FIELDS * RIM + 1, tiles, SUB, columns), F32)
+def place_tile(ref, held, lines, rows, group, f, q, chunk, t):
+    used = min(SUB, chunk_levels(chunk) - SUB * t)
+    base = (first_level(chunk) + SUB * t) * rows
+    row = first_rows()[group] + q
+    for lane in range(2):
+        ref[pl.ds(0, used), pl.ds(lane * LANES, LANES)] = held[
+            f, lane, pl.ds(base + row, used, stride=rows), :
+        ]
+    for extra in range(SUB - used):
+        if f < 2:
+            line = lines[EXTRA * f + extra, pl.ds(row, 1), :]
+        else:
+            line = jnp.zeros((1, 2 * LANES), F32)
+        ref[pl.ds(used + extra, 1), :] = line
+
+
+def halves_kernel(rows, held, lines, *halves):
+    for c in range(len(CHUNKS)):
+        for t in range(CHUNKS[c]):
+            for f in range(FIELDS):
+                for group in range(2):
+                    for q in range(RIM):
+                        ref = halves[2 * c + group].at[f * RIM + q, t]
+                        place_tile(ref, held, lines, rows, group, f, q, c, t)
+
+
+def pack_edges(fields, wind, surface, depth):
+    levels, rows, columns = fields[0].shape
+    flat = [item.reshape(levels * rows, columns) for item in fields]
+    arguments = [
+        pltpu.with_memory_space_constraint(item, pltpu.HBM)
+        for item in (*flat, wind, surface, depth)
+    ]
+    vmem = pl.BlockSpec(memory_space=pltpu.VMEM)
+    return pl.pallas_call(
+        functools.partial(edges_kernel, rows),
+        out_shape=[jax.ShapeDtypeStruct((2, sum(CHUNKS), SUB, LANES), F32)] * 2
+        + [
+            jax.ShapeDtypeStruct((FIELDS, 2, levels * rows, LANES), F32),
+            jax.ShapeDtypeStruct((2 * EXTRA, rows, columns), F32),
+        ],
+        in_specs=[pl.BlockSpec(memory_space=pltpu.HBM)] * len(arguments),
+        out_specs=[vmem] * 4,
+        scratch_shapes=[
+            pltpu.VMEM((FIELDS, 2, RIM, SUB, columns), F32),
+            pltpu.VMEM(depth.shape, depth.dtype),
+            pltpu.SemaphoreType.DMA((FIELDS, 2)),
+            pltpu.SemaphoreType.DMA((3,)),
+        ],
+        compiler_params=pltpu.CompilerParams(vmem_limit_bytes=PACK_VMEM),
+        name="edges",
+    )(*arguments)
+
+
+def pack_halves(rows, held, lines):
+    vmem = pl.BlockSpec(memory_space=pltpu.VMEM)
+    shapes = [
+        jax.ShapeDtypeStruct((FIELDS * RIM + 1, tiles, SUB, lines.shape[-1]), F32)
         for tiles in CHUNKS
         for _ in range(2)
     ]
-
-
-def pack(fields, lines):
-    levels, rows, columns = fields[0].shape
-    flat = [item.reshape(levels * rows, columns) for item in fields]
-    shapes = half_shapes(columns)
-    shapes += [jax.ShapeDtypeStruct((2, sum(CHUNKS), SUB, LANES), F32)] * 2
-    *halves, across_a, across_b = pl.pallas_call(
-        functools.partial(pack_kernel, rows),
+    return pl.pallas_call(
+        functools.partial(halves_kernel, rows),
         out_shape=shapes,
-        in_specs=[pl.BlockSpec(memory_space=pltpu.HBM)] * (FIELDS + 3),
-        out_specs=[pl.BlockSpec(memory_space=pltpu.VMEM)] * len(shapes),
-        scratch_shapes=[
-            pltpu.VMEM((FIELDS, 2, levels * rows, LANES), F32),
-            pltpu.SemaphoreType.DMA((FIELDS, 2)),
-            pltpu.VMEM((2 * EXTRA, rows, columns), F32),
-            pltpu.VMEM((rows, columns), jnp.int32),
-            pltpu.SemaphoreType.DMA((3,)),
-        ],
+        in_specs=[vmem] * 2,
+        out_specs=[vmem] * len(shapes),
         compiler_params=pltpu.CompilerParams(vmem_limit_bytes=PACK_VMEM),
-        name="pack",
-    )(*[pltpu.with_memory_space_constraint(item, pltpu.HBM) for item in (*flat, *lines)])
-    return halves, across_a, across_b
+        name="halves",
+    )(held, lines)
 
 
 def rims_kernel(across_a, across_b, *refs):
@@ -350,10 +378,11 @@
 
     def tendency(get, lowest, highest, carry_at, emit, finish=None):
         pressure(get, lowest, highest, carry_at)
-        for group in GROUPS:
-            first_pass(get, lowest, highest, group)
-        for group in GROUPS:
-            second_pass(lowest, highest, group, emit)
+        widths = [own if finish is not None and group[0] > 1 else wide for group in GROUPS]
+        for group, width in zip(GROUPS, widths):
+            first_pass(get, lowest, highest, group, width)
+        for group, width in zip(GROUPS, widths):
+            second_pass(lowest, highest, group, emit, width)
             if finish is not None:
                 finish(group)
 
@@ -361,7 +390,7 @@
         values = [get(f, a) for f in group]
         return values, [east_of(x) for x in values], [west_of(x) for x in values]
 
-    def first_pass(get, lowest, highest, group):
+    def first_pass(get, lowest, highest, group, width):
         span = range(len(group))
         below = [get(f, lowest - 2) for f in group]
         here, east, west = turned(get, group, lowest - 1)
@@ -381,7 +410,11 @@
             if lowest <= a <= highest:
                 flows = [here[group.index(f)] if f in group else get(f, a) for f in range(2)]
                 u, v = (-0.5 * ADVECT) * flows[0], (-0.5 * ADVECT) * flows[1]
-                mixed = [u * (right[i] + left[i]) + v * (up[i] + up_before[i]) for i in span]
+                mixed = [
+                    u[:, :width] * (right[i] + left[i])[:, :width]
+                    + v[:, :width] * (up[i] + up_before[i])[:, :width]
+                    for i in span
+                ]
                 for i, f in enumerate(group):
                     if f < 2:
                         turn = rotate[pl.ds(a, 1), :] * wets[a]
@@ -390,36 +423,39 @@
                     if f == 1:
                         mixed[i] = mixed[i] - (turn * flows[0] + press_y[a])
                 for i, f in enumerate(group):
-                    mixes[f, a] = mixed[i]
+                    mixes[f, a, :, pl.ds(0, width)] = mixed[i]
             for i, f in enumerate(group):
                 laps[f, a] = lap[i]
             if a <= highest:
                 here, east, west = after, east_after, west_after
 
-    def second_pass(lowest, highest, group, emit):
+    def second_pass(lowest, highest, group, emit, width):
         span = range(len(group))
+        part = pl.ds(0, width)
 
         def get(f, a):
             return laps[f, a]
 
-        below = [get(f, lowest - 1) for f in group]
+        below = [laps[f, lowest - 1, :, part] for f in group]
         here, east, west = turned(get, group, lowest)
-        face = wets_y[lowest - 1]
-        up = [face * (x - y) for x, y in zip(here, below)]
+        face = wets_y[lowest - 1, :, part]
+        up = [face * (x[:, :width] - y) for x, y in zip(here, below)]
         for a in range(lowest, highest + 1):
             if a < highest:
                 after, east_after, west_after = turned(get, group, a + 1)
             else:
                 after = [get(f, a + 1) for f in group]
-            face, side_x, side_w = wets_y[a], wets_x[a], wets_w[a]
+            face, side_x, side_w = (ref[a, :, part] for ref in (wets_y, wets_x, wets_w))
+            near = [x[:, :width] for x in here]
             up_before = up
-            up = [face * (x - y) for x, y in zip(after, here)]
+            up = [face * (x[:, :width] - y) for x, y in zip(after, near)]
             smooth = [
-                (side_x * (east[i] - here[i]) - side_w * (here[i] - west[i]))
+                (side_x * (east[i][:, :width] - near[i]) - side_w * (near[i] - west[i][:, :width]))
                 + (up[i] - up_before[i])
                 for i in span
             ]
-            emit(a, group, [mixes[f, a] - KAPPA * smooth[i] for i, f in enumerate(group)])
+            mixed = [mixes[f, a, :, part] for f in group]
+            emit(a, group, [x - KAPPA * y for x, y in zip(mixed, smooth)])
             if a < highest:
                 here, east, west = after, east_after, west_after
 
@@ -457,7 +493,11 @@
 
         def emit_second(a, group, values):
             values = winded(a, group, values)
-            news = [0.5 * ((cur[f, a] + between[f, a]) + value) for f, value in zip(group, values)]
+            part = pl.ds(0, values[0].shape[-1])
+            news = [
+                0.5 * ((cur[f, a, :, part] + between[f, a, :, part]) + value)
+                for f, value in zip(group, values)
+            ]
             r = a - RIM
             adds = [sums[f, r] + wets[a] * new for f, new in zip(group, news) if f < 2]
             for f, add in zip(group, adds):
@@ -627,7 +667,7 @@
     levels, rows, columns = eastward_flow.shape
     assert rows == 2 * RIM and columns == 2 * LANES and levels + EXTRA == SUB * sum(CHUNKS)
     along_y, along_x = lax.axis_size("by"), lax.axis_size("bx")
-    pairs_y = (swaps(along_y, 0, False), swaps(along_y, 1, False))
+    pairs_y = (swaps(along_y, 1, False), swaps(along_y, 0, False))
     pairs_x = (swaps(along_x, 0, True), swaps(along_x, 1, True))
     row_index = lax.axis_index("by") * rows - RIM + jnp.arange(rows + 2 * RIM)
     rotate = 1.2 * jnp.sin(
@@ -636,15 +676,16 @@
     rotate = jnp.broadcast_to(rotate[:, None], (rows + 2 * RIM, columns + LANES))
 
     fields = (eastward_flow, northward_flow, heat_anomaly, salt_anomaly)
-    lines = (air_stress_forcing, earlier_sea_height_load, ocean_layer_depths)
-    halves, edge_a, edge_b = pack(fields, lines)
+    edge_a, edge_b, held, lines = pack_edges(
+        fields, air_stress_forcing, earlier_sea_height_load, ocean_layer_depths
+    )
+    halves = pack_halves(rows, held, lines)
     across_a = lax.ppermute(edge_a, "bx", pairs_x[0])
     across_b = lax.ppermute(edge_b, "bx", pairs_x[1])
     halves = put_rims(halves, across_a, across_b)
 
     def send(own):
-        met_b = lax.ppermute(own[1], "by", pairs_y[1])
-        return lax.ppermute(own[0], "by", pairs_y[0]), met_b
+        return [lax.ppermute(item, "by", pairs) for item, pairs in zip(own, pairs_y)]
 
     rims = [send(halves[chunk]) for chunk in range(AHEAD)]
     kept, news = None, None

time: 50.7 us -> 51.6 us (1.018); the launches traced: 50.4 us -> 50.7 us
  starting transfers between devices: 19.5 us -> 17 us
  waiting for transfers between devices: 7.7 us -> 10.2 us
    ppermute x10, waiting for transfers between devices: 4.22 us -> 7.22 us  [send(): lax.ppermute(item, 'by', pairs)]
    ppermute x10, starting transfers between devices: 17.9 us -> 15.3 us  [send(): lax.ppermute(item, 'by', pairs)]
    pallas_call x1 -> x2, Pallas kernels: 2.49 us -> 2.78 us  [the longest x1 2.35 us: pack_edges(): pl.pallas_call(functools.partial(edges_kernel, rows), out_shape=[jax.Shap...]
  transfers between devices with their start and end apart: 12 -> 12, of which waited for: 4 -> 6; matrix products, arithmetic and copies ran while one was open for 0% -> 0% of each run, Pallas kernels for 28% -> 28%
where the time goes in v3:
time: 51.6 us; the launch traced here: 50.7 us
  Pallas kernels  22.6 us (44%)
  starting transfers between devices  17 us (33%)
  waiting for transfers between devices  10.2 us (20%)
  between operations  0.82 us (2%)
    pallas_call x4, Pallas kernels, step(): pl.pallas_call(functools.partial(step_kernel, chunk, rows), out_shape=sha...  18.4 us
    ppermute x10, starting transfers between devices, send(): lax.ppermute(item, 'by', pairs)  15.3 us
    ppermute x10, waiting for transfers between devices, send(): lax.ppermute(item, 'by', pairs)  7.22 us
    ppermute x1, waiting for transfers between devices, body(): across_b = lax.ppermute(edge_b, 'bx', pairs_x[1])  3.03 us
    pallas_call x1, Pallas kernels, pack_edges(): pl.pallas_call(functools.partial(edges_kernel, rows), out_shape=[jax.Shap...  2.35 us
    ppermute x1, starting transfers between devices, body(): across_b = lax.ppermute(edge_b, 'bx', pairs_x[1])  1.54 us
  transfers between devices with their start and end apart: 12, of which 6 were waited for; matrix products, arithmetic and copies ran while one was open for 0% of the time, Pallas kernels for 28%

profile of v3, /device:TPU:12, one launch (start us, length us, event | category | flops | bytes accessed | tf_op | source)
XLA Modules:
  0.0 50.7 jit_solution(3488004617350144535)
XLA Ops:
  0.6 2.3 %edges.1 = (f32[2,8,8,128]{3,2,1,0:T(8,128)S(1)}, f32[2,8,8,128]{3,2,1,0:T(8,128)S(1)}, f32[4,2,496,128]{3,2,1,0:T(8,128)S(1)}, f32[4,8,256]{2,1,0:T(8,128)S(1)}) custom-call(f32[496,256]{1,0:T(8,128)} %bitcast.12, f32[496,256]{1,0:T(8,128)} %bitcast.13, f32[496,256]{1,0:T(8,128)} %bitcast.14, f32[496,256]{1,0:T(8,128)} %bitcast.15, f32[2,8,256]{2,1,0:T(8,128)} %refs_4_.1, ...), custom_call_target="tpu_custom_call" | custom-call | tf_op jit(solution)/shard_map/edges/pallas_call | solution.py:172
  3.0 0.1 collective-permute-start
  3.1 1.5 %collective-permute-start.1 = (f32[2,8,8,128]{3,2,1,0:T(8,128)S(1)}, f32[2,8,8,128]{3,2,1,0:T(8,128)S(1)}, u32[]{:S(2)}, u32[]{:S(2)}) collective-permute-start(f32[2,8,8,128]{3,2,1,0:T(8,128)S(1)} %get-tuple-element.61), channel_id=1, source_target_pairs={{1,2},{2,1},{3,4},{4,3},{5,6},{6,5},{7,0},{0,7},{9,10},{10,9},{11,... | collective-permute-start | bytes 196616 | tf_op jit(solution)/shard_map/ppermute | solution.py:684
  4.6 0.4 halves.1
  5.0 3.0 %collective-permute-done.1.across_b = f32[2,8,8,128]{3,2,1,0:T(8,128)S(1)} collective-permute-done((f32[2,8,8,128]{3,2,1,0:T(8,128)S(1)}, f32[2,8,8,128]{3,2,1,0:T(8,128)S(1)}, u32[]{:S(2)}, u32[]{:S(2)}) %collective-permute-start.1) | collective-permute-done | bytes 65568 | tf_op jit(solution)/shard_map/ppermute | solution.py:684
  8.1 0.3 rims.1
  8.4 3.5 %collective-permute-start.2 = (f32[17,2,8,256]{3,2,1,0:T(8,128)S(1)}, f32[17,2,8,256]{3,2,1,0:T(8,128)S(1)}, u32[]{:S(2)}, u32[]{:S(2)}) collective-permute-start(f32[17,2,8,256]{3,2,1,0:T(8,128)S(1)} %get-tuple-element.74.refs_2_), channel_id=1, source_target_pairs={{8,16},{16,8},{9,17},{17,9},{10,18},{18,10},{11,19},{19,11},{12,20... | collective-permute-start | bytes 835592 | tf_op jit(solution)/shard_map/ppermute | solution.py:688
  11.9 0.1 collective-permute-start.3
  11.9 2.4 %collective-permute-start.8 = (f32[17,2,8,256]{3,2,1,0:T(8,128)S(1)}, f32[17,2,8,256]{3,2,1,0:T(8,128)S(1)}, u32[]{:S(2)}, u32[]{:S(2)}) collective-permute-start(f32[17,2,8,256]{3,2,1,0:T(8,128)S(1)} %get-tuple-element.83.refs_2_), channel_id=1, source_target_pairs={{8,16},{16,8},{9,17},{17,9},{10,18},{18,10},{11,19},{19,11},{12,20... | collective-permute-start | bytes 835592 | tf_op jit(solution)/shard_map/ppermute | solution.py:688
  14.4 0.4 collective-permute-start.9
  14.7 3.2 %collective-permute-start.6 = (f32[17,2,8,256]{3,2,1,0:T(8,128)S(1)}, f32[17,2,8,256]{3,2,1,0:T(8,128)S(1)}, u32[]{:S(2)}, u32[]{:S(2)}) collective-permute-start(f32[17,2,8,256]{3,2,1,0:T(8,128)S(1)} %get-tuple-element.81.refs_2_), channel_id=1, source_target_pairs={{8,16},{16,8},{9,17},{17,9},{10,18},{18,10},{11,19},{19,11},{12,20... | collective-permute-start | bytes 835592 | tf_op jit(solution)/shard_map/ppermute | solution.py:688
  17.9 1.9 %collective-permute-done.2.refs_1_ = f32[17,2,8,256]{3,2,1,0:T(8,128)S(1)} collective-permute-done((f32[17,2,8,256]{3,2,1,0:T(8,128)S(1)}, f32[17,2,8,256]{3,2,1,0:T(8,128)S(1)}, u32[]{:S(2)}, u32[]{:S(2)}) %collective-permute-start.2) | collective-permute-done | bytes 278560 | tf_op jit(solution)/shard_map/ppermute | solution.py:688
  19.9 1.7 %collective-permute-done.3.refs_4_ = f32[17,2,8,256]{3,2,1,0:T(8,128)S(1)} collective-permute-done((f32[17,2,8,256]{3,2,1,0:T(8,128)S(1)}, f32[17,2,8,256]{3,2,1,0:T(8,128)S(1)}, u32[]{:S(2)}, u32[]{:S(2)}) %collective-permute-start.3) | collective-permute-done | bytes 278560 | tf_op jit(solution)/shard_map/ppermute | solution.py:688
  21.6 4.7 %step.4 = (f32[496,256]{1,0:T(8,128)}, f32[496,256]{1,0:T(8,128)}, f32[496,256]{1,0:T(8,128)}, f32[496,256]{1,0:T(8,128)}, f32[4,16,8,384]{3,2,1,0:T(8,128)S(1)}...) custom-call(f32[16,384]{1,0:T(8,128)S(1)} %broadcast_in_dim.2.refs_0_, ...), custom_call_target="tpu_custom_call" | custom-call | tf_op jit(solution)/shard_map/step/pallas_call | solution.py:583
  26.3 2.3 %collective-permute-start.4 = (f32[17,2,8,256]{3,2,1,0:T(8,128)S(1)}, f32[17,2,8,256]{3,2,1,0:T(8,128)S(1)}, u32[]{:S(2)}, u32[]{:S(2)}) collective-permute-start(f32[17,2,8,256]{3,2,1,0:T(8,128)S(1)} %get-tuple-element.78.refs_2_), channel_id=1, source_target_pairs={{8,16},{16,8},{9,17},{17,9},{10,18},{18,10},{11,19},{19,11},{12,20... | collective-permute-start | bytes 835592 | tf_op jit(solution)/shard_map/ppermute | solution.py:688
  28.8 4.6 %step.5 = (f32[496,256]{1,0:T(8,128)}, f32[496,256]{1,0:T(8,128)}, f32[496,256]{1,0:T(8,128)}, f32[496,256]{1,0:T(8,128)}, f32[24,8,384]{2,1,0:T(8,128)S(1)}, /*index=5*/f32[2,8,8,384]{3,2,1,0:T(8,128)S(1)}) custom-call(f32[16,384]{1,0:T(8,128)S(1)} %broadcast_in_dim.2.refs_0_, ...), custom_call_target="tpu_custom_call", output_to_operand_aliasing={{0}: (8, {}), {1}: (9, {}), {2}: (10, {}), {3}: (11, {})} | custom-call | tf_op jit(solution)/shard_map/step/pallas_call | solution.py:583
  33.3 0.1 collective-permute-done.7.refs_4_
  33.5 4.6 %step.6 = (f32[496,256]{1,0:T(8,128)}, f32[496,256]{1,0:T(8,128)}, f32[496,256]{1,0:T(8,128)}, f32[496,256]{1,0:T(8,128)}, f32[24,8,384]{2,1,0:T(8,128)S(1)}, /*index=5*/f32[2,8,8,384]{3,2,1,0:T(8,128)S(1)}) custom-call(f32[16,384]{1,0:T(8,128)S(1)} %broadcast_in_dim.2.refs_0_, ...), custom_call_target="tpu_custom_call", output_to_operand_aliasing={{0}: (8, {}), {1}: (9, {}), {2}: (10, {}), {3}: (11, {})} | custom-call | tf_op jit(solution)/shard_map/step/pallas_call | solution.py:583
  38.0 4.5 %step.7 = (f32[496,256]{1,0:T(8,128)}, f32[496,256]{1,0:T(8,128)}, f32[496,256]{1,0:T(8,128)}, f32[496,256]{1,0:T(8,128)}, f32[2,4,384]{2,1,0:T(4,128)S(1)}, /*index=5*/f32[2,4,384]{2,1,0:T(4,128)S(1)}) custom-call(f32[16,384]{1,0:T(8,128)S(1)} %broadcast_in_dim.2.refs_0_, ...), custom_call_target="tpu_custom_call", output_to_operand_aliasing={{0}: (8, {}), {1}: (9, {}), {2}: (10, {}), {3}: (11, {})} | custom-call | tf_op jit(solution)/shard_map/step/pallas_call | solution.py:583
  42.6 3.4 %collective-permute-start.10 = (f32[2,4,384]{2,1,0:T(4,128)S(1)}, f32[2,4,384]{2,1,0:T(4,128)S(1)}, u32[]{:S(2)}, u32[]{:S(2)}) collective-permute-start(f32[2,4,384]{2,1,0:T(4,128)S(1)} %get-tuple-element.113.own_a), channel_id=1, source_target_pairs={{8,16},{16,8},{9,17},{17,9},{10,18},{18,10},{11,19},{19,11},{12,20... | collective-permute-start | bytes 36872 | tf_op jit(solution)/shard_map/ppermute | solution.py:688
  46.1 0.2 prepare.1.ready
  46.3 1.9 %collective-permute-done.10.met_a = f32[2,4,384]{2,1,0:T(4,128)S(1)} collective-permute-done((f32[2,4,384]{2,1,0:T(4,128)S(1)}, f32[2,4,384]{2,1,0:T(4,128)S(1)}, u32[]{:S(2)}, u32[]{:S(2)}) %collective-permute-start.10) | collective-permute-done | bytes 12320 | tf_op jit(solution)/shard_map/ppermute | solution.py:688
  48.2 1.6 %collective-permute-done.11.met_b = f32[2,4,384]{2,1,0:T(4,128)S(1)} collective-permute-done((f32[2,4,384]{2,1,0:T(4,128)S(1)}, f32[2,4,384]{2,1,0:T(4,128)S(1)}, u32[]{:S(2)}, u32[]{:S(2)}) %collective-permute-start.11) | collective-permute-done | bytes 12320 | tf_op jit(solution)/shard_map/ppermute | solution.py:688
  49.8 1.0 %solve.1 = f32[8,256]{1,0:T(8,128)} custom-call(f32[10,16,384]{2,1,0:T(8,128)S(1)} %prepare.1.ready, f32[2,4,384]{2,1,0:T(4,128)S(1)} %collective-permute-done.10.met_a, f32[2,4,384]{2,1,0:T(4,128)S(1)} %get-tuple-element.113.own_a, f32[2,4,384]{2,1,0:T(4,128)S(1)} %get-tuple-element.114.own_b, f32[2,4,384]{2,1,0:T(4,128)S(1)} %collective-permute-done.11.met_b), custom_call_target="tpu_custom_call" | custom-call | tf_op jit(solution)/shard_map/solve/pallas_call | solution.py:721
  (11 shorter events, 0.3 us)
Async XLA Ops:
  3.0 2.1 %collective-permute-start = (f32[2,8,8,128]{3,2,1,0:T(8,128)S(1)}, f32[2,8,8,128]{3,2,1,0:T(8,128)S(1)}, u32[]{:S(2)}, u32[]{:S(2)}) collective-permute-start(f32[2,8,8,128]{3,2,1,0:T(8,128)S(1)} %get-tuple-element.60), channel_id=1, source_target_pairs={{0,1},{1,0},{2,3},{3,2},{4,5},{5,4},{6,7},{7,6},{8,9},{9,8},{10,11... | collective-permute-start | bytes 196616 | tf_op jit(solution)/shard_map/ppermute | solution.py:683
  3.1 5.0 %collective-permute-start.1 = (f32[2,8,8,128]{3,2,1,0:T(8,128)S(1)}, f32[2,8,8,128]{3,2,1,0:T(8,128)S(1)}, u32[]{:S(2)}, u32[]{:S(2)}) collective-permute-start(f32[2,8,8,128]{3,2,1,0:T(8,128)S(1)} %get-tuple-element.61), channel_id=1, source_target_pairs={{1,2},{2,1},{3,4},{4,3},{5,6},{6,5},{7,0},{0,7},{9,10},{10,9},{11,... | collective-permute-start | bytes 196616 | tf_op jit(solution)/shard_map/ppermute | solution.py:684
  8.4 11.5 %collective-permute-start.2 = (f32[17,2,8,256]{3,2,1,0:T(8,128)S(1)}, f32[17,2,8,256]{3,2,1,0:T(8,128)S(1)}, u32[]{:S(2)}, u32[]{:S(2)}) collective-permute-start(f32[17,2,8,256]{3,2,1,0:T(8,128)S(1)} %get-tuple-element.74.refs_2_), channel_id=1, source_target_pairs={{8,16},{16,8},{9,17},{17,9},{10,18},{18,10},{11,19},{19,11},{12,20... | collective-permute-start | bytes 835592 | tf_op jit(solution)/shard_map/ppermute | solution.py:688
  11.9 9.7 %collective-permute-start.3 = (f32[17,2,8,256]{3,2,1,0:T(8,128)S(1)}, f32[17,2,8,256]{3,2,1,0:T(8,128)S(1)}, u32[]{:S(2)}, u32[]{:S(2)}) collective-permute-start(f32[17,2,8,256]{3,2,1,0:T(8,128)S(1)} %get-tuple-element.75.refs_3_), channel_id=1, source_target_pairs={{0,8},{8,0},{16,24},{24,16},{1,9},{9,1},{17,25},{25,17},{2,10},{10... | collective-permute-start | bytes 835592 | tf_op jit(solution)/shard_map/ppermute | solution.py:688
  11.9 16.7 %collective-permute-start.8 = (f32[17,2,8,256]{3,2,1,0:T(8,128)S(1)}, f32[17,2,8,256]{3,2,1,0:T(8,128)S(1)}, u32[]{:S(2)}, u32[]{:S(2)}) collective-permute-start(f32[17,2,8,256]{3,2,1,0:T(8,128)S(1)} %get-tuple-element.83.refs_2_), channel_id=1, source_target_pairs={{8,16},{16,8},{9,17},{17,9},{10,18},{18,10},{11,19},{19,11},{12,20... | collective-permute-start | bytes 835592 | tf_op jit(solution)/shard_map/ppermute | solution.py:688
  14.4 14.4 %collective-permute-start.9 = (f32[17,2,8,256]{3,2,1,0:T(8,128)S(1)}, f32[17,2,8,256]{3,2,1,0:T(8,128)S(1)}, u32[]{:S(2)}, u32[]{:S(2)}) collective-permute-start(f32[17,2,8,256]{3,2,1,0:T(8,128)S(1)} %get-tuple-element.84.refs_3_), channel_id=1, source_target_pairs={{0,8},{8,0},{16,24},{24,16},{1,9},{9,1},{17,25},{25,17},{2,10},{10... | collective-permute-start | bytes 835592 | tf_op jit(solution)/shard_map/ppermute | solution.py:688
  14.7 18.6 %collective-permute-start.6 = (f32[17,2,8,256]{3,2,1,0:T(8,128)S(1)}, f32[17,2,8,256]{3,2,1,0:T(8,128)S(1)}, u32[]{:S(2)}, u32[]{:S(2)}) collective-permute-start(f32[17,2,8,256]{3,2,1,0:T(8,128)S(1)} %get-tuple-element.81.refs_2_), channel_id=1, source_target_pairs={{8,16},{16,8},{9,17},{17,9},{10,18},{18,10},{11,19},{19,11},{12,20... | collective-permute-start | bytes 835592 | tf_op jit(solution)/shard_map/ppermute | solution.py:688
  19.8 13.6 %collective-permute-start.7 = (f32[17,2,8,256]{3,2,1,0:T(8,128)S(1)}, f32[17,2,8,256]{3,2,1,0:T(8,128)S(1)}, u32[]{:S(2)}, u32[]{:S(2)}) collective-permute-start(f32[17,2,8,256]{3,2,1,0:T(8,128)S(1)} %get-tuple-element.82.refs_3_), channel_id=1, source_target_pairs={{0,8},{8,0},{16,24},{24,16},{1,9},{9,1},{17,25},{25,17},{2,10},{10... | collective-permute-start | bytes 835592 | tf_op jit(solution)/shard_map/ppermute | solution.py:688
  26.3 11.7 %collective-permute-start.4 = (f32[17,2,8,256]{3,2,1,0:T(8,128)S(1)}, f32[17,2,8,256]{3,2,1,0:T(8,128)S(1)}, u32[]{:S(2)}, u32[]{:S(2)}) collective-permute-start(f32[17,2,8,256]{3,2,1,0:T(8,128)S(1)} %get-tuple-element.78.refs_2_), channel_id=1, source_target_pairs={{8,16},{16,8},{9,17},{17,9},{10,18},{18,10},{11,19},{19,11},{12,20... | collective-permute-start | bytes 835592 | tf_op jit(solution)/shard_map/ppermute | solution.py:688
  28.7 9.4 %collective-permute-start.5 = (f32[17,2,8,256]{3,2,1,0:T(8,128)S(1)}, f32[17,2,8,256]{3,2,1,0:T(8,128)S(1)}, u32[]{:S(2)}, u32[]{:S(2)}) collective-permute-start(f32[17,2,8,256]{3,2,1,0:T(8,128)S(1)} %get-tuple-element.79.refs_3_), channel_id=1, source_target_pairs={{0,8},{8,0},{16,24},{24,16},{1,9},{9,1},{17,25},{25,17},{2,10},{10... | collective-permute-start | bytes 835592 | tf_op jit(solution)/shard_map/ppermute | solution.py:688
  42.6 5.6 %collective-permute-start.10 = (f32[2,4,384]{2,1,0:T(4,128)S(1)}, f32[2,4,384]{2,1,0:T(4,128)S(1)}, u32[]{:S(2)}, u32[]{:S(2)}) collective-permute-start(f32[2,4,384]{2,1,0:T(4,128)S(1)} %get-tuple-element.113.own_a), channel_id=1, source_target_pairs={{8,16},{16,8},{9,17},{17,9},{10,18},{18,10},{11,19},{19,11},{12,20... | collective-permute-start | bytes 36872 | tf_op jit(solution)/shard_map/ppermute | solution.py:688
  46.0 3.8 %collective-permute-start.11 = (f32[2,4,384]{2,1,0:T(4,128)S(1)}, f32[2,4,384]{2,1,0:T(4,128)S(1)}, u32[]{:S(2)}, u32[]{:S(2)}) collective-permute-start(f32[2,4,384]{2,1,0:T(4,128)S(1)} %get-tuple-element.114.own_b), channel_id=1, source_target_pairs={{0,8},{8,0},{16,24},{24,16},{1,9},{9,1},{17,25},{25,17},{2,10},{10... | collective-permute-start | bytes 36872 | tf_op jit(solution)/shard_map/ppermute | solution.py:688

commit v4 on v3

--- a/solution.py
+++ b/solution.py
@@ -24,7 +24,7 @@
 RIM = 4
 EDGE = 8
 EXTRA = 2
-CHUNKS = (2, 2, 2, 2)
+CHUNKS = (3, 3, 2)
 AHEAD = 3
 FAR = 1000000
 BATCH = 4

time: 51.6 us -> 53.5 us (1.037)
  waiting for transfers between devices: 10.2 us -> 14.4 us
  starting transfers between devices: 17 us -> 13.5 us
  Pallas kernels: 22.6 us -> 23.7 us
    ppermute x10 -> x8, waiting for transfers between devices: 7.22 us -> 11.4 us  [send(): lax.ppermute(item, 'by', pairs)]
    ppermute x10 -> x8, starting transfers between devices: 15.3 us -> 11.9 us  [send(): lax.ppermute(item, 'by', pairs)]
    pallas_call x4 -> x3, Pallas kernels: 18.4 us -> 19.6 us  [step(): pl.pallas_call(functools.partial(step_kernel, chunk, rows), out_shape=sha...]
  transfers between devices with their start and end apart: 12 -> 10, of which waited for: 6 -> 6; matrix products, arithmetic and copies ran while one was open for 0% -> 0% of each run, Pallas kernels for 28% -> 28%
where the time goes in v4:
time: 53.5 us; the launch traced here: 52.5 us
  Pallas kernels  23.7 us (44%)
  waiting for transfers between devices  14.4 us (27%)
  starting transfers between devices  13.5 us (25%)
  between operations  0.78 us (1%)
    pallas_call x3, Pallas kernels, step(): pl.pallas_call(functools.partial(step_kernel, chunk, rows), out_shape=sha...  19.6 us
    ppermute x8, starting transfers between devices, send(): lax.ppermute(item, 'by', pairs)  11.9 us
    ppermute x8, waiting for transfers between devices, send(): lax.ppermute(item, 'by', pairs)  11.4 us
    ppermute x1, waiting for transfers between devices, body(): across_b = lax.ppermute(edge_b, 'bx', pairs_x[1])  3.03 us
    pallas_call x1, Pallas kernels, pack_edges(): pl.pallas_call(functools.partial(edges_kernel, rows), out_shape=[jax.Shap...  2.35 us
    ppermute x1, starting transfers between devices, body(): across_b = lax.ppermute(edge_b, 'bx', pairs_x[1])  1.54 us
  transfers between devices with their start and end apart: 10, of which 6 were waited for; matrix products, arithmetic and copies ran while one was open for 0% of the time, Pallas kernels for 28%

profile of v4, /device:TPU:12, one launch (start us, length us, event | category | flops | bytes accessed | tf_op | source)
XLA Modules:
  0.0 52.5 jit_solution(85910208680645349)
XLA Ops:
  0.6 2.3 %edges.1 = (f32[2,8,8,128]{3,2,1,0:T(8,128)S(1)}, f32[2,8,8,128]{3,2,1,0:T(8,128)S(1)}, f32[4,2,496,128]{3,2,1,0:T(8,128)S(1)}, f32[4,8,256]{2,1,0:T(8,128)S(1)}) custom-call(f32[496,256]{1,0:T(8,128)} %bitcast.12, f32[496,256]{1,0:T(8,128)} %bitcast.13, f32[496,256]{1,0:T(8,128)} %bitcast.14, f32[496,256]{1,0:T(8,128)} %bitcast.15, f32[2,8,256]{2,1,0:T(8,128)} %refs_4_.1, ...), custom_call_target="tpu_custom_call" | custom-call | tf_op jit(solution)/shard_map/edges/pallas_call | solution.py:172
  3.0 0.1 collective-permute-start
  3.1 1.5 %collective-permute-start.1 = (f32[2,8,8,128]{3,2,1,0:T(8,128)S(1)}, f32[2,8,8,128]{3,2,1,0:T(8,128)S(1)}, u32[]{:S(2)}, u32[]{:S(2)}) collective-permute-start(f32[2,8,8,128]{3,2,1,0:T(8,128)S(1)} %get-tuple-element.47), channel_id=1, source_target_pairs={{1,2},{2,1},{3,4},{4,3},{5,6},{6,5},{7,0},{0,7},{9,10},{10,9},{11,... | collective-permute-start | bytes 196616 | tf_op jit(solution)/shard_map/ppermute | solution.py:684
  4.6 0.4 halves.1
  5.0 3.0 %collective-permute-done.1.across_b = f32[2,8,8,128]{3,2,1,0:T(8,128)S(1)} collective-permute-done((f32[2,8,8,128]{3,2,1,0:T(8,128)S(1)}, f32[2,8,8,128]{3,2,1,0:T(8,128)S(1)}, u32[]{:S(2)}, u32[]{:S(2)}) %collective-permute-start.1) | collective-permute-done | bytes 65568 | tf_op jit(solution)/shard_map/ppermute | solution.py:684
  8.1 0.2 rims.1
  8.3 3.5 %collective-permute-start.4 = (f32[17,3,8,256]{3,2,1,0:T(8,128)S(1)}, f32[17,3,8,256]{3,2,1,0:T(8,128)S(1)}, u32[]{:S(2)}, u32[]{:S(2)}) collective-permute-start(f32[17,3,8,256]{3,2,1,0:T(8,128)S(1)} %get-tuple-element.58.refs_2_), channel_id=1, source_target_pairs={{8,16},{16,8},{9,17},{17,9},{10,18},{18,10},{11,19},{19,11},{12,20... | collective-permute-start | bytes 1253384 | tf_op jit(solution)/shard_map/ppermute | solution.py:688
  11.8 0.1 collective-permute-start.5
  11.8 2.4 %collective-permute-start.6 = (f32[17,3,8,256]{3,2,1,0:T(8,128)S(1)}, f32[17,3,8,256]{3,2,1,0:T(8,128)S(1)}, u32[]{:S(2)}, u32[]{:S(2)}) collective-permute-start(f32[17,3,8,256]{3,2,1,0:T(8,128)S(1)} %get-tuple-element.61.refs_2_), channel_id=1, source_target_pairs={{8,16},{16,8},{9,17},{17,9},{10,18},{18,10},{11,19},{19,11},{12,20... | collective-permute-start | bytes 1253384 | tf_op jit(solution)/shard_map/ppermute | solution.py:688
  14.2 0.4 collective-permute-start.7
  14.6 3.2 %collective-permute-start.2 = (f32[17,2,8,256]{3,2,1,0:T(8,128)S(1)}, f32[17,2,8,256]{3,2,1,0:T(8,128)}, u32[]{:S(2)}, u32[]{:S(2)}) collective-permute-start(f32[17,2,8,256]{3,2,1,0:T(8,128)S(1)} %get-tuple-element.56.refs_2_), channel_id=1, source_target_pairs={{8,16},{16,8},{9,17},{17,9},{10,18},{18,10},{11,19},{19,11},{12,20... | collective-permute-start | bytes 835592 | tf_op jit(solution)/shard_map/ppermute | solution.py:688
  17.8 5.0 %collective-permute-done.4.refs_1_ = f32[17,3,8,256]{3,2,1,0:T(8,128)S(1)} collective-permute-done((f32[17,3,8,256]{3,2,1,0:T(8,128)S(1)}, f32[17,3,8,256]{3,2,1,0:T(8,128)S(1)}, u32[]{:S(2)}, u32[]{:S(2)}) %collective-permute-start.4) | collective-permute-done | bytes 417824 | tf_op jit(solution)/shard_map/ppermute | solution.py:688
  22.8 1.7 %collective-permute-done.5.refs_4_ = f32[17,3,8,256]{3,2,1,0:T(8,128)} collective-permute-done((f32[17,3,8,256]{3,2,1,0:T(8,128)S(1)}, f32[17,3,8,256]{3,2,1,0:T(8,128)}, u32[]{:S(2)}, u32[]{:S(2)}) %collective-permute-start.5) | collective-permute-done | bytes 417824 | tf_op jit(solution)/shard_map/ppermute | solution.py:688
  24.5 0.1 broadcast_in_dim.2.refs_0_
  24.6 7.6 %step.3 = (f32[496,256]{1,0:T(8,128)}, f32[496,256]{1,0:T(8,128)}, f32[496,256]{1,0:T(8,128)}, f32[496,256]{1,0:T(8,128)}, f32[4,16,8,384]{3,2,1,0:T(8,128)S(1)}...) custom-call(f32[16,384]{1,0:T(8,128)S(1)} %broadcast_in_dim.2.refs_0_, ...), custom_call_target="tpu_custom_call" | custom-call | tf_op jit(solution)/shard_map/step/pallas_call | solution.py:583
  32.2 1.2 %collective-permute-done.7.refs_4_ = f32[17,3,8,256]{3,2,1,0:T(8,128)S(1)} collective-permute-done((f32[17,3,8,256]{3,2,1,0:T(8,128)S(1)}, f32[17,3,8,256]{3,2,1,0:T(8,128)S(1)}, u32[]{:S(2)}, u32[]{:S(2)}) %collective-permute-start.7) | collective-permute-done | bytes 417824 | tf_op jit(solution)/shard_map/ppermute | solution.py:688
  33.4 6.5 %step.4 = (f32[496,256]{1,0:T(8,128)}, f32[496,256]{1,0:T(8,128)}, f32[496,256]{1,0:T(8,128)}, f32[496,256]{1,0:T(8,128)}, f32[24,8,384]{2,1,0:T(8,128)S(1)}, /*index=5*/f32[2,8,8,384]{3,2,1,0:T(8,128)S(1)}) custom-call(f32[16,384]{1,0:T(8,128)S(1)} %broadcast_in_dim.2.refs_0_, ...), custom_call_target="tpu_custom_call", output_to_operand_aliasing={{0}: (8, {}), {1}: (9, {}), {2}: (10, {}), {3}: (11, {})} | custom-call | tf_op jit(solution)/shard_map/step/pallas_call | solution.py:583
  39.9 5.6 %step.5 = (f32[496,256]{1,0:T(8,128)}, f32[496,256]{1,0:T(8,128)}, f32[496,256]{1,0:T(8,128)}, f32[496,256]{1,0:T(8,128)}, f32[2,4,384]{2,1,0:T(4,128)S(1)}, /*index=5*/f32[2,4,384]{2,1,0:T(4,128)S(1)}) custom-call(f32[16,384]{1,0:T(8,128)S(1)} %broadcast_in_dim.2.refs_0_, ...), custom_call_target="tpu_custom_call", output_to_operand_aliasing={{0}: (8, {}), {1}: (9, {}), {2}: (10, {}), {3}: (11, {})} | custom-call | tf_op jit(solution)/shard_map/step/pallas_call | solution.py:583
  45.4 2.3 %collective-permute-start.8 = (f32[2,4,384]{2,1,0:T(4,128)S(1)}, f32[2,4,384]{2,1,0:T(4,128)S(1)}, u32[]{:S(2)}, u32[]{:S(2)}) collective-permute-start(f32[2,4,384]{2,1,0:T(4,128)S(1)} %get-tuple-element.85.own_a), channel_id=1, source_target_pairs={{8,16},{16,8},{9,17},{17,9},{10,18},{18,10},{11,19},{19,11},{12,20... | collective-permute-start | bytes 36872 | tf_op jit(solution)/shard_map/ppermute | solution.py:688
  47.8 0.1 collective-permute-start.9
  47.9 0.2 prepare.1.ready
  48.1 3.0 %collective-permute-done.8.met_a = f32[2,4,384]{2,1,0:T(4,128)S(1)} collective-permute-done((f32[2,4,384]{2,1,0:T(4,128)S(1)}, f32[2,4,384]{2,1,0:T(4,128)S(1)}, u32[]{:S(2)}, u32[]{:S(2)}) %collective-permute-start.8) | collective-permute-done | bytes 12320 | tf_op jit(solution)/shard_map/ppermute | solution.py:688
  51.0 0.5 %collective-permute-done.9.met_b = f32[2,4,384]{2,1,0:T(4,128)S(1)} collective-permute-done((f32[2,4,384]{2,1,0:T(4,128)S(1)}, f32[2,4,384]{2,1,0:T(4,128)S(1)}, u32[]{:S(2)}, u32[]{:S(2)}) %collective-permute-start.9) | collective-permute-done | bytes 12320 | tf_op jit(solution)/shard_map/ppermute | solution.py:688
  51.6 1.0 %solve.1 = f32[8,256]{1,0:T(8,128)} custom-call(f32[10,16,384]{2,1,0:T(8,128)S(1)} %prepare.1.ready, f32[2,4,384]{2,1,0:T(4,128)S(1)} %collective-permute-done.8.met_a, f32[2,4,384]{2,1,0:T(4,128)S(1)} %get-tuple-element.85.own_a, f32[2,4,384]{2,1,0:T(4,128)S(1)} %get-tuple-element.86.own_b, f32[2,4,384]{2,1,0:T(4,128)S(1)} %collective-permute-done.9.met_b), custom_call_target="tpu_custom_call" | custom-call | tf_op jit(solution)/shard_map/solve/pallas_call | solution.py:721
  (6 shorter events, 0.1 us)
Async XLA Ops:
  3.0 2.1 %collective-permute-start = (f32[2,8,8,128]{3,2,1,0:T(8,128)S(1)}, f32[2,8,8,128]{3,2,1,0:T(8,128)S(1)}, u32[]{:S(2)}, u32[]{:S(2)}) collective-permute-start(f32[2,8,8,128]{3,2,1,0:T(8,128)S(1)} %get-tuple-element.46), channel_id=1, source_target_pairs={{0,1},{1,0},{2,3},{3,2},{4,5},{5,4},{6,7},{7,6},{8,9},{9,8},{10,11... | collective-permute-start | bytes 196616 | tf_op jit(solution)/shard_map/ppermute | solution.py:683
  3.1 5.0 %collective-permute-start.1 = (f32[2,8,8,128]{3,2,1,0:T(8,128)S(1)}, f32[2,8,8,128]{3,2,1,0:T(8,128)S(1)}, u32[]{:S(2)}, u32[]{:S(2)}) collective-permute-start(f32[2,8,8,128]{3,2,1,0:T(8,128)S(1)} %get-tuple-element.47), channel_id=1, source_target_pairs={{1,2},{2,1},{3,4},{4,3},{5,6},{6,5},{7,0},{0,7},{9,10},{10,9},{11,... | collective-permute-start | bytes 196616 | tf_op jit(solution)/shard_map/ppermute | solution.py:684
  8.3 14.5 %collective-permute-start.4 = (f32[17,3,8,256]{3,2,1,0:T(8,128)S(1)}, f32[17,3,8,256]{3,2,1,0:T(8,128)S(1)}, u32[]{:S(2)}, u32[]{:S(2)}) collective-permute-start(f32[17,3,8,256]{3,2,1,0:T(8,128)S(1)} %get-tuple-element.58.refs_2_), channel_id=1, source_target_pairs={{8,16},{16,8},{9,17},{17,9},{10,18},{18,10},{11,19},{19,11},{12,20... | collective-permute-start | bytes 1253384 | tf_op jit(solution)/shard_map/ppermute | solution.py:688
  11.8 12.8 %collective-permute-start.5 = (f32[17,3,8,256]{3,2,1,0:T(8,128)S(1)}, f32[17,3,8,256]{3,2,1,0:T(8,128)}, u32[]{:S(2)}, u32[]{:S(2)}) collective-permute-start(f32[17,3,8,256]{3,2,1,0:T(8,128)S(1)} %get-tuple-element.59.refs_3_), channel_id=1, source_target_pairs={{0,8},{8,0},{16,24},{24,16},{1,9},{9,1},{17,25},{25,17},{2,10},{10... | collective-permute-start | bytes 1253384 | tf_op jit(solution)/shard_map/ppermute | solution.py:688
  11.8 20.3 %collective-permute-start.6 = (f32[17,3,8,256]{3,2,1,0:T(8,128)S(1)}, f32[17,3,8,256]{3,2,1,0:T(8,128)S(1)}, u32[]{:S(2)}, u32[]{:S(2)}) collective-permute-start(f32[17,3,8,256]{3,2,1,0:T(8,128)S(1)} %get-tuple-element.61.refs_2_), channel_id=1, source_target_pairs={{8,16},{16,8},{9,17},{17,9},{10,18},{18,10},{11,19},{19,11},{12,20... | collective-permute-start | bytes 1253384 | tf_op jit(solution)/shard_map/ppermute | solution.py:688
  14.2 19.2 %collective-permute-start.7 = (f32[17,3,8,256]{3,2,1,0:T(8,128)S(1)}, f32[17,3,8,256]{3,2,1,0:T(8,128)S(1)}, u32[]{:S(2)}, u32[]{:S(2)}) collective-permute-start(f32[17,3,8,256]{3,2,1,0:T(8,128)S(1)} %get-tuple-element.62.refs_3_), channel_id=1, source_target_pairs={{0,8},{8,0},{16,24},{24,16},{1,9},{9,1},{17,25},{25,17},{2,10},{10... | collective-permute-start | bytes 1253384 | tf_op jit(solution)/shard_map/ppermute | solution.py:688
  14.6 25.3 %collective-permute-start.2 = (f32[17,2,8,256]{3,2,1,0:T(8,128)S(1)}, f32[17,2,8,256]{3,2,1,0:T(8,128)}, u32[]{:S(2)}, u32[]{:S(2)}) collective-permute-start(f32[17,2,8,256]{3,2,1,0:T(8,128)S(1)} %get-tuple-element.56.refs_2_), channel_id=1, source_target_pairs={{8,16},{16,8},{9,17},{17,9},{10,18},{18,10},{11,19},{19,11},{12,20... | collective-permute-start | bytes 835592 | tf_op jit(solution)/shard_map/ppermute | solution.py:688
  22.7 17.1 %collective-permute-start.3 = (f32[17,2,8,256]{3,2,1,0:T(8,128)S(1)}, f32[17,2,8,256]{3,2,1,0:T(8,128)}, u32[]{:S(2)}, u32[]{:S(2)}) collective-permute-start(f32[17,2,8,256]{3,2,1,0:T(8,128)S(1)} %get-tuple-element.57.refs_3_), channel_id=1, source_target_pairs={{0,8},{8,0},{16,24},{24,16},{1,9},{9,1},{17,25},{25,17},{2,10},{10... | collective-permute-start | bytes 835592 | tf_op jit(solution)/shard_map/ppermute | solution.py:688
  45.4 5.6 %collective-permute-start.8 = (f32[2,4,384]{2,1,0:T(4,128)S(1)}, f32[2,4,384]{2,1,0:T(4,128)S(1)}, u32[]{:S(2)}, u32[]{:S(2)}) collective-permute-start(f32[2,4,384]{2,1,0:T(4,128)S(1)} %get-tuple-element.85.own_a), channel_id=1, source_target_pairs={{8,16},{16,8},{9,17},{17,9},{10,18},{18,10},{11,19},{19,11},{12,20... | collective-permute-start | bytes 36872 | tf_op jit(solution)/shard_map/ppermute | solution.py:688
  47.8 3.8 %collective-permute-start.9 = (f32[2,4,384]{2,1,0:T(4,128)S(1)}, f32[2,4,384]{2,1,0:T(4,128)S(1)}, u32[]{:S(2)}, u32[]{:S(2)}) collective-permute-start(f32[2,4,384]{2,1,0:T(4,128)S(1)} %get-tuple-element.86.own_b), channel_id=1, source_target_pairs={{0,8},{8,0},{16,24},{24,16},{1,9},{9,1},{17,25},{25,17},{2,10},{10... | collective-permute-start | bytes 36872 | tf_op jit(solution)/shard_map/ppermute | solution.py:688

commit v5 on v3

--- a/solution.py
+++ b/solution.py
@@ -64,7 +64,7 @@
 
 
 def parities():
-    return 1 - (lax.axis_index("by") & 1), lax.axis_index("bx") & 1
+    return lax.axis_index("by") & 1, lax.axis_index("bx") & 1
 
 
 def first_rows():
@@ -92,47 +92,43 @@
             copy(f, lane).start()
     for item in small:
         item.start()
+    across_a[...] = jnp.zeros(across_a.shape, F32)
+    across_b[...] = jnp.zeros(across_b.shape, F32)
     for item in small:
         item.wait()
     lines[0] = depth[...].astype(F32)
+    lanes = lax.broadcasted_iota(jnp.int32, (SUB, LANES), 1)
+    odd = jnp.broadcast_to(parities()[1], (SUB, LANES)) == 1
+    tiles = [(c, t) for c in range(len(CHUNKS)) for t in range(CHUNKS[c])]
     for f in range(FIELDS):
         for lane in range(2):
             copy(f, lane).wait()
-
-    used = SUB - EXTRA
-    for f in range(FIELDS):
         for group in range(2):
             for q in range(RIM):
                 place_tile(mixed.at[f, group, q], held, lines, rows, group, f, q, 0, CHUNKS[0] - 1)
-
-    lanes = lax.broadcasted_iota(jnp.int32, (SUB, LANES), 1)
-    odd = jnp.broadcast_to(parities()[1], (SUB, LANES)) == 1
-    slot = 0
-    for c in range(len(CHUNKS)):
-        for t in range(CHUNKS[c]):
+        for slot, (c, t) in enumerate(tiles):
             base = (first_level(c) + SUB * t) * rows
             for group in range(2):
-                west = jnp.zeros((SUB, LANES), F32)
-                east = jnp.zeros((SUB, LANES), F32)
+                west, east = across_a[group, slot], across_b[group, slot]
                 for q in range(RIM):
-                    for f in range(FIELDS):
-                        place = (q * FIELDS + f) * EDGE
-                        other = (place - EDGE) % LANES
-                        if c == 0 and t == CHUNKS[0] - 1:
-                            low = mixed[f, group, q, :, pl.ds(0, LANES)]
-                            high = mixed[f, group, q, :, pl.ds(LANES, LANES)]
-                        else:
-                            row = pl.ds(base + first_rows()[group] + q, SUB, stride=rows)
-                            low = held[f, 0, row, :]
-                            high = held[f, 1, row, :]
-                        if place:
-                            low = pltpu.roll(low, place, 1)
-                            high = pltpu.roll(high, place, 1)
-                        west = jnp.where((lanes >= place) & (lanes < place + EDGE), low, west)
-                        east = jnp.where((lanes >= other) & (lanes < other + EDGE), high, east)
-                across_a[group, slot] = jnp.where(odd, west, east)
-                across_b[group, slot] = jnp.where(odd, east, west)
-            slot += 1
+                    place = (q * FIELDS + f) * EDGE
+                    other = (place - EDGE) % LANES
+                    if c == 0 and t == CHUNKS[0] - 1:
+                        low = mixed[f, group, q, :, pl.ds(0, LANES)]
+                        high = mixed[f, group, q, :, pl.ds(LANES, LANES)]
+                    else:
+                        row = pl.ds(base + first_rows()[group] + q, SUB, stride=rows)
+                        low = held[f, 0, row, :]
+                        high = held[f, 1, row, :]
+                    if place:
+                        low = pltpu.roll(low, place, 1)
+                        high = pltpu.roll(high, place, 1)
+                    west = jnp.where((lanes >= place) & (lanes < place + EDGE), low, west)
+                    east = jnp.where((lanes >= other) & (lanes < other + EDGE), high, east)
+                if f == FIELDS - 1:
+                    west, east = jnp.where(odd, west, east), jnp.where(odd, east, west)
+                across_a[group, slot] = west
+                across_b[group, slot] = east
 
 
 def place_tile(ref, held, lines, rows, group, f, q, chunk, t):
@@ -151,14 +147,18 @@
         ref[pl.ds(used + extra, 1), :] = line
 
 
-def halves_kernel(rows, held, lines, *halves):
-    for c in range(len(CHUNKS)):
+def halves_kernel(rows, chunks, held, lines, across_a, across_b, *halves):
+    for k, c in enumerate(chunks):
         for t in range(CHUNKS[c]):
-            for f in range(FIELDS):
-                for group in range(2):
+            slot = sum(CHUNKS[:c]) + t
+            for group in range(2):
+                half = halves[2 * k + group]
+                for f in range(FIELDS):
                     for q in range(RIM):
-                        ref = halves[2 * c + group].at[f * RIM + q, t]
+                        ref = half.at[f * RIM + q, t]
                         place_tile(ref, held, lines, rows, group, f, q, c, t)
+                half[FIELDS * RIM, t, :, pl.ds(0, LANES)] = across_a[group, slot]
+                half[FIELDS * RIM, t, :, pl.ds(LANES, LANES)] = across_b[group, slot]
 
 
 def pack_edges(fields, wind, surface, depth):
@@ -189,57 +189,22 @@
     )(*arguments)
 
 
-def pack_halves(rows, held, lines):
+def pack_halves(rows, chunks, held, lines, across_a, across_b):
     vmem = pl.BlockSpec(memory_space=pltpu.VMEM)
     shapes = [
-        jax.ShapeDtypeStruct((FIELDS * RIM + 1, tiles, SUB, lines.shape[-1]), F32)
-        for tiles in CHUNKS
+        jax.ShapeDtypeStruct((FIELDS * RIM + 1, CHUNKS[c], SUB, lines.shape[-1]), F32)
+        for c in chunks
         for _ in range(2)
     ]
-    return pl.pallas_call(
-        functools.partial(halves_kernel, rows),
+    outs = pl.pallas_call(
+        functools.partial(halves_kernel, rows, chunks),
         out_shape=shapes,
-        in_specs=[vmem] * 2,
+        in_specs=[vmem] * 4,
         out_specs=[vmem] * len(shapes),
-        compiler_params=pltpu.CompilerParams(vmem_limit_bytes=PACK_VMEM),
+        compiler_params=pltpu.CompilerParams(vmem_limit_bytes=SMALL_VMEM),
         name="halves",
-    )(held, lines)
-
-
-def rims_kernel(across_a, across_b, *refs):
-    count = 2 * len(CHUNKS)
-    halves, sems = refs[count : 2 * count], refs[2 * count]
-    copies = []
-    for k, half in enumerate(halves):
-        slots = pl.ds(sum(CHUNKS[: k // 2]), CHUNKS[k // 2])
-        for lane, across in enumerate((across_a, across_b)):
-            copies.append(
-                pltpu.make_async_copy(
-                    across.at[k % 2, slots],
-                    half.at[FIELDS * RIM, :, :, pl.ds(lane * LANES, LANES)],
-                    sems.at[k, lane],
-                )
-            )
-    for copy in copies:
-        copy.start()
-    for copy in copies:
-        copy.wait()
-
-
-def put_rims(halves, across_a, across_b):
-    count = len(halves)
-    anywhere = pl.BlockSpec(memory_space=pl.ANY)
-    outs = pl.pallas_call(
-        rims_kernel,
-        out_shape=[jax.ShapeDtypeStruct(item.shape, F32) for item in halves],
-        in_specs=[anywhere] * (count + 2),
-        out_specs=[anywhere] * count,
-        scratch_shapes=[pltpu.SemaphoreType.DMA((count, 2))],
-        input_output_aliases={2 + k: k for k in range(count)},
-        compiler_params=pltpu.CompilerParams(vmem_limit_bytes=SMALL_VMEM),
-        name="rims",
-    )(across_a, across_b, *halves)
-    return [list(outs[k : k + 2]) for k in range(0, count, 2)]
+    )(held, lines, across_a, across_b)
+    return [list(outs[k : k + 2]) for k in range(0, len(outs), 2)]
 
 
 def east_of(value):
@@ -264,7 +229,7 @@
         return taken
 
     (rotate,) = take(1)
-    met_a, own_a, own_b, met_b = blocks = take(4)
+    blocks = take(4)
     if not first:
         deeps_in, carry_in, sums_in = take(3)
         take(FIELDS)
@@ -294,7 +259,7 @@
         sums[...] = sums_in[...]
 
     lanes = lax.broadcasted_iota(jnp.int32, (SUB, LANES), 1)
-    own = own_a.shape[-1]
+    own = blocks[0].shape[-1]
     wide = own + LANES
     every = range(FIELDS)
     odd_y, odd_x = parities()
@@ -667,7 +632,7 @@
     levels, rows, columns = eastward_flow.shape
     assert rows == 2 * RIM and columns == 2 * LANES and levels + EXTRA == SUB * sum(CHUNKS)
     along_y, along_x = lax.axis_size("by"), lax.axis_size("bx")
-    pairs_y = (swaps(along_y, 1, False), swaps(along_y, 0, False))
+    pairs_y = (swaps(along_y, 0, False), swaps(along_y, 1, False))
     pairs_x = (swaps(along_x, 0, True), swaps(along_x, 1, True))
     row_index = lax.axis_index("by") * rows - RIM + jnp.arange(rows + 2 * RIM)
     rotate = 1.2 * jnp.sin(
@@ -679,10 +644,11 @@
     edge_a, edge_b, held, lines = pack_edges(
         fields, air_stress_forcing, earlier_sea_height_load, ocean_layer_depths
     )
-    halves = pack_halves(rows, held, lines)
     across_a = lax.ppermute(edge_a, "bx", pairs_x[0])
     across_b = lax.ppermute(edge_b, "bx", pairs_x[1])
-    halves = put_rims(halves, across_a, across_b)
+    made = (held, lines, across_a, across_b)
+    halves = pack_halves(rows, (0,), *made)
+    halves += pack_halves(rows, tuple(range(1, len(CHUNKS))), *made)
 
     def send(own):
         return [lax.ppermute(item, "by", pairs) for item, pairs in zip(own, pairs_y)]
@@ -692,7 +658,7 @@
     for chunk in range(len(CHUNKS)):
         own_a, own_b = halves[chunk]
         met_a, met_b = rims[chunk]
-        blocks = (met_a, own_a, own_b, met_b)
+        blocks = [met_a, own_a, own_b, met_b]
         outs = step(chunk, rows, levels, columns, rotate, blocks, kept, news)
         news, rest = outs[:FIELDS], outs[FIELDS:]
         if chunk == 0:

time: 51.6 us -> 50.4 us (0.977); the launches traced: 50.7 us -> 50.1 us
  waiting for transfers between devices: 10.2 us -> 7.04 us
  starting transfers between devices: 17 us -> 19.8 us
    ppermute x10, waiting for transfers between devices: 7.22 us -> 3.56 us  [send(): lax.ppermute(item, 'by', pairs)]
    ppermute x10, starting transfers between devices: 15.3 us -> 18.2 us  [send(): lax.ppermute(item, 'by', pairs)]
  transfers between devices with their start and end apart: 12 -> 12, of which waited for: 6 -> 4; matrix products, arithmetic and copies ran while one was open for 0% -> 0% of each run, Pallas kernels for 28% -> 29%
where the time goes in v5:
time: 50.4 us; the launch traced here: 50.1 us
  Pallas kernels  22.3 us (44%)
  starting transfers between devices  19.8 us (39%)
  waiting for transfers between devices  7.04 us (14%)
  between operations  0.83 us (2%)
    pallas_call x4, Pallas kernels, step(): pl.pallas_call(functools.partial(step_kernel, chunk, rows), out_shape=sha...  18.4 us
    ppermute x10, starting transfers between devices, send(): lax.ppermute(item, 'by', pairs)  18.2 us
    ppermute x10, waiting for transfers between devices, send(): lax.ppermute(item, 'by', pairs)  3.56 us
    ppermute x1, waiting for transfers between devices, body(): across_b = lax.ppermute(edge_b, 'bx', pairs_x[1])  3.47 us
    pallas_call x1, Pallas kernels, pack_edges(): pl.pallas_call(functools.partial(edges_kernel, rows), out_shape=[jax.Shap...  2.36 us
    ppermute x1, starting transfers between devices, body(): across_b = lax.ppermute(edge_b, 'bx', pairs_x[1])  1.54 us
  transfers between devices with their start and end apart: 12, of which 4 were waited for; matrix products, arithmetic and copies ran while one was open for 0% of the time, Pallas kernels for 29%

profile of v5, /device:TPU:12, one launch (start us, length us, event | category | flops | bytes accessed | tf_op | source)
XLA Modules:
  0.0 50.1 jit_solution(15677714318282038339)
XLA Ops:
  0.6 2.4 %edges.1 = (f32[2,8,8,128]{3,2,1,0:T(8,128)S(1)}, f32[2,8,8,128]{3,2,1,0:T(8,128)S(1)}, f32[4,2,496,128]{3,2,1,0:T(8,128)S(1)}, f32[4,8,256]{2,1,0:T(8,128)S(1)}) custom-call(f32[496,256]{1,0:T(8,128)} %bitcast.12, f32[496,256]{1,0:T(8,128)} %bitcast.13, f32[496,256]{1,0:T(8,128)} %bitcast.14, f32[496,256]{1,0:T(8,128)} %bitcast.15, f32[2,8,256]{2,1,0:T(8,128)} %refs_4_.1, ...), custom_call_target="tpu_custom_call" | custom-call | tf_op jit(solution)/shard_map/edges/pallas_call | solution.py:172
  3.0 0.1 collective-permute-start
  3.1 1.5 %collective-permute-start.1 = (f32[2,8,8,128]{3,2,1,0:T(8,128)S(1)}, f32[2,8,8,128]{3,2,1,0:T(8,128)S(1)}, u32[]{:S(2)}, u32[]{:S(2)}) collective-permute-start(f32[2,8,8,128]{3,2,1,0:T(8,128)S(1)} %get-tuple-element.55), channel_id=1, source_target_pairs={{1,2},{2,1},{3,4},{4,3},{5,6},{6,5},{7,0},{0,7},{9,10},{10,9},{11,... | collective-permute-start | bytes 196616 | tf_op jit(solution)/shard_map/ppermute | solution.py:648
  4.6 3.5 %collective-permute-done.1.across_b = f32[2,8,8,128]{3,2,1,0:T(8,128)S(1)} collective-permute-done((f32[2,8,8,128]{3,2,1,0:T(8,128)S(1)}, f32[2,8,8,128]{3,2,1,0:T(8,128)S(1)}, u32[]{:S(2)}, u32[]{:S(2)}) %collective-permute-start.1) | collective-permute-done | bytes 65568 | tf_op jit(solution)/shard_map/ppermute | solution.py:648
  8.1 0.1 halves.3
  8.2 0.2 collective-permute-start.2
  8.4 5.0 %collective-permute-start.3 = (f32[17,2,8,256]{3,2,1,0:T(8,128)S(1)}, f32[17,2,8,256]{3,2,1,0:T(8,128)S(1)}, u32[]{:S(2)}, u32[]{:S(2)}) collective-permute-start(f32[17,2,8,256]{3,2,1,0:T(8,128)S(1)} %get-tuple-element.59.refs_3_), channel_id=1, source_target_pairs={{8,16},{16,8},{9,17},{17,9},{10,18},{18,10},{11,19},{19,11},{12,20... | collective-permute-start | bytes 835592 | tf_op jit(solution)/shard_map/ppermute | solution.py:654
  13.4 0.3 halves.2
  13.7 0.1 collective-permute-start.8
  13.8 1.9 %collective-permute-start.9 = (f32[17,2,8,256]{3,2,1,0:T(8,128)S(1)}, f32[17,2,8,256]{3,2,1,0:T(8,128)S(1)}, u32[]{:S(2)}, u32[]{:S(2)}) collective-permute-start(f32[17,2,8,256]{3,2,1,0:T(8,128)S(1)} %get-tuple-element.68.refs_3_), channel_id=1, source_target_pairs={{8,16},{16,8},{9,17},{17,9},{10,18},{18,10},{11,19},{19,11},{12,20... | collective-permute-start | bytes 835592 | tf_op jit(solution)/shard_map/ppermute | solution.py:654
  15.7 0.8 %collective-permute-start.6 = (f32[17,2,8,256]{3,2,1,0:T(8,128)S(1)}, f32[17,2,8,256]{3,2,1,0:T(8,128)S(1)}, u32[]{:S(2)}, u32[]{:S(2)}) collective-permute-start(f32[17,2,8,256]{3,2,1,0:T(8,128)S(1)} %get-tuple-element.65.refs_2_), channel_id=1, source_target_pairs={{0,8},{8,0},{16,24},{24,16},{1,9},{9,1},{17,25},{25,17},{2,10},{10... | collective-permute-start | bytes 835592 | tf_op jit(solution)/shard_map/ppermute | solution.py:654
  16.6 0.8 %collective-permute-done.2.refs_1_ = f32[17,2,8,256]{3,2,1,0:T(8,128)S(1)} collective-permute-done((f32[17,2,8,256]{3,2,1,0:T(8,128)S(1)}, f32[17,2,8,256]{3,2,1,0:T(8,128)S(1)}, u32[]{:S(2)}, u32[]{:S(2)}) %collective-permute-start.2) | collective-permute-done | bytes 278560 | tf_op jit(solution)/shard_map/ppermute | solution.py:654
  17.4 4.0 %collective-permute-start.7 = (f32[17,2,8,256]{3,2,1,0:T(8,128)S(1)}, f32[17,2,8,256]{3,2,1,0:T(8,128)S(1)}, u32[]{:S(2)}, u32[]{:S(2)}) collective-permute-start(f32[17,2,8,256]{3,2,1,0:T(8,128)S(1)} %get-tuple-element.66.refs_3_), channel_id=1, source_target_pairs={{8,16},{16,8},{9,17},{17,9},{10,18},{18,10},{11,19},{19,11},{12,20... | collective-permute-start | bytes 835592 | tf_op jit(solution)/shard_map/ppermute | solution.py:654
  21.4 0.1 broadcast_in_dim.2.refs_0_
  21.5 4.7 %step.4 = (f32[496,256]{1,0:T(8,128)}, f32[496,256]{1,0:T(8,128)}, f32[496,256]{1,0:T(8,128)}, f32[496,256]{1,0:T(8,128)}, f32[4,16,8,384]{3,2,1,0:T(8,128)S(1)}...) custom-call(f32[16,384]{1,0:T(8,128)S(1)} %broadcast_in_dim.2.refs_0_, ...), custom_call_target="tpu_custom_call" | custom-call | tf_op jit(solution)/shard_map/step/pallas_call | solution.py:548
  26.2 3.5 %collective-permute-start.5 = (f32[17,2,8,256]{3,2,1,0:T(8,128)S(1)}, f32[17,2,8,256]{3,2,1,0:T(8,128)S(1)}, u32[]{:S(2)}, u32[]{:S(2)}) collective-permute-start(f32[17,2,8,256]{3,2,1,0:T(8,128)S(1)} %get-tuple-element.63.refs_3_), channel_id=1, source_target_pairs={{8,16},{16,8},{9,17},{17,9},{10,18},{18,10},{11,19},{19,11},{12,20... | collective-permute-start | bytes 835592 | tf_op jit(solution)/shard_map/ppermute | solution.py:654
  29.7 4.6 %step.5 = (f32[496,256]{1,0:T(8,128)}, f32[496,256]{1,0:T(8,128)}, f32[496,256]{1,0:T(8,128)}, f32[496,256]{1,0:T(8,128)}, f32[24,8,384]{2,1,0:T(8,128)S(1)}, /*index=5*/f32[2,8,8,384]{3,2,1,0:T(8,128)S(1)}) custom-call(f32[16,384]{1,0:T(8,128)S(1)} %broadcast_in_dim.2.refs_0_, ...), custom_call_target="tpu_custom_call", output_to_operand_aliasing={{0}: (8, {}), {1}: (9, {}), {2}: (10, {}), {3}: (11, {})} | custom-call | tf_op jit(solution)/shard_map/step/pallas_call | solution.py:548
  34.3 4.6 %step.6 = (f32[496,256]{1,0:T(8,128)}, f32[496,256]{1,0:T(8,128)}, f32[496,256]{1,0:T(8,128)}, f32[496,256]{1,0:T(8,128)}, f32[24,8,384]{2,1,0:T(8,128)S(1)}, /*index=5*/f32[2,8,8,384]{3,2,1,0:T(8,128)S(1)}) custom-call(f32[16,384]{1,0:T(8,128)S(1)} %broadcast_in_dim.2.refs_0_, ...), custom_call_target="tpu_custom_call", output_to_operand_aliasing={{0}: (8, {}), {1}: (9, {}), {2}: (10, {}), {3}: (11, {})} | custom-call | tf_op jit(solution)/shard_map/step/pallas_call | solution.py:548
  38.9 4.5 %step.7 = (f32[496,256]{1,0:T(8,128)}, f32[496,256]{1,0:T(8,128)}, f32[496,256]{1,0:T(8,128)}, f32[496,256]{1,0:T(8,128)}, f32[2,4,384]{2,1,0:T(4,128)S(1)}, /*index=5*/f32[2,4,384]{2,1,0:T(4,128)S(1)}) custom-call(f32[16,384]{1,0:T(8,128)S(1)} %broadcast_in_dim.2.refs_0_, ...), custom_call_target="tpu_custom_call", output_to_operand_aliasing={{0}: (8, {}), {1}: (9, {}), {2}: (10, {}), {3}: (11, {})} | custom-call | tf_op jit(solution)/shard_map/step/pallas_call | solution.py:548
  43.5 2.6 %collective-permute-start.11 = (f32[2,4,384]{2,1,0:T(4,128)S(1)}, f32[2,4,384]{2,1,0:T(4,128)S(1)}, u32[]{:S(2)}, u32[]{:S(2)}) collective-permute-start(f32[2,4,384]{2,1,0:T(4,128)S(1)} %get-tuple-element.98.own_b), channel_id=1, source_target_pairs={{8,16},{16,8},{9,17},{17,9},{10,18},{18,10},{11,19},{19,11},{12,20... | collective-permute-start | bytes 36872 | tf_op jit(solution)/shard_map/ppermute | solution.py:654
  46.2 0.2 prepare.1.ready
  46.4 0.8 %collective-permute-done.10.met_a = f32[2,4,384]{2,1,0:T(4,128)S(1)} collective-permute-done((f32[2,4,384]{2,1,0:T(4,128)S(1)}, f32[2,4,384]{2,1,0:T(4,128)S(1)}, u32[]{:S(2)}, u32[]{:S(2)}) %collective-permute-start.10) | collective-permute-done | bytes 12320 | tf_op jit(solution)/shard_map/ppermute | solution.py:654
  47.2 1.9 %collective-permute-done.11.met_b = f32[2,4,384]{2,1,0:T(4,128)S(1)} collective-permute-done((f32[2,4,384]{2,1,0:T(4,128)S(1)}, f32[2,4,384]{2,1,0:T(4,128)S(1)}, u32[]{:S(2)}, u32[]{:S(2)}) %collective-permute-start.11) | collective-permute-done | bytes 12320 | tf_op jit(solution)/shard_map/ppermute | solution.py:654
  49.1 1.0 %solve.1 = f32[8,256]{1,0:T(8,128)} custom-call(f32[10,16,384]{2,1,0:T(8,128)S(1)} %prepare.1.ready, f32[2,4,384]{2,1,0:T(4,128)S(1)} %collective-permute-done.10.met_a, f32[2,4,384]{2,1,0:T(4,128)S(1)} %get-tuple-element.97.own_a, f32[2,4,384]{2,1,0:T(4,128)S(1)} %get-tuple-element.98.own_b, f32[2,4,384]{2,1,0:T(4,128)S(1)} %collective-permute-done.11.met_b), custom_call_target="tpu_custom_call" | custom-call | tf_op jit(solution)/shard_map/solve/pallas_call | solution.py:687
  (11 shorter events, 0.2 us)
Async XLA Ops:
  3.0 1.6 %collective-permute-start = (f32[2,8,8,128]{3,2,1,0:T(8,128)S(1)}, f32[2,8,8,128]{3,2,1,0:T(8,128)S(1)}, u32[]{:S(2)}, u32[]{:S(2)}) collective-permute-start(f32[2,8,8,128]{3,2,1,0:T(8,128)S(1)} %get-tuple-element.54), channel_id=1, source_target_pairs={{0,1},{1,0},{2,3},{3,2},{4,5},{5,4},{6,7},{7,6},{8,9},{9,8},{10,11... | collective-permute-start | bytes 196616 | tf_op jit(solution)/shard_map/ppermute | solution.py:647
  3.1 5.0 %collective-permute-start.1 = (f32[2,8,8,128]{3,2,1,0:T(8,128)S(1)}, f32[2,8,8,128]{3,2,1,0:T(8,128)S(1)}, u32[]{:S(2)}, u32[]{:S(2)}) collective-permute-start(f32[2,8,8,128]{3,2,1,0:T(8,128)S(1)} %get-tuple-element.55), channel_id=1, source_target_pairs={{1,2},{2,1},{3,4},{4,3},{5,6},{6,5},{7,0},{0,7},{9,10},{10,9},{11,... | collective-permute-start | bytes 196616 | tf_op jit(solution)/shard_map/ppermute | solution.py:648
  8.2 9.1 %collective-permute-start.2 = (f32[17,2,8,256]{3,2,1,0:T(8,128)S(1)}, f32[17,2,8,256]{3,2,1,0:T(8,128)S(1)}, u32[]{:S(2)}, u32[]{:S(2)}) collective-permute-start(f32[17,2,8,256]{3,2,1,0:T(8,128)S(1)} %get-tuple-element.58.refs_2_), channel_id=1, source_target_pairs={{0,8},{8,0},{16,24},{24,16},{1,9},{9,1},{17,25},{25,17},{2,10},{10... | collective-permute-start | bytes 835592 | tf_op jit(solution)/shard_map/ppermute | solution.py:654
  8.4 13.0 %collective-permute-start.3 = (f32[17,2,8,256]{3,2,1,0:T(8,128)S(1)}, f32[17,2,8,256]{3,2,1,0:T(8,128)S(1)}, u32[]{:S(2)}, u32[]{:S(2)}) collective-permute-start(f32[17,2,8,256]{3,2,1,0:T(8,128)S(1)} %get-tuple-element.59.refs_3_), channel_id=1, source_target_pairs={{8,16},{16,8},{9,17},{17,9},{10,18},{18,10},{11,19},{19,11},{12,20... | collective-permute-start | bytes 835592 | tf_op jit(solution)/shard_map/ppermute | solution.py:654
  13.7 12.6 %collective-permute-start.8 = (f32[17,2,8,256]{3,2,1,0:T(8,128)S(1)}, f32[17,2,8,256]{3,2,1,0:T(8,128)S(1)}, u32[]{:S(2)}, u32[]{:S(2)}) collective-permute-start(f32[17,2,8,256]{3,2,1,0:T(8,128)S(1)} %get-tuple-element.67.refs_2_), channel_id=1, source_target_pairs={{0,8},{8,0},{16,24},{24,16},{1,9},{9,1},{17,25},{25,17},{2,10},{10... | collective-permute-start | bytes 835592 | tf_op jit(solution)/shard_map/ppermute | solution.py:654
  13.8 15.9 %collective-permute-start.9 = (f32[17,2,8,256]{3,2,1,0:T(8,128)S(1)}, f32[17,2,8,256]{3,2,1,0:T(8,128)S(1)}, u32[]{:S(2)}, u32[]{:S(2)}) collective-permute-start(f32[17,2,8,256]{3,2,1,0:T(8,128)S(1)} %get-tuple-element.68.refs_3_), channel_id=1, source_target_pairs={{8,16},{16,8},{9,17},{17,9},{10,18},{18,10},{11,19},{19,11},{12,20... | collective-permute-start | bytes 835592 | tf_op jit(solution)/shard_map/ppermute | solution.py:654
  15.7 18.6 %collective-permute-start.6 = (f32[17,2,8,256]{3,2,1,0:T(8,128)S(1)}, f32[17,2,8,256]{3,2,1,0:T(8,128)S(1)}, u32[]{:S(2)}, u32[]{:S(2)}) collective-permute-start(f32[17,2,8,256]{3,2,1,0:T(8,128)S(1)} %get-tuple-element.65.refs_2_), channel_id=1, source_target_pairs={{0,8},{8,0},{16,24},{24,16},{1,9},{9,1},{17,25},{25,17},{2,10},{10... | collective-permute-start | bytes 835592 | tf_op jit(solution)/shard_map/ppermute | solution.py:654
  17.4 16.9 %collective-permute-start.7 = (f32[17,2,8,256]{3,2,1,0:T(8,128)S(1)}, f32[17,2,8,256]{3,2,1,0:T(8,128)S(1)}, u32[]{:S(2)}, u32[]{:S(2)}) collective-permute-start(f32[17,2,8,256]{3,2,1,0:T(8,128)S(1)} %get-tuple-element.66.refs_3_), channel_id=1, source_target_pairs={{8,16},{16,8},{9,17},{17,9},{10,18},{18,10},{11,19},{19,11},{12,20... | collective-permute-start | bytes 835592 | tf_op jit(solution)/shard_map/ppermute | solution.py:654
  26.1 12.7 %collective-permute-start.4 = (f32[17,2,8,256]{3,2,1,0:T(8,128)S(1)}, f32[17,2,8,256]{3,2,1,0:T(8,128)S(1)}, u32[]{:S(2)}, u32[]{:S(2)}) collective-permute-start(f32[17,2,8,256]{3,2,1,0:T(8,128)S(1)} %get-tuple-element.62.refs_2_), channel_id=1, source_target_pairs={{0,8},{8,0},{16,24},{24,16},{1,9},{9,1},{17,25},{25,17},{2,10},{10... | collective-permute-start | bytes 835592 | tf_op jit(solution)/shard_map/ppermute | solution.py:654
  26.2 12.7 %collective-permute-start.5 = (f32[17,2,8,256]{3,2,1,0:T(8,128)S(1)}, f32[17,2,8,256]{3,2,1,0:T(8,128)S(1)}, u32[]{:S(2)}, u32[]{:S(2)}) collective-permute-start(f32[17,2,8,256]{3,2,1,0:T(8,128)S(1)} %get-tuple-element.63.refs_3_), channel_id=1, source_target_pairs={{8,16},{16,8},{9,17},{17,9},{10,18},{18,10},{11,19},{19,11},{12,20... | collective-permute-start | bytes 835592 | tf_op jit(solution)/shard_map/ppermute | solution.py:654
  43.5 3.8 %collective-permute-start.10 = (f32[2,4,384]{2,1,0:T(4,128)S(1)}, f32[2,4,384]{2,1,0:T(4,128)S(1)}, u32[]{:S(2)}, u32[]{:S(2)}) collective-permute-start(f32[2,4,384]{2,1,0:T(4,128)S(1)} %get-tuple-element.97.own_a), channel_id=1, source_target_pairs={{0,8},{8,0},{16,24},{24,16},{1,9},{9,1},{17,25},{25,17},{2,10},{10... | collective-permute-start | bytes 36872 | tf_op jit(solution)/shard_map/ppermute | solution.py:654
  43.5 5.6 %collective-permute-start.11 = (f32[2,4,384]{2,1,0:T(4,128)S(1)}, f32[2,4,384]{2,1,0:T(4,128)S(1)}, u32[]{:S(2)}, u32[]{:S(2)}) collective-permute-start(f32[2,4,384]{2,1,0:T(4,128)S(1)} %get-tuple-element.98.own_b), channel_id=1, source_target_pairs={{8,16},{16,8},{9,17},{17,9},{10,18},{18,10},{11,19},{19,11},{12,20... | collective-permute-start | bytes 36872 | tf_op jit(solution)/shard_map/ppermute | solution.py:654

commit v6 on v5

--- a/solution.py
+++ b/solution.py
@@ -27,7 +27,7 @@
 CHUNKS = (2, 2, 2, 2)
 AHEAD = 3
 FAR = 1000000
-BATCH = 4
+BATCH = 7
 GROUPS = ((0,), (1,), (2,), (3,))
 SMALL_VMEM = 4 * 1024 * 1024
 PACK_VMEM = 8 * 1024 * 1024

time: 50.4 us -> 50.7 us (level)
  no operation moved by 1% of the time
where the time goes in v6:
time: 50.7 us; the launch traced here: 50.3 us
  Pallas kernels  22.5 us (44%)
  starting transfers between devices  19.8 us (39%)
  waiting for transfers between devices  7.04 us (14%)
  between operations  0.83 us (2%)
    pallas_call x4, Pallas kernels, step(): pl.pallas_call(functools.partial(step_kernel, chunk, rows), out_shape=sha...  18.6 us
    ppermute x10, starting transfers between devices, send(): lax.ppermute(item, 'by', pairs)  18.2 us
    ppermute x10, waiting for transfers between devices, send(): lax.ppermute(item, 'by', pairs)  3.56 us
    ppermute x1, waiting for transfers between devices, body(): across_b = lax.ppermute(edge_b, 'bx', pairs_x[1])  3.47 us
    pallas_call x1, Pallas kernels, pack_edges(): pl.pallas_call(functools.partial(edges_kernel, rows), out_shape=[jax.Shap...  2.36 us
    ppermute x1, starting transfers between devices, body(): across_b = lax.ppermute(edge_b, 'bx', pairs_x[1])  1.54 us
  transfers between devices with their start and end apart: 12, of which 4 were waited for; matrix products, arithmetic and copies ran while one was open for 0% of the time, Pallas kernels for 29%

profile of v6, /device:TPU:12, one launch (start us, length us, event | category | flops | bytes accessed | tf_op | source)
XLA Modules:
  0.0 50.3 jit_solution(4190472594076271271)
XLA Ops:
  0.6 2.4 %edges.1 = (f32[2,8,8,128]{3,2,1,0:T(8,128)S(1)}, f32[2,8,8,128]{3,2,1,0:T(8,128)S(1)}, f32[4,2,496,128]{3,2,1,0:T(8,128)S(1)}, f32[4,8,256]{2,1,0:T(8,128)S(1)}) custom-call(f32[496,256]{1,0:T(8,128)} %bitcast.12, f32[496,256]{1,0:T(8,128)} %bitcast.13, f32[496,256]{1,0:T(8,128)} %bitcast.14, f32[496,256]{1,0:T(8,128)} %bitcast.15, f32[2,8,256]{2,1,0:T(8,128)} %refs_4_.1, ...), custom_call_target="tpu_custom_call" | custom-call | tf_op jit(solution)/shard_map/edges/pallas_call | solution.py:172
  3.0 0.1 collective-permute-start
  3.1 1.5 %collective-permute-start.1 = (f32[2,8,8,128]{3,2,1,0:T(8,128)S(1)}, f32[2,8,8,128]{3,2,1,0:T(8,128)S(1)}, u32[]{:S(2)}, u32[]{:S(2)}) collective-permute-start(f32[2,8,8,128]{3,2,1,0:T(8,128)S(1)} %get-tuple-element.55), channel_id=1, source_target_pairs={{1,2},{2,1},{3,4},{4,3},{5,6},{6,5},{7,0},{0,7},{9,10},{10,9},{11,... | collective-permute-start | bytes 196616 | tf_op jit(solution)/shard_map/ppermute | solution.py:648
  4.6 3.5 %collective-permute-done.1.across_b = f32[2,8,8,128]{3,2,1,0:T(8,128)S(1)} collective-permute-done((f32[2,8,8,128]{3,2,1,0:T(8,128)S(1)}, f32[2,8,8,128]{3,2,1,0:T(8,128)S(1)}, u32[]{:S(2)}, u32[]{:S(2)}) %collective-permute-start.1) | collective-permute-done | bytes 65568 | tf_op jit(solution)/shard_map/ppermute | solution.py:648
  8.1 0.1 halves.3
  8.2 0.2 collective-permute-start.2
  8.4 5.0 %collective-permute-start.3 = (f32[17,2,8,256]{3,2,1,0:T(8,128)S(1)}, f32[17,2,8,256]{3,2,1,0:T(8,128)S(1)}, u32[]{:S(2)}, u32[]{:S(2)}) collective-permute-start(f32[17,2,8,256]{3,2,1,0:T(8,128)S(1)} %get-tuple-element.59.refs_3_), channel_id=1, source_target_pairs={{8,16},{16,8},{9,17},{17,9},{10,18},{18,10},{11,19},{19,11},{12,20... | collective-permute-start | bytes 835592 | tf_op jit(solution)/shard_map/ppermute | solution.py:654
  13.4 0.3 halves.2
  13.8 1.9 %collective-permute-start.9 = (f32[17,2,8,256]{3,2,1,0:T(8,128)S(1)}, f32[17,2,8,256]{3,2,1,0:T(8,128)S(1)}, u32[]{:S(2)}, u32[]{:S(2)}) collective-permute-start(f32[17,2,8,256]{3,2,1,0:T(8,128)S(1)} %get-tuple-element.68.refs_3_), channel_id=1, source_target_pairs={{8,16},{16,8},{9,17},{17,9},{10,18},{18,10},{11,19},{19,11},{12,20... | collective-permute-start | bytes 835592 | tf_op jit(solution)/shard_map/ppermute | solution.py:654
  15.7 0.8 %collective-permute-start.6 = (f32[17,2,8,256]{3,2,1,0:T(8,128)S(1)}, f32[17,2,8,256]{3,2,1,0:T(8,128)S(1)}, u32[]{:S(2)}, u32[]{:S(2)}) collective-permute-start(f32[17,2,8,256]{3,2,1,0:T(8,128)S(1)} %get-tuple-element.65.refs_2_), channel_id=1, source_target_pairs={{0,8},{8,0},{16,24},{24,16},{1,9},{9,1},{17,25},{25,17},{2,10},{10... | collective-permute-start | bytes 835592 | tf_op jit(solution)/shard_map/ppermute | solution.py:654
  16.6 0.8 %collective-permute-done.2.refs_1_ = f32[17,2,8,256]{3,2,1,0:T(8,128)S(1)} collective-permute-done((f32[17,2,8,256]{3,2,1,0:T(8,128)S(1)}, f32[17,2,8,256]{3,2,1,0:T(8,128)S(1)}, u32[]{:S(2)}, u32[]{:S(2)}) %collective-permute-start.2) | collective-permute-done | bytes 278560 | tf_op jit(solution)/shard_map/ppermute | solution.py:654
  17.4 4.0 %collective-permute-start.7 = (f32[17,2,8,256]{3,2,1,0:T(8,128)S(1)}, f32[17,2,8,256]{3,2,1,0:T(8,128)S(1)}, u32[]{:S(2)}, u32[]{:S(2)}) collective-permute-start(f32[17,2,8,256]{3,2,1,0:T(8,128)S(1)} %get-tuple-element.66.refs_3_), channel_id=1, source_target_pairs={{8,16},{16,8},{9,17},{17,9},{10,18},{18,10},{11,19},{19,11},{12,20... | collective-permute-start | bytes 835592 | tf_op jit(solution)/shard_map/ppermute | solution.py:654
  21.5 4.7 %step.4 = (f32[496,256]{1,0:T(8,128)}, f32[496,256]{1,0:T(8,128)}, f32[496,256]{1,0:T(8,128)}, f32[496,256]{1,0:T(8,128)}, f32[4,16,8,384]{3,2,1,0:T(8,128)S(1)}...) custom-call(f32[16,384]{1,0:T(8,128)S(1)} %broadcast_in_dim.2.refs_0_, ...), custom_call_target="tpu_custom_call" | custom-call | tf_op jit(solution)/shard_map/step/pallas_call | solution.py:548
  26.1 0.1 collective-permute-start.4
  26.2 3.5 %collective-permute-start.5 = (f32[17,2,8,256]{3,2,1,0:T(8,128)S(1)}, f32[17,2,8,256]{3,2,1,0:T(8,128)S(1)}, u32[]{:S(2)}, u32[]{:S(2)}) collective-permute-start(f32[17,2,8,256]{3,2,1,0:T(8,128)S(1)} %get-tuple-element.63.refs_3_), channel_id=1, source_target_pairs={{8,16},{16,8},{9,17},{17,9},{10,18},{18,10},{11,19},{19,11},{12,20... | collective-permute-start | bytes 835592 | tf_op jit(solution)/shard_map/ppermute | solution.py:654
  29.7 4.6 %step.5 = (f32[496,256]{1,0:T(8,128)}, f32[496,256]{1,0:T(8,128)}, f32[496,256]{1,0:T(8,128)}, f32[496,256]{1,0:T(8,128)}, f32[24,8,384]{2,1,0:T(8,128)S(1)}, /*index=5*/f32[2,8,8,384]{3,2,1,0:T(8,128)S(1)}) custom-call(f32[16,384]{1,0:T(8,128)S(1)} %broadcast_in_dim.2.refs_0_, ...), custom_call_target="tpu_custom_call", output_to_operand_aliasing={{0}: (8, {}), {1}: (9, {}), {2}: (10, {}), {3}: (11, {})} | custom-call | tf_op jit(solution)/shard_map/step/pallas_call | solution.py:548
  34.4 4.6 %step.6 = (f32[496,256]{1,0:T(8,128)}, f32[496,256]{1,0:T(8,128)}, f32[496,256]{1,0:T(8,128)}, f32[496,256]{1,0:T(8,128)}, f32[24,8,384]{2,1,0:T(8,128)S(1)}, /*index=5*/f32[2,8,8,384]{3,2,1,0:T(8,128)S(1)}) custom-call(f32[16,384]{1,0:T(8,128)S(1)} %broadcast_in_dim.2.refs_0_, ...), custom_call_target="tpu_custom_call", output_to_operand_aliasing={{0}: (8, {}), {1}: (9, {}), {2}: (10, {}), {3}: (11, {})} | custom-call | tf_op jit(solution)/shard_map/step/pallas_call | solution.py:548
  39.0 4.6 %step.7 = (f32[496,256]{1,0:T(8,128)}, f32[496,256]{1,0:T(8,128)}, f32[496,256]{1,0:T(8,128)}, f32[496,256]{1,0:T(8,128)}, f32[2,4,384]{2,1,0:T(4,128)S(1)}, /*index=5*/f32[2,4,384]{2,1,0:T(4,128)S(1)}) custom-call(f32[16,384]{1,0:T(8,128)S(1)} %broadcast_in_dim.2.refs_0_, ...), custom_call_target="tpu_custom_call", output_to_operand_aliasing={{0}: (8, {}), {1}: (9, {}), {2}: (10, {}), {3}: (11, {})} | custom-call | tf_op jit(solution)/shard_map/step/pallas_call | solution.py:548
  43.7 0.1 collective-permute-start.10
  43.7 2.6 %collective-permute-start.11 = (f32[2,4,384]{2,1,0:T(4,128)S(1)}, f32[2,4,384]{2,1,0:T(4,128)S(1)}, u32[]{:S(2)}, u32[]{:S(2)}) collective-permute-start(f32[2,4,384]{2,1,0:T(4,128)S(1)} %get-tuple-element.98.own_b), channel_id=1, source_target_pairs={{8,16},{16,8},{9,17},{17,9},{10,18},{18,10},{11,19},{19,11},{12,20... | collective-permute-start | bytes 36872 | tf_op jit(solution)/shard_map/ppermute | solution.py:654
  46.4 0.2 prepare.1.ready
  46.6 0.8 %collective-permute-done.10.met_a = f32[2,4,384]{2,1,0:T(4,128)S(1)} collective-permute-done((f32[2,4,384]{2,1,0:T(4,128)S(1)}, f32[2,4,384]{2,1,0:T(4,128)S(1)}, u32[]{:S(2)}, u32[]{:S(2)}) %collective-permute-start.10) | collective-permute-done | bytes 12320 | tf_op jit(solution)/shard_map/ppermute | solution.py:654
  47.4 1.9 %collective-permute-done.11.met_b = f32[2,4,384]{2,1,0:T(4,128)S(1)} collective-permute-done((f32[2,4,384]{2,1,0:T(4,128)S(1)}, f32[2,4,384]{2,1,0:T(4,128)S(1)}, u32[]{:S(2)}, u32[]{:S(2)}) %collective-permute-start.11) | collective-permute-done | bytes 12320 | tf_op jit(solution)/shard_map/ppermute | solution.py:654
  49.3 1.0 %solve.1 = f32[8,256]{1,0:T(8,128)} custom-call(f32[10,16,384]{2,1,0:T(8,128)S(1)} %prepare.1.ready, f32[2,4,384]{2,1,0:T(4,128)S(1)} %collective-permute-done.10.met_a, f32[2,4,384]{2,1,0:T(4,128)S(1)} %get-tuple-element.97.own_a, f32[2,4,384]{2,1,0:T(4,128)S(1)} %get-tuple-element.98.own_b, f32[2,4,384]{2,1,0:T(4,128)S(1)} %collective-permute-done.11.met_b), custom_call_target="tpu_custom_call" | custom-call | tf_op jit(solution)/shard_map/solve/pallas_call | solution.py:687
  (11 shorter events, 0.2 us)
Async XLA Ops:
  3.0 1.6 %collective-permute-start = (f32[2,8,8,128]{3,2,1,0:T(8,128)S(1)}, f32[2,8,8,128]{3,2,1,0:T(8,128)S(1)}, u32[]{:S(2)}, u32[]{:S(2)}) collective-permute-start(f32[2,8,8,128]{3,2,1,0:T(8,128)S(1)} %get-tuple-element.54), channel_id=1, source_target_pairs={{0,1},{1,0},{2,3},{3,2},{4,5},{5,4},{6,7},{7,6},{8,9},{9,8},{10,11... | collective-permute-start | bytes 196616 | tf_op jit(solution)/shard_map/ppermute | solution.py:647
  3.1 5.0 %collective-permute-start.1 = (f32[2,8,8,128]{3,2,1,0:T(8,128)S(1)}, f32[2,8,8,128]{3,2,1,0:T(8,128)S(1)}, u32[]{:S(2)}, u32[]{:S(2)}) collective-permute-start(f32[2,8,8,128]{3,2,1,0:T(8,128)S(1)} %get-tuple-element.55), channel_id=1, source_target_pairs={{1,2},{2,1},{3,4},{4,3},{5,6},{6,5},{7,0},{0,7},{9,10},{10,9},{11,... | collective-permute-start | bytes 196616 | tf_op jit(solution)/shard_map/ppermute | solution.py:648
  8.2 9.1 %collective-permute-start.2 = (f32[17,2,8,256]{3,2,1,0:T(8,128)S(1)}, f32[17,2,8,256]{3,2,1,0:T(8,128)S(1)}, u32[]{:S(2)}, u32[]{:S(2)}) collective-permute-start(f32[17,2,8,256]{3,2,1,0:T(8,128)S(1)} %get-tuple-element.58.refs_2_), channel_id=1, source_target_pairs={{0,8},{8,0},{16,24},{24,16},{1,9},{9,1},{17,25},{25,17},{2,10},{10... | collective-permute-start | bytes 835592 | tf_op jit(solution)/shard_map/ppermute | solution.py:654
  8.4 13.0 %collective-permute-start.3 = (f32[17,2,8,256]{3,2,1,0:T(8,128)S(1)}, f32[17,2,8,256]{3,2,1,0:T(8,128)S(1)}, u32[]{:S(2)}, u32[]{:S(2)}) collective-permute-start(f32[17,2,8,256]{3,2,1,0:T(8,128)S(1)} %get-tuple-element.59.refs_3_), channel_id=1, source_target_pairs={{8,16},{16,8},{9,17},{17,9},{10,18},{18,10},{11,19},{19,11},{12,20... | collective-permute-start | bytes 835592 | tf_op jit(solution)/shard_map/ppermute | solution.py:654
  13.7 12.5 %collective-permute-start.8 = (f32[17,2,8,256]{3,2,1,0:T(8,128)S(1)}, f32[17,2,8,256]{3,2,1,0:T(8,128)S(1)}, u32[]{:S(2)}, u32[]{:S(2)}) collective-permute-start(f32[17,2,8,256]{3,2,1,0:T(8,128)S(1)} %get-tuple-element.67.refs_2_), channel_id=1, source_target_pairs={{0,8},{8,0},{16,24},{24,16},{1,9},{9,1},{17,25},{25,17},{2,10},{10... | collective-permute-start | bytes 835592 | tf_op jit(solution)/shard_map/ppermute | solution.py:654
  13.8 15.9 %collective-permute-start.9 = (f32[17,2,8,256]{3,2,1,0:T(8,128)S(1)}, f32[17,2,8,256]{3,2,1,0:T(8,128)S(1)}, u32[]{:S(2)}, u32[]{:S(2)}) collective-permute-start(f32[17,2,8,256]{3,2,1,0:T(8,128)S(1)} %get-tuple-element.68.refs_3_), channel_id=1, source_target_pairs={{8,16},{16,8},{9,17},{17,9},{10,18},{18,10},{11,19},{19,11},{12,20... | collective-permute-start | bytes 835592 | tf_op jit(solution)/shard_map/ppermute | solution.py:654
  15.7 18.6 %collective-permute-start.6 = (f32[17,2,8,256]{3,2,1,0:T(8,128)S(1)}, f32[17,2,8,256]{3,2,1,0:T(8,128)S(1)}, u32[]{:S(2)}, u32[]{:S(2)}) collective-permute-start(f32[17,2,8,256]{3,2,1,0:T(8,128)S(1)} %get-tuple-element.65.refs_2_), channel_id=1, source_target_pairs={{0,8},{8,0},{16,24},{24,16},{1,9},{9,1},{17,25},{25,17},{2,10},{10... | collective-permute-start | bytes 835592 | tf_op jit(solution)/shard_map/ppermute | solution.py:654
  17.4 17.0 %collective-permute-start.7 = (f32[17,2,8,256]{3,2,1,0:T(8,128)S(1)}, f32[17,2,8,256]{3,2,1,0:T(8,128)S(1)}, u32[]{:S(2)}, u32[]{:S(2)}) collective-permute-start(f32[17,2,8,256]{3,2,1,0:T(8,128)S(1)} %get-tuple-element.66.refs_3_), channel_id=1, source_target_pairs={{8,16},{16,8},{9,17},{17,9},{10,18},{18,10},{11,19},{19,11},{12,20... | collective-permute-start | bytes 835592 | tf_op jit(solution)/shard_map/ppermute | solution.py:654
  26.1 12.9 %collective-permute-start.4 = (f32[17,2,8,256]{3,2,1,0:T(8,128)S(1)}, f32[17,2,8,256]{3,2,1,0:T(8,128)S(1)}, u32[]{:S(2)}, u32[]{:S(2)}) collective-permute-start(f32[17,2,8,256]{3,2,1,0:T(8,128)S(1)} %get-tuple-element.62.refs_2_), channel_id=1, source_target_pairs={{0,8},{8,0},{16,24},{24,16},{1,9},{9,1},{17,25},{25,17},{2,10},{10... | collective-permute-start | bytes 835592 | tf_op jit(solution)/shard_map/ppermute | solution.py:654
  26.2 12.8 %collective-permute-start.5 = (f32[17,2,8,256]{3,2,1,0:T(8,128)S(1)}, f32[17,2,8,256]{3,2,1,0:T(8,128)S(1)}, u32[]{:S(2)}, u32[]{:S(2)}) collective-permute-start(f32[17,2,8,256]{3,2,1,0:T(8,128)S(1)} %get-tuple-element.63.refs_3_), channel_id=1, source_target_pairs={{8,16},{16,8},{9,17},{17,9},{10,18},{18,10},{11,19},{19,11},{12,20... | collective-permute-start | bytes 835592 | tf_op jit(solution)/shard_map/ppermute | solution.py:654
  43.7 3.8 %collective-permute-start.10 = (f32[2,4,384]{2,1,0:T(4,128)S(1)}, f32[2,4,384]{2,1,0:T(4,128)S(1)}, u32[]{:S(2)}, u32[]{:S(2)}) collective-permute-start(f32[2,4,384]{2,1,0:T(4,128)S(1)} %get-tuple-element.97.own_a), channel_id=1, source_target_pairs={{0,8},{8,0},{16,24},{24,16},{1,9},{9,1},{17,25},{25,17},{2,10},{10... | collective-permute-start | bytes 36872 | tf_op jit(solution)/shard_map/ppermute | solution.py:654
  43.7 5.6 %collective-permute-start.11 = (f32[2,4,384]{2,1,0:T(4,128)S(1)}, f32[2,4,384]{2,1,0:T(4,128)S(1)}, u32[]{:S(2)}, u32[]{:S(2)}) collective-permute-start(f32[2,4,384]{2,1,0:T(4,128)S(1)} %get-tuple-element.98.own_b), channel_id=1, source_target_pairs={{8,16},{16,8},{9,17},{17,9},{10,18},{18,10},{11,19},{19,11},{12,20... | collective-permute-start | bytes 36872 | tf_op jit(solution)/shard_map/ppermute | solution.py:654
